TPU v7x, 32 devices: a whole 2x2x4 slice. The times are simulated.
32 devices in a mesh: wide: 16 (over z, y, x), narrow: 2 (over core).
Axes of the slice: x: 2, y: 2, z: 4, core: 2. Of those that a mesh axis runs over, the one named last changes fastest.
Arguments:
- tokens: bfloat16 [31360, 512], P(('wide', 'narrow')), may hold values from -6 to 6
- mask: int32 [160, 196], P(('wide', 'narrow')), may hold values 0 or 1
- ln1_gain: float32 [2, 512], replicated, may hold values from 0.5 to 1.5
- ln1_bias: float32 [2, 512], replicated, may hold values from -4 to 4
- in_weight: bfloat16 [2, 512, 3072], P(None, ('wide', 'narrow')), may hold values from -0.25 to 0.25
- in_bias: float32 [2, 3072], replicated, may hold values from -6 to 6
- ln2_gain: float32 [2, 1536], replicated, may hold values from 0.5 to 1.5
- ln2_bias: float32 [2, 1536], replicated, may hold values from -4 to 4
- spatial_weight: bfloat16 [2, 196, 196], replicated, may hold values from -0.4375 to 0.4375
- spatial_bias: float32 [2, 196], replicated, may hold values from -6 to 6
- out_weight: bfloat16 [2, 1536, 512], P(None, ('wide', 'narrow')), may hold values from -0.15625 to 0.15625
- out_bias: float32 [2, 512], replicated, may hold values from -4 to 4
- cotangent: bfloat16 [31360, 512], P(('wide', 'narrow')), may hold values from -6 to 6
Outputs:
- layer_out: bfloat16 [31360, 512], P(('wide', 'narrow'))
- input_grad: float32 [31360, 512], P(('wide', 'narrow'))
- ln1_gain_grad: float32 [2, 512], replicated
- ln1_bias_grad: float32 [2, 512], replicated
- in_weight_grad: float32 [2, 512, 3072], P(None, ('wide', 'narrow'))
- in_bias_grad: float32 [2, 3072], replicated
- ln2_gain_grad: float32 [2, 1536], replicated
- ln2_bias_grad: float32 [2, 1536], replicated
- spatial_weight_grad: float32 [2, 196, 196], replicated
- spatial_bias_grad: float32 [2, 196], replicated
- out_weight_grad: float32 [2, 1536, 512], P(None, ('wide', 'narrow'))
- out_bias_grad: float32 [2, 512], replicated
All inputs are finite; a program needn't handle non-finite values. No bound on the sum of `mask` on one device may be relied on, other than what follows from the above.
Results may differ from a plain program's by a relative error of at most 0.009.
Values may be sent and summed in bfloat16 or wider, within the bound.
No kernel may reach another device: no remote copies, remote signals or barrier semaphores. Data moves between devices by JAX's collectives and lax.ppermute only.
A program may use at most 192 MiB of HBM per device.

v0:
```python
import jax
import jax.numpy as jnp
from jax import lax
from jax.sharding import PartitionSpec as P

EPS = 1e-05


def norm_forward(values, norm_gain, norm_bias):
    average = jnp.mean(values, -1, keepdims=True)
    centred = values - average
    spread = jnp.mean(centred * centred, -1, keepdims=True)
    inverse = lax.rsqrt(spread + EPS)
    white = centred * inverse
    return (white * norm_gain + norm_bias, white, inverse)


def norm_backward(upstream, white, inverse, norm_gain):
    scaled = upstream * norm_gain
    result = inverse * (
        scaled
        - jnp.mean(scaled, -1, keepdims=True)
        - white * jnp.mean(scaled * white, -1, keepdims=True)
    )
    return (result, jnp.sum(upstream * white, 0), jnp.sum(upstream, 0))


def forward_layer(inputs, valid, gathered, small_set):
    w_in, w_out = gathered
    gain_one, bias_one, b_in, gain_two, bias_two, w_sp, b_sp, b_out = small_set
    normed_one, white_one, inv_one = norm_forward(inputs, gain_one, bias_one)
    normed = normed_one.astype(jnp.bfloat16)
    hidden = jnp.dot(normed, w_in, preferred_element_type=jnp.float32) + b_in
    active = jax.nn.gelu(hidden)
    half_width = w_out.shape[0]
    left_part = active[:, :half_width]
    right_part = active[:, half_width:]
    normed_two, white_two, inv_two = norm_forward(right_part, gain_two, bias_two)
    spatial_in = (normed_two * valid).astype(jnp.bfloat16)
    slots = w_sp.shape[0]
    cube = spatial_in.reshape(-1, slots, half_width)
    mixed = (
        jnp.einsum("pq,iqg->ipg", w_sp, cube, preferred_element_type=jnp.float32)
        + b_sp[None, :, None]
    )
    mixed = mixed.reshape(-1, half_width)
    gated = (left_part * mixed * valid).astype(jnp.bfloat16)
    branch = jnp.dot(gated, w_out, preferred_element_type=jnp.float32) + b_out
    stored = (
        normed,
        white_one,
        inv_one,
        hidden,
        left_part,
        white_two,
        inv_two,
        spatial_in,
        mixed,
        gated,
    )
    return (inputs + branch, stored)


def backward_layer(upstream, stored, valid, gathered, small_set):
    w_in, w_out = gathered
    gain_one, bias_one, b_in, gain_two, bias_two, w_sp, b_sp, b_out = small_set
    normed, white_one, inv_one, hidden, left_part, white_two, inv_two, spatial_in, mixed, gated = (
        stored
    )
    half_width = w_out.shape[0]
    slots = w_sp.shape[0]
    branch_grad = upstream.astype(jnp.bfloat16)
    out_bias_grad = jnp.sum(branch_grad.astype(jnp.float32), 0)
    out_weight_grad = jnp.einsum(
        "rg,rd->gd", gated, branch_grad, preferred_element_type=jnp.float32
    )
    gated_grad = jnp.einsum("rd,gd->rg", branch_grad, w_out, preferred_element_type=jnp.float32)
    left_grad = gated_grad * mixed * valid
    mixed_grad = (gated_grad * left_part * valid).astype(jnp.bfloat16)
    mixed_cube = mixed_grad.reshape(-1, slots, half_width)
    spatial_bias_grad = jnp.sum(mixed_cube.astype(jnp.float32), axis=(0, 2))
    spatial_weight_grad = jnp.einsum(
        "ipg,iqg->pq",
        mixed_cube,
        spatial_in.reshape(-1, slots, half_width),
        preferred_element_type=jnp.float32,
    )
    spatial_grad = jnp.einsum(
        "pq,ipg->iqg", w_sp, mixed_cube, preferred_element_type=jnp.float32
    ).reshape(-1, half_width)
    right_grad, gain_two_grad, bias_two_grad = norm_backward(
        spatial_grad * valid, white_two, inv_two, gain_two
    )
    unused_value, gelu_back = jax.vjp(jax.nn.gelu, hidden)
    hidden_grad = gelu_back(jnp.concatenate([left_grad, right_grad], 1))[0].astype(jnp.bfloat16)
    in_bias_grad = jnp.sum(hidden_grad.astype(jnp.float32), 0)
    in_weight_grad = jnp.einsum(
        "rd,rh->dh", normed, hidden_grad, preferred_element_type=jnp.float32
    )
    normed_grad = jnp.einsum("rh,dh->rd", hidden_grad, w_in, preferred_element_type=jnp.float32)
    input_grad, gain_one_grad, bias_one_grad = norm_backward(
        normed_grad, white_one, inv_one, gain_one
    )
    large_terms = (in_weight_grad, out_weight_grad)
    small_terms = (
        gain_one_grad,
        bias_one_grad,
        in_bias_grad,
        gain_two_grad,
        bias_two_grad,
        spatial_weight_grad,
        spatial_bias_grad,
        out_bias_grad,
    )
    return (input_grad + upstream, large_terms, small_terms)


def shards(
    tokens,
    mask,
    ln1_gain,
    ln1_bias,
    in_weight,
    in_bias,
    ln2_gain,
    ln2_bias,
    spatial_weight,
    spatial_bias,
    out_weight,
    out_bias,
    cotangent,
):
    layer_count = in_weight.shape[0]
    valid = mask.astype(jnp.float32).reshape(-1, 1)

    def small_of(layer_pos):
        return (
            ln1_gain[layer_pos],
            ln1_bias[layer_pos],
            in_bias[layer_pos],
            ln2_gain[layer_pos],
            ln2_bias[layer_pos],
            spatial_weight[layer_pos],
            spatial_bias[layer_pos],
            out_bias[layer_pos],
        )

    layer_inputs = []
    forward_weights = []
    current = tokens.astype(jnp.float32)
    for layer_pos in range(layer_count):
        layer_inputs.append(current)
        gathered = (
            lax.all_gather(in_weight[layer_pos], ("wide", "narrow"), axis=0, tiled=True),
            lax.all_gather(out_weight[layer_pos], ("wide", "narrow"), axis=0, tiled=True),
        )
        forward_weights.append(gathered)
        current, unused_store = forward_layer(current, valid, gathered, small_of(layer_pos))
    layer_out = current.astype(jnp.bfloat16)
    upstream = cotangent.astype(jnp.float32)
    large_list = [None] * layer_count
    small_list = [None] * layer_count
    for layer_pos in reversed(range(layer_count)):
        gathered = (
            lax.all_gather(in_weight[layer_pos], ("wide", "narrow"), axis=0, tiled=True),
            lax.all_gather(out_weight[layer_pos], ("wide", "narrow"), axis=0, tiled=True),
        )
        unused_out, stored = forward_layer(
            layer_inputs[layer_pos], valid, gathered, small_of(layer_pos)
        )
        upstream, large_terms, small_terms = backward_layer(
            upstream, stored, valid, gathered, small_of(layer_pos)
        )
        large_list[layer_pos] = large_terms
        small_list[layer_pos] = small_terms
    in_stack = jnp.stack([pair[0] for pair in large_list])
    out_stack = jnp.stack([pair[1] for pair in large_list])
    small_stack = [jnp.stack([entry[member] for entry in small_list]) for member in range(8)]
    in_stack, out_stack = (
        lax.psum_scatter(in_stack, ("wide", "narrow"), scatter_dimension=1, tiled=True),
        lax.psum_scatter(out_stack, ("wide", "narrow"), scatter_dimension=1, tiled=True),
    )
    small_stack = lax.psum(
        (
            small_stack[0],
            small_stack[1],
            small_stack[2],
            small_stack[3],
            small_stack[4],
            small_stack[5],
            small_stack[6],
            small_stack[7],
        ),
        ("wide", "narrow"),
    )
    return (
        layer_out,
        upstream,
        small_stack[0],
        small_stack[1],
        in_stack,
        small_stack[2],
        small_stack[3],
        small_stack[4],
        small_stack[5],
        small_stack[6],
        out_stack,
        small_stack[7],
    )


def solution(mesh):
    in_specs = (
        P(("wide", "narrow"), None),
        P(("wide", "narrow"), None),
        P(),
        P(),
        P(None, ("wide", "narrow"), None),
        P(),
        P(),
        P(),
        P(),
        P(),
        P(None, ("wide", "narrow"), None),
        P(),
        P(("wide", "narrow"), None),
    )
    out_specs = (
        P(("wide", "narrow"), None),
        P(("wide", "narrow"), None),
        P(),
        P(),
        P(None, ("wide", "narrow"), None),
        P(),
        P(),
        P(),
        P(),
        P(),
        P(None, ("wide", "narrow"), None),
        P(),
    )
    return jax.shard_map(shards, mesh=mesh, in_specs=in_specs, out_specs=out_specs, check_vma=False)
```

profile of v0, /device:TPU:0, one launch (start us, length us, event | category | flops | bytes accessed | tf_op | source)
XLA Modules:
  0.0 767.6 jit_solution(9478792961464371595)
XLA Ops:
  26.1 47.0 %all-gather.9.cloned.1.call-done = bf16[1,512,3072]{2,1,0:T(8,128)(2,1)} async-done(((bf16[1,16,3072]{2,1,0:T(8,128)(2,1)}), bf16[1,512,3072]{2,1,0:T(8,128)(2,1)}) %all-gather.9.cloned.1.call-update) | async-done | bytes 3145744 | tf_op jit(solution)/shard_map/all_gather | solution.py:154
  73.2 11.0 %multiply_multiply_fusion.5 = (f32[980,3072]{1,0:T(8,128)S(1)}, f32[980,3072]{1,0:T(8,128)}) fusion(f32[3072]{0:T(1024)S(1)} %bitcast.126, bf16[1,512,3072]{2,1,0:T(8,128)(2,1)} %all-gather.9.cloned.1.call-done, bf16[980,512]{1,0:T(8,128)(2,1)} %param.13, f32[512]{0:T(512)S(1)} %bitcast.140, f32[512]{0:T(512)S(1)} %bitcast.132, ...), kind=kOutput, calls=%fused_computation.24 | convolution fusion | flops 3112919040 | bytes 28257952 | tf_op jit(solution)/shard_map/dot_general | solution.py:33
  85.3 3.3 copy-done
  88.5 2.6 multiply_convert_fusion.5
  91.2 2.7 reshape.182
  93.9 3.7 add_bitcast_fusion.1
  97.6 5.4 reshape.183
  103.0 6.8 multiply_convert_fusion.4
  109.8 20.6 %all-gather.11.cloned.1.call-done = bf16[1,1536,512]{2,1,0:T(8,128)(2,1)} async-done(((bf16[1,48,512]{2,1,0:T(8,128)(2,1)}), bf16[1,1536,512]{2,1,0:T(8,128)(2,1)}) %all-gather.11.cloned.1.call-update) | async-done | bytes 1572880 | tf_op jit(solution)/shard_map/all_gather | solution.py:155
  130.4 4.2 fusion.64
  135.0 56.7 %all-gather.13.cloned.1.call-done = bf16[1,512,3072]{2,1,0:T(8,128)(2,1)} async-done(((bf16[1,16,3072]{2,1,0:T(8,128)(2,1)}), bf16[1,512,3072]{2,1,0:T(8,128)(2,1)}) %all-gather.13.cloned.1.call-update) | async-done | bytes 3145744 | tf_op jit(solution)/shard_map/all_gather | solution.py:154
  191.7 10.0 %multiply_multiply_fusion.4 = (f32[980,3072]{1,0:T(8,128)S(1)}, f32[980,3072]{1,0:T(8,128)}) fusion(f32[3072]{0:T(1024)S(1)} %bitcast.129, bf16[1,512,3072]{2,1,0:T(8,128)(2,1)} %all-gather.13.cloned.1.call-done, f32[980,512]{1,0:T(8,128)S(1)} %get-tuple-element.99, f32[512]{0:T(512)S(1)} %bitcast.142, f32[512]{0:T(512)S(1)} %bitcast.136, ...), kind=kOutput, calls=%fused_computation.23 | convolution fusion | flops 3112417280 | bytes 29261472 | tf_op jit(solution)/shard_map/dot_general | solution.py:33
  201.7 4.4 copy-done.3
  206.5 42.3 %all-gather.15.cloned.1.call-done = bf16[1,1536,512]{2,1,0:T(8,128)(2,1)} async-done(((bf16[1,48,512]{2,1,0:T(8,128)(2,1)}), bf16[1,1536,512]{2,1,0:T(8,128)(2,1)}) %all-gather.15.cloned.1.call-update) | async-done | bytes 1572880 | tf_op jit(solution)/shard_map/all_gather | solution.py:155
  248.8 9.0 %convert_reduce_fusion.2 = (f32[980]{0:T(1024)}, bf16[980,1536]{1,0:T(8,128)(2,1)}, f32[980]{0:T(1024)S(1)}, f32[980,1536]{1,0:T(8,128)}) fusion(f32[980]{0:T(1024)S(1)} %mul.222, f32[980,3072]{1,0:T(8,128)} %copy-done.3, f32[980]{0:T(1024)S(1)} %broadcast_multiply_fusion.4, bf16[980,512]{1,0:T(8,128)(2,1)S(1)} %copy-done.21, ...), kind=kOutput, calls=%fused_computation.30 | convolution fusion | flops 1553446912 | bytes 23665984 | tf_op jit(solution)/shard_map/rd,gd->rg/dot_general | solution.py:77
  257.7 3.0 reshape.186
  260.8 5.4 multiply_reduce_fusion.9
  268.1 5.4 reshape.187
  273.6 6.3 multiply_reduce_fusion.2
  279.9 6.8 subtract_multiply_fusion.1
  286.7 2.7 reshape.184
  289.4 3.5 convolution_bitcast_fusion.6
  292.9 3.7 add_bitcast_fusion
  296.6 5.6 reshape.185
  302.1 9.2 %multiply_multiply_fusion.7 = (f32[980,1536]{1,0:T(8,128)S(1)}, bf16[980,1536]{1,0:T(8,128)(2,1)}) fusion(f32[980,1536]{1,0:T(8,128)} %get-tuple-element.102, f32[980,1536]{1,0:T(8,128)} %reshape.185, f32[980]{0:T(1024)S(1)} %mul.222, f32[980,3072]{1,0:T(8,128)} %copy-done.3), kind=kLoop, calls=%fused_computation.41 | loop fusion | flops 7526400 | bytes 27098960 | tf_op jit(solution)/shard_map/mul | solution.py:78
  311.4 12.1 %convert_reduce_fusion = (f32[3072]{0:T(1024)S(1)}, bf16[980,3072]{1,0:T(8,128)(2,1)S(1)}) fusion(f32[980,3072]{1,0:T(8,128)} %get-tuple-element.101, f32[3072]{0:T(1024)S(1)} %bitcast.130, f32[980,1536]{1,0:T(8,128)S(1)} %bitcast.123, f32[980,1536]{1,0:T(8,128)S(1)} %get-tuple-element.77), kind=kLoop, calls=%fused_computation.21 | loop fusion | flops 72250368 | bytes 30130176 | tf_op jit(solution)/shard_map/reduce_sum | solution.py:96
  323.5 3.9 multiply_reduce_fusion.10
  329.3 3.5 convolution_bitcast_fusion.5
  332.8 3.5 convolution_bitcast_fusion.4
  339.0 4.8 convert_reduce_fusion.3
  343.7 4.1 reshape.188
  347.9 2.9 convolution_bitcast_fusion.7
  351.6 6.3 pad_maximum_fusion.3
  359.8 4.0 multiply_reduce_fusion.8
  363.9 5.7 reshape.189
  369.6 5.8 multiply_reduce_fusion.3
  375.9 5.6 subtract_multiply_fusion
  381.6 11.9 %convert_reduce_fusion.1 = (f32[3072]{0:T(1024)S(1)}, bf16[980,3072]{1,0:T(8,128)(2,1)S(1)}) fusion(f32[980,3072]{1,0:T(8,128)} %get-tuple-element.97, f32[3072]{0:T(1024)S(1)} %bitcast.127, f32[980,1536]{1,0:T(8,128)S(1)} %subtract_multiply_fusion, f32[980,1536]{1,0:T(8,128)S(1)} %bitcast.125), kind=kLoop, calls=%fused_computation.22 | loop fusion | flops 72250368 | bytes 30130176 | tf_op jit(solution)/shard_map/reduce_sum | solution.py:96
  393.5 6.1 convolution_bitcast_fusion.1
  399.7 6.1 convolution_bitcast_fusion
  405.9 8.6 %pad_maximum_fusion = f32[2,512,3072]{2,1,0:T(8,128)} fusion(f32[1,512,3072]{2,1,0:T(8,128)} %convolution_bitcast_fusion, f32[1,512,3072]{2,1,0:T(8,128)S(1)} %convolution_bitcast_fusion.1), kind=kLoop, calls=%fused_computation.4 | loop fusion | flops 3145728 | bytes 25165824 | tf_op jit(solution)/shard_map/stack | solution.py:176
  415.7 8.6 %fusion.36 = (f32[512]{0:T(512)S(1)}, f32[980]{0:T(1024)S(1)}, f32[980]{0:T(1024)S(1)}, f32[512]{0:T(512)S(1)}, f32[980,512]{1,0:T(8,128)}) fusion(bf16[980,512]{1,0:T(8,128)(2,1)S(1)} %copy-done.14, f32[980]{0:T(1024)S(1)} %add_rsqrt_fusion.3, f32[980]{0:T(1024)S(1)} %broadcast_multiply_fusion.11, f32[512]{0:T(512)S(1)} %bitcast.134, ...), kind=kOutput, calls=%fused_computation.87 | convolution fusion | flops 3087827968 | bytes 12199232 | tf_op jit(solution)/shard_map/rh,dh->rd/dot_general | solution.py:100
  424.5 40.6 %all-reduce = (f32[2,512]{1,0:T(2,128)}, f32[2,512]{1,0:T(2,128)}, f32[2,3072]{1,0:T(2,128)}, f32[2,1536]{1,0:T(2,128)}, f32[2,1536]{1,0:T(2,128)}, /*index=5*/f32[2,196]{1,0:T(2,128)}, f32[2,512]{1,0:T(2,128)}) all-reduce(f32[2,512]{1,0:T(2,128)S(1)} %pad_maximum_fusion.8, ...), channel_id=1, replica_groups=mesh['wide'=16,'narrow'=2] {'wide','narrow'}, use_global_device_ids=true, to_apply=%region_18.0 | all-reduce | flops 15752 | bytes 126016 | tf_op jit(solution)/shard_map/psum | solution.py:183
  465.0 3.7 fusion.35
  469.3 2.7 add_convert_fusion
  472.0 4.5 all-reduce.3.cloned.1.call-done
  478.4 120.6 %reduce-scatter.5.cloned.1.call-done = f32[2,48,512]{2,1,0:T(8,128)} async-done(((f32[2,1536,512]{2,1,0:T(8,128)}), f32[2,48,512]{2,1,0:T(8,128)}) %reduce-scatter.5.cloned.1.call-update) | async-done | bytes 196624 | tf_op jit(solution)/shard_map/reduce_scatter | solution.py:181
  599.1 161.2 %reduce-scatter.3.cloned.1.call-done = f32[2,16,3072]{2,1,0:T(8,128)} async-done(((f32[2,512,3072]{2,1,0:T(8,128)}), f32[2,16,3072]{2,1,0:T(8,128)}) %reduce-scatter.3.cloned.1.call-update) | async-done | bytes 393232 | tf_op jit(solution)/shard_map/reduce_scatter | solution.py:180
  (178 shorter events, 34.3 us)
Async XLA Ops:
  7.2 66.0 %all-gather.9.cloned.1.call-start = ((), (), s32[]{:S(2)}) async-start(), calls=%async_computation.5 | async-start | bytes 3244032 | tf_op jit(solution)/shard_map/all_gather | solution.py:154
  8.9 121.5 %all-gather.11.cloned.1.call-start = ((), (), s32[]{:S(2)}) async-start(), calls=%async_computation.6 | async-start | bytes 1622016 | tf_op jit(solution)/shard_map/all_gather | solution.py:155
  10.4 181.3 %all-gather.13.cloned.1.call-start = ((), (), s32[]{:S(2)}) async-start(), calls=%async_computation.7 | async-start | bytes 3244032 | tf_op jit(solution)/shard_map/all_gather | solution.py:154
  11.2 237.6 %all-gather.15.cloned.1.call-start = ((), (), s32[]{:S(2)}) async-start(), calls=%async_computation.8 | async-start | bytes 1622016 | tf_op jit(solution)/shard_map/all_gather | solution.py:155
  11.7 464.7 %all-reduce.3.cloned.1.call-start = ((), (), s32[]{:S(2)}) async-start(), calls=%async_computation.3 | async-start | bytes 819200 | tf_op jit(solution)/shard_map/psum | solution.py:183
  18.9 65.2 %copy-start.30 = (f32[1,512]{1,0:T(1,128)}, f32[1,512]{1,0:T(1,128)S(1)}, u32[]{:S(2)}) copy-start(f32[1,512]{1,0:T(1,128)S(1)} %get-tuple-element.93) | copy-start | bytes 6148
  84.2 4.4 copy-start
  88.5 5.3 copy-start.36
  103.0 27.4 %copy-start.13 = (bf16[980,512]{1,0:T(8,128)(2,1)S(1)}, bf16[980,512]{1,0:T(8,128)(2,1)}, u32[]{:S(2)}) copy-start(bf16[980,512]{1,0:T(8,128)(2,1)} %param.13) | copy-start | bytes 3010564
  103.0 27.4 %copy-start.40 = (f32[1,512]{1,0:T(1,128)S(1)}, f32[1,512]{1,0:T(1,128)}, u32[]{:S(2)}) copy-start(f32[1,512]{1,0:T(1,128)} %get-tuple-element.89) | copy-start | bytes 6148
  130.4 61.3 %copy-start.28 = (f32[1,512]{1,0:T(1,128)S(1)}, f32[1,512]{1,0:T(1,128)}, u32[]{:S(2)}) copy-start(f32[1,512]{1,0:T(1,128)} %get-tuple-element.90) | copy-start | bytes 6148
  130.4 61.3 %copy-start.32 = (f32[1,512]{1,0:T(1,128)S(1)}, f32[1,512]{1,0:T(1,128)}, u32[]{:S(2)}) copy-start(f32[1,512]{1,0:T(1,128)} %get-tuple-element.92) | copy-start | bytes 6148
  134.6 67.1 %copy-start.6 = (f32[980,512]{1,0:T(8,128)}, f32[980,512]{1,0:T(8,128)S(1)}, u32[]{:S(2)}) copy-start(f32[980,512]{1,0:T(8,128)S(1)} %get-tuple-element.99) | copy-start | bytes 6021124
  201.7 4.4 copy-start.3
  201.7 47.1 %copy-start.21 = (bf16[980,512]{1,0:T(8,128)(2,1)S(1)}, bf16[980,512]{1,0:T(8,128)(2,1)}, u32[]{:S(2)}) copy-start(bf16[980,512]{1,0:T(8,128)(2,1)} %param.25) | copy-start | bytes 3010564
  260.8 12.8 %copy-start.16 = (bf16[5,196,1536]{2,1,0:T(8,128)(2,1)}, bf16[5,196,1536]{2,1,0:T(8,128)(2,1)S(1)}, u32[]{:S(2)}) copy-start(bf16[5,196,1536]{2,1,0:T(8,128)(2,1)S(1)} %reshape.186) | copy-start | bytes 9031684
  273.5 6.4 copy-start.1
  273.5 6.4 copy-start.24
  273.5 6.4 copy-start.34
  286.7 6.2 copy-start.35
  296.6 14.8 %slice-start.7 = ((s8[6045696]{0:T(1024)(128)(4,1)}), s8[1851392]{0:T(1024)(128)(4,1)S(1)}, s32[]{:S(2)}) async-start(s8[6045696]{0:T(1024)(128)(4,1)} %bitcast.122), calls=%async_computation.16 | async-start | bytes 3702784
  302.1 9.2 %slice-start.8 = ((s8[6045696]{0:T(1024)(128)(4,1)}), s8[4194304]{0:T(1024)(128)(4,1)S(1)}, s32[]{:S(2)}) async-start(s8[6045696]{0:T(1024)(128)(4,1)} %bitcast.122), calls=%async_computation.17 | async-start | bytes 8388608
  311.4 12.1 %copy-start.7 = (f32[980,512]{1,0:T(8,128)S(1)}, f32[980,512]{1,0:T(8,128)}, u32[]{:S(2)}) copy-start(f32[980,512]{1,0:T(8,128)} %copy-done.6) | copy-start | bytes 6021124
  311.4 12.1 %copy-start.29 = (f32[1,512]{1,0:T(1,128)S(1)}, f32[1,512]{1,0:T(1,128)}, u32[]{:S(2)}) copy-start(f32[1,512]{1,0:T(1,128)} %get-tuple-element.90) | copy-start | bytes 6148
  311.4 12.1 %copy-start.41 = (bf16[1,512,3072]{2,1,0:T(8,128)(2,1)S(1)}, bf16[1,512,3072]{2,1,0:T(8,128)(2,1)}, u32[]{:S(2)}) copy-start(bf16[1,512,3072]{2,1,0:T(8,128)(2,1)} %all-gather.13.cloned.1.call-done) | copy-start | bytes 9437188
  327.5 5.3 copy-start.18
  327.5 8.8 %slice-start.3 = ((s8[6045696]{0:T(1024)(128)(4,1)}), s8[4194304]{0:T(1024)(128)(4,1)S(1)}, s32[]{:S(2)}) async-start(s8[6045696]{0:T(1024)(128)(4,1)} %bitcast.118), calls=%async_computation.12 | async-start | bytes 8388608
  328.6 7.7 %copy-start.12 = (f32[980,512]{1,0:T(8,128)}, f32[980,512]{1,0:T(8,128)S(1)}, u32[]{:S(2)}) copy-start(f32[980,512]{1,0:T(8,128)S(1)} %get-tuple-element.64) | copy-start | bytes 6021124
  329.3 7.0 slice-start
  329.3 7.0 slice-start.1
  329.3 8.1 %slice-start.4 = ((s8[6045696]{0:T(1024)(128)(4,1)}), s8[1851392]{0:T(1024)(128)(4,1)S(1)}, s32[]{:S(2)}) async-start(s8[6045696]{0:T(1024)(128)(4,1)} %bitcast.118), calls=%async_computation.13 | async-start | bytes 3702784
  332.8 5.1 copy-start.20
  332.8 6.2 slice-start.2
  343.7 4.1 copy-start.11
  351.6 247.5 %reduce-scatter.5.cloned.1.call-start = ((), (), s32[]{:S(2)}) async-start(), calls=%async_computation.4 | async-start | bytes 6488064 | tf_op jit(solution)/shard_map/reduce_scatter | solution.py:181
  357.9 402.4 %reduce-scatter.3.cloned.1.call-start = ((), (), s32[]{:S(2)}) async-start(), calls=%async_computation.2 | async-start | bytes 12976128 | tf_op jit(solution)/shard_map/reduce_scatter | solution.py:180
  369.6 6.3 copy-start.2
  369.6 11.9 %slice-start.9 = ((s8[6045696]{0:T(1024)(128)(4,1)}), s8[4194304]{0:T(1024)(128)(4,1)S(1)}, s32[]{:S(2)}) async-start(s8[6045696]{0:T(1024)(128)(4,1)} %bitcast.124), calls=%async_computation.18 | async-start | bytes 8388608
  375.9 5.7 slice-start.10
  375.9 23.8 %slice-start.5 = ((s8[6045696]{0:T(1024)(128)(4,1)}), s8[4194304]{0:T(1024)(128)(4,1)S(1)}, s32[]{:S(2)}) async-start(s8[6045696]{0:T(1024)(128)(4,1)} %bitcast.120), calls=%async_computation.14 | async-start | bytes 8388608
  381.5 11.9 %copy-start.31 = (f32[1,512]{1,0:T(1,128)S(1)}, f32[1,512]{1,0:T(1,128)}, u32[]{:S(2)}) copy-start(f32[1,512]{1,0:T(1,128)} %copy-done.30) | copy-start | bytes 6148
  381.6 18.1 %slice-start.6 = ((s8[6045696]{0:T(1024)(128)(4,1)}), s8[1851392]{0:T(1024)(128)(4,1)S(1)}, s32[]{:S(2)}) async-start(s8[6045696]{0:T(1024)(128)(4,1)} %bitcast.120), calls=%async_computation.15 | async-start | bytes 3702784
  393.5 6.2 copy-start.5
  393.5 6.2 copy-start.8
  393.5 6.2 copy-start.33
  424.3 44.4 %copy-start.9 = (f32[980,512]{1,0:T(8,128)S(1)}, f32[980,512]{1,0:T(8,128)}, u32[]{:S(2)}) copy-start(f32[980,512]{1,0:T(8,128)} %copy-done.6) | copy-start | bytes 6021124
  424.3 44.4 %copy-start.39 = (f32[1,512]{1,0:T(1,128)S(1)}, f32[1,512]{1,0:T(1,128)}, u32[]{:S(2)}) copy-start(f32[1,512]{1,0:T(1,128)} %get-tuple-element.88) | copy-start | bytes 6148
  465.0 4.3 copy-start.42
  (13 other events, 28.0 us)
Sparse Core Ops, SparseCore 0:
  11.4 61.6 all-gather.8
  76.6 53.7 all-gather.10
  133.8 57.8 all-gather.12
  195.0 53.7 all-gather.14
  351.7 124.7 all-reduce.2
  483.5 115.5 reduce-scatter.4
  605.7 154.5 reduce-scatter.2
where the time goes:
time: 779 us; the launch traced here: 768 us
  waiting for transfers between devices  454 us (58%)
  matrix products  96.6 us (12%)
  other arithmetic  94 us (12%)
  local copies, waits for them, and re-layouts  66.8 us (9%)
  blocking collectives  40.6 us (5%)
  between operations  15.2 us (2%)
    reduce_scatter x1, waiting for transfers between devices, shards(): lax.psum_scatter(in_stack, ('wide', 'narrow'), scatter_dimension=1, tiled...  161 us
    reduce_scatter x1, waiting for transfers between devices, shards(): lax.psum_scatter(out_stack, ('wide', 'narrow'), scatter_dimension=1, tile...  121 us
    all_gather x2, waiting for transfers between devices, shards(): lax.all_gather(in_weight[layer_pos], ('wide', 'narrow'), axis=0, tiled=True)  104 us
    all_gather x2, waiting for transfers between devices, shards(): lax.all_gather(out_weight[layer_pos], ('wide', 'narrow'), axis=0, tiled=T...  62.8 us
    psum x1, blocking collectives, shards(): lax.psum((small_stack[0], small_stack[1], small_stack[2], small_stack[3],...  40.6 us
    reduce_sum x2, other arithmetic, backward_layer(): in_bias_grad = jnp.sum(hidden_grad.astype(jnp.float32), 0)  23.9 us
    dot_general x2, matrix products, forward_layer(): hidden = jnp.dot(normed, w_in, preferred_element_type=jnp.float32) + b_in  21 us
    unnamed x109, local copies, waits for them, and re-layouts  17.6 us
  transfers between devices with their start and end apart: 7, of which 7 were waited for; matrix products, arithmetic and copies ran while one was open for 18% of the time, Pallas kernels for 0%

commit v1 on v0

v1 whole, which is shorter than its diff:
```python
import jax
import jax.numpy as jnp
from jax import lax
from jax.experimental import pallas as pl
from jax.experimental.pallas import tpu as pltpu
from jax.sharding import PartitionSpec as P

EPS = 1e-05
AXES = ("wide", "narrow")
F32 = jnp.float32
BF16 = jnp.bfloat16
TANH_ONE = 2 * 0.7978845608028654
TANH_THREE = 8 * 0.7978845608028654 * 0.044715
COLUMNS = 256
BLOCK = 16
GROUP = 512
VMEM_BYTES = 60 * 1024 * 1024
WEIGHTS = ("b_in", "gain_one", "bias_one", "gain_two", "bias_two", "b_out")
SUMS = ("b_out", "b_in", "spatial", "gain_two", "bias_two", "gain_one", "bias_one")


def dot(a, b):
    return jnp.dot(a, b, preferred_element_type=F32)


def dot_last(a, b):
    return lax.dot_general(a, b, (((1,), (1,)), ((), ())), preferred_element_type=F32)


def dot_first(a, b):
    return lax.dot_general(a, b, (((0,), (0,)), ((), ())), preferred_element_type=F32)


def gelu_pair(half):
    square = half * half
    tanh = jnp.tanh(half * (TANH_ONE + TANH_THREE * square))
    upper = 1.0 + tanh
    value = half * upper
    slope = upper + value * (1.0 - tanh) * (TANH_ONE + (3 * TANH_THREE) * square)
    return value, slope


def fold_rows(values):
    total = values[:8]
    for row in range(8, values.shape[0], 8):
        total = total + values[row : row + 8]
    return total


def fold_columns(values):
    total = values[:, :128]
    for column in range(128, values.shape[1], 128):
        total = total + values[:, column : column + 128]
    return total


def white_of(values):
    centred = values - jnp.mean(values, -1, keepdims=True)
    inverse = lax.rsqrt(jnp.mean(centred * centred, -1, keepdims=True) + EPS)
    return centred * inverse, inverse


def cuts(width):
    return [slice(c, c + COLUMNS) for c in range(0, width, COLUMNS)]


def in_columns(w_in, start):
    at = start % GROUP
    return w_in[start // GROUP, :, at : at + COLUMNS]


def forward_image(values, live, valid, mixer, slot_pad, w, t, slots):
    rows = values.shape[0]
    half_width = t["white"].shape[1]
    cut = slots // BLOCK * BLOCK
    white_one, unused_inverse = white_of(values)
    t["normed"][...] = (white_one * w["gain_one"][...] + w["bias_one"][...]).astype(BF16)
    total = None
    for sl in cuts(half_width):
        at = half_width + sl.start
        half = dot(t["normed"][...], in_columns(w["w_in"], at)) + w["b_in"][:, at : at + COLUMNS]
        value, slope = gelu_pair(half)
        t["right"][:, sl] = value
        t["right_slope"][:, sl] = slope.astype(BF16)
        part = fold_columns(value)
        total = part if total is None else total + part
    average = jnp.sum(total, -1, keepdims=True) * (1.0 / half_width)
    total = None
    for sl in cuts(half_width):
        centred = t["right"][:, sl] - average
        part = fold_columns(centred * centred)
        total = part if total is None else total + part
    spread = jnp.sum(total, -1, keepdims=True) * (1.0 / half_width)
    inverse = lax.rsqrt(spread + EPS) * live
    row = lax.broadcasted_iota(jnp.int32, (rows - cut, COLUMNS), 0)
    for sl in cuts(half_width):
        white = (t["right"][:, sl] - average) * inverse
        t["white"][:, sl] = white.astype(BF16)
        slot_in = white * w["gain_two"][:, sl] + w["bias_two"][:, sl]
        t["slot_in"][:cut, sl] = slot_in[:cut].astype(BF16)
        last = jnp.where(row < slots - cut, slot_in[cut:], slot_pad[:, sl])
        t["slot_in"][cut:, sl] = last.astype(BF16)
    for sl in cuts(half_width):
        half = dot(t["normed"][...], in_columns(w["w_in"], sl.start)) + w["b_in"][:, sl]
        left, slope = gelu_pair(half)
        mixed = dot(mixer, t["slot_in"][:, sl])
        t["gated"][:, sl] = (left * mixed).astype(BF16)
        t["left"][:, sl] = left.astype(BF16)
        t["left_slope"][:, sl] = (mixed * slope).astype(BF16)
    branch = dot(t["gated"][...], w["w_out"][...].reshape(half_width, -1)) * valid
    return values + (branch + w["b_out"][...]), inverse


def backward_image(upstream, valid, mixer_back, inverse, w, t, hidden_grad, sums, slots):
    rows = upstream.shape[0]
    half_width = t["white"].shape[1]
    cut = slots // BLOCK * BLOCK
    for sl in cuts(half_width):
        blocks = slice(sl.start // BLOCK, sl.stop // BLOCK)
        gated_grad = dot_last(upstream, w["w_out"][blocks].reshape(COLUMNS, -1))
        t["mixed_grad"][:, sl] = (gated_grad * t["left"][:, sl].astype(F32)).astype(BF16)
        left_grad = gated_grad * t["left_slope"][:, sl].astype(F32)
        hidden_grad[:, sl] = left_grad.astype(BF16)
        sums["b_in"][:, sl] += fold_rows(left_grad)
    outer = dot_last(t["slot_in"][...], t["mixed_grad"][...])
    is_slot = lax.broadcasted_iota(jnp.int32, (rows, 1), 0) < slots
    sums["spatial"][...] += outer * jnp.where(is_slot, valid, 1.0)
    back = mixer_back.astype(F32)
    by_bias = outer[slots + 2 : slots + 3] + outer[slots + 3 : slots + 4]
    by_gain = outer[slots + 4 : slots + 5] + outer[slots + 5 : slots + 6]
    mean_scaled = jnp.sum(back * by_gain, -1, keepdims=True) * (1.0 / half_width)
    mean_white = jnp.sum(back * (outer - by_bias), -1, keepdims=True) * (1.0 / half_width)
    for sl in cuts(half_width):
        at = half_width + sl.start
        slot_grad = dot(mixer_back, t["mixed_grad"][:, sl])
        white = t["white"][:, sl].astype(F32)
        sums["gain_two"][:, sl] += fold_rows(slot_grad * white)
        sums["bias_two"][:, sl] += slot_grad[cut:]
        scaled = slot_grad * w["gain_two"][:, sl] - mean_scaled - white * mean_white
        right_grad = scaled * inverse * t["right_slope"][:, sl].astype(F32)
        hidden_grad[:, at : at + COLUMNS] = right_grad.astype(BF16)
        sums["b_in"][:, at : at + COLUMNS] += fold_rows(right_grad)


def backward_norm(values, hidden_grad, upstream, w, sums):
    white, inverse = white_of(values)
    normed_grad = None
    for group in range(w["w_in"].shape[0]):
        part = dot_last(hidden_grad[:, group * GROUP : (group + 1) * GROUP], w["w_in"][group])
        normed_grad = part if normed_grad is None else normed_grad + part
    sums["gain_one"][...] += fold_rows(normed_grad * white)
    sums["bias_one"][...] += fold_rows(normed_grad)
    scaled = normed_grad * w["gain_one"][...]
    mean = jnp.mean(scaled, -1, keepdims=True)
    mean_white = jnp.mean(scaled * white, -1, keepdims=True)
    return upstream + inverse * (scaled - mean - white * mean_white)


def load_blocks(owner, pieces, w_in, w_out, sem):
    per = w_out.shape[0] * BLOCK // w_out.shape[2] if w_out is not None else pieces[0].shape[1] - w_in.shape[0]
    groups = pieces[0].shape[1] - per
    position = 0
    for piece in pieces:
        count = piece.shape[0]

        def start(at, carry, piece=piece, position=position):
            block = owner[position + at]
            if w_in is not None:
                rows = pl.ds(pl.multiple_of(block * BLOCK, BLOCK), BLOCK)
                pltpu.make_async_copy(piece.at[at, :groups], w_in.at[:, rows], sem).start()
            if w_out is not None:
                rows = pl.ds(block * per, per)
                pltpu.make_async_copy(piece.at[at, groups:], w_out.at[rows], sem).start()
            return carry

        lax.fori_loop(0, count, start, 0)
        position += count
    if w_in is not None:
        pltpu.make_async_copy(w_in, w_in, sem).wait()
    if w_out is not None:
        pltpu.make_async_copy(w_out, w_out, sem).wait()


def zero(refs):
    for ref in refs:
        ref[...] = jnp.zeros_like(ref)


def whole(shape):
    return pl.BlockSpec(shape, lambda *i: (0,) * len(shape))


def image(rows, columns):
    return pl.BlockSpec((1, rows, columns), lambda i, *unused: (i, 0, 0))


def anywhere(count):
    return [pl.BlockSpec(memory_space=pl.ANY)] * count


def call(kernel, name, grid, in_specs, outs, out_specs, scratch, flops, table=0, aliases=None):
    return pl.pallas_call(
        kernel,
        grid_spec=pltpu.PrefetchScalarGridSpec(
            num_scalar_prefetch=table,
            grid=grid,
            in_specs=in_specs,
            out_specs=out_specs,
            scratch_shapes=scratch,
        ),
        out_shape=[jax.ShapeDtypeStruct(shape, dtype) for shape, dtype in outs],
        input_output_aliases=aliases or {},
        compiler_params=pltpu.CompilerParams(vmem_limit_bytes=VMEM_BYTES),
        cost_estimate=pl.CostEstimate(flops=flops, bytes_accessed=20_000_000, transcendentals=0),
        name=name,
    )


def weight_scratch(width, hidden):
    return [
        pltpu.VMEM((hidden // GROUP, width, GROUP), BF16),
        pltpu.VMEM((hidden // 2 // BLOCK, BLOCK, width), BF16),
        pltpu.SemaphoreType.DMA,
    ]


def sum_shapes(rows, width, hidden, slots):
    return {
        "b_out": (8, width),
        "b_in": (8, hidden),
        "spatial": (rows, rows),
        "gain_two": (8, hidden // 2),
        "bias_two": (rows - slots // BLOCK * BLOCK, hidden // 2),
        "gain_one": (8, width),
        "bias_one": (8, width),
    }


def forward_save(values, valid, live, mixer, slot_pad, w, owner, pieces, slots):
    images, rows, width = values.shape
    hidden = w["b_in"].shape[1]
    gate = hidden // 2
    outs = {
        "values": (width, F32),
        "normed": (width, BF16),
        "left": (gate, BF16),
        "left_slope": (gate, BF16),
        "white": (gate, BF16),
        "right_slope": (gate, BF16),
        "slot_in": (gate, BF16),
        "gated": (gate, BF16),
        "inverse": (1, F32),
    }
    n_w, n_p, n_o = len(WEIGHTS), len(pieces), len(outs)

    def kernel(owner_ref, values_ref, valid_ref, live_ref, mixer_ref, pad_ref, *refs):
        weights = dict(zip(WEIGHTS, refs[:n_w]))
        out = dict(zip(outs, refs[n_w + n_p : n_w + n_p + n_o]))
        right, weights["w_in"], weights["w_out"], sem = refs[n_w + n_p + n_o :]

        @pl.when(pl.program_id(0) == 0)
        def _():
            load_blocks(owner_ref, refs[n_w : n_w + n_p], weights["w_in"], weights["w_out"], sem)

        kept = {name: ref.at[0] for name, ref in out.items()}
        kept["right"] = right
        result, inverse = forward_image(
            values_ref[0].astype(F32), live_ref[...], valid_ref[0], mixer_ref[0], pad_ref, weights, kept, slots
        )
        out["values"][0] = result
        out["inverse"][0] = inverse

    results = call(
        kernel,
        "forward_save",
        (images,),
        [image(rows, width), image(rows, 1), whole((rows, 1)), image(rows, rows), whole(slot_pad.shape)]
        + [whole(w[name].shape) for name in WEIGHTS]
        + anywhere(n_p),
        [((images, rows, columns), dtype) for columns, dtype in outs.values()],
        [image(rows, columns) for columns, unused in outs.values()],
        [pltpu.VMEM((rows, gate), F32)] + weight_scratch(width, hidden),
        12_000_000_000,
        table=1,
    )(owner, values, valid, live, mixer, slot_pad, *[w[name] for name in WEIGHTS], *pieces)
    return dict(zip(outs, results))


def forward_backward(values, cotangent, valid, live, mixer, mixer_back, slot_pad, w, owner, pieces, slots):
    images, rows, width = values.shape
    hidden = w["b_in"].shape[1]
    gate = hidden // 2
    outs = {
        "values": (width, BF16),
        "normed": (width, BF16),
        "gated": (gate, BF16),
        "hidden_grad": (hidden, BF16),
        "masked": (width, BF16),
        "upstream": (width, F32),
    }
    shapes = sum_shapes(rows, width, hidden, slots)
    scratch_names = ("right", "left", "left_slope", "white", "right_slope", "slot_in", "mixed_grad")
    n_w, n_p, n_o, n_s = len(WEIGHTS), len(pieces), len(outs), len(SUMS)

    def kernel(owner_ref, values_ref, cot_ref, valid_ref, live_ref, mixer_ref, back_ref, pad_ref, *refs):
        weights = dict(zip(WEIGHTS, refs[:n_w]))
        rest = refs[n_w + n_p :]
        out = dict(zip(outs, rest[:n_o]))
        sums = dict(zip(SUMS, rest[n_o : n_o + n_s]))
        kept = dict(zip(scratch_names, rest[n_o + n_s :]))
        weights["w_in"], weights["w_out"], sem = rest[n_o + n_s + len(scratch_names) :]

        @pl.when(pl.program_id(0) == 0)
        def _():
            load_blocks(owner_ref, refs[n_w : n_w + n_p], weights["w_in"], weights["w_out"], sem)
            zero(sums.values())

        kept["normed"] = out["normed"].at[0]
        kept["gated"] = out["gated"].at[0]
        here = values_ref[0]
        result, inverse = forward_image(
            here, live_ref[...], valid_ref[0], mixer_ref[0], pad_ref, weights, kept, slots
        )
        out["values"][0] = result.astype(BF16)
        upstream = cot_ref[0].astype(F32)
        sums["b_out"][...] += fold_rows(upstream)
        masked = (upstream * valid_ref[0]).astype(BF16)
        out["masked"][0] = masked
        hidden_grad = out["hidden_grad"].at[0]
        backward_image(masked, valid_ref[0], back_ref[0], inverse, weights, kept, hidden_grad, sums, slots)
        out["upstream"][0] = backward_norm(here, hidden_grad, upstream, weights, sums)

    results = call(
        kernel,
        "forward_backward",
        (images,),
        [image(rows, width)] * 2
        + [image(rows, 1), whole((rows, 1)), image(rows, rows), image(rows, rows), whole(slot_pad.shape)]
        + [whole(w[name].shape) for name in WEIGHTS]
        + anywhere(n_p),
        [((images, rows, columns), dtype) for columns, dtype in outs.values()]
        + [(shapes[name], F32) for name in SUMS],
        [image(rows, columns) for columns, unused in outs.values()] + [whole(shapes[name]) for name in SUMS],
        [pltpu.VMEM((rows, gate), F32)] + [pltpu.VMEM((rows, gate), BF16)] * 6 + weight_scratch(width, hidden),
        24_000_000_000,
        table=1,
    )(owner, values, cotangent, valid, live, mixer, mixer_back, slot_pad, *[w[name] for name in WEIGHTS], *pieces)
    return dict(zip(outs, results)), dict(zip(SUMS, results[n_o:]))


def backward_gate(upstream, kept, valid, mixer_back, w, owner, pieces, slots):
    images, rows, width = upstream.shape
    hidden = w["b_in"].shape[1]
    gate = hidden // 2
    shapes = sum_shapes(rows, width, hidden, slots)
    names = SUMS[:5]
    reads = ("left", "left_slope", "white", "right_slope", "slot_in", "inverse")
    n_p, n_r = len(pieces), len(reads)

    def kernel(owner_ref, up_ref, valid_ref, back_ref, gain_ref, *refs):
        t = {name: ref.at[0] for name, ref in zip(reads, refs)}
        rest = refs[n_r + n_p :]
        hidden_grad, masked_ref = rest[:2]
        sums = dict(zip(names, rest[2 : 2 + len(names)]))
        t["mixed_grad"], w_out, sem = rest[2 + len(names) :]

        @pl.when(pl.program_id(0) == 0)
        def _():
            load_blocks(owner_ref, refs[n_r : n_r + n_p], None, w_out, sem)
            zero(sums.values())

        branch_grad = up_ref[0].astype(BF16).astype(F32)
        sums["b_out"][...] += fold_rows(branch_grad)
        masked = (branch_grad * valid_ref[0]).astype(BF16)
        masked_ref[0] = masked
        weights = {"w_out": w_out, "gain_two": gain_ref}
        backward_image(
            masked, valid_ref[0], back_ref[0], t["inverse"][...], weights, t, hidden_grad.at[0], sums, slots
        )

    results = call(
        kernel,
        "backward_gate",
        (images,),
        [image(rows, width), image(rows, 1), image(rows, rows), whole((1, gate))]
        + [image(rows, gate)] * 5
        + [image(rows, 1)]
        + anywhere(n_p),
        [((images, rows, hidden), BF16), ((images, rows, width), BF16)] + [(shapes[name], F32) for name in names],
        [image(rows, hidden), image(rows, width)] + [whole(shapes[name]) for name in names],
        [pltpu.VMEM((rows, gate), BF16)] + weight_scratch(width, hidden)[1:],
        9_000_000_000,
        table=1,
    )(owner, upstream, valid, mixer_back, w["gain_two"], *[kept[name] for name in reads], *pieces)
    return results[0], results[1], dict(zip(names, results[2:]))


def backward_first(values, hidden_grad, upstream, w, owner, pieces):
    images, rows, width = values.shape
    hidden = hidden_grad.shape[2]
    n_p = len(pieces)

    def kernel(owner_ref, values_ref, grad_ref, up_ref, gain_ref, *refs):
        out, gain_sum, bias_sum, w_in, sem = refs[n_p:]

        @pl.when(pl.program_id(0) == 0)
        def _():
            load_blocks(owner_ref, refs[:n_p], w_in, None, sem)
            zero((gain_sum, bias_sum))

        out[0] = backward_norm(
            values_ref[0].astype(F32),
            grad_ref.at[0],
            up_ref[0],
            {"w_in": w_in, "gain_one": gain_ref},
            {"gain_one": gain_sum, "bias_one": bias_sum},
        )

    scratch = weight_scratch(width, hidden)
    return call(
        kernel,
        "backward_first",
        (images,),
        [image(rows, width), image(rows, hidden), image(rows, width), whole((1, width))] + anywhere(n_p),
        [((images, rows, width), F32)] + [((8, width), F32)] * 2,
        [image(rows, width)] + [whole((8, width))] * 2,
        [scratch[0], scratch[2]],
        6_000_000_000,
        table=1,
    )(owner, values, hidden_grad, upstream, w["gain_one"], *pieces)


def in_weight_blocks(owner, normed, hidden_grad, first, count, held):
    depth, width = normed.shape
    half = width // BLOCK // 2

    def kernel(owner_ref, left, right, one, other, result):
        result[...] = dot_first(left[...], right[...])
        for at in range(half):
            for out, block in ((one, owner_ref[at]), (other, owner_ref[half + at])):
                rows = pl.ds(pl.multiple_of(block * BLOCK, BLOCK), BLOCK)
                out[at, 0] = result[rows].astype(BF16)

    spec = pl.BlockSpec((half, 1, BLOCK, GROUP), lambda g, *unused: (0, g, 0, 0))
    return call(
        kernel,
        "in_weight_blocks",
        (count,),
        [whole((depth, width)), pl.BlockSpec((depth, GROUP), lambda g, *unused: (0, first + g))],
        [((half, held, BLOCK, GROUP), BF16)] * 2,
        [spec] * 2,
        [pltpu.VMEM((width, GROUP), F32)],
        2 * depth * width * GROUP * count,
        table=1,
    )(owner, normed, hidden_grad)


def out_weight_blocks(owner, gated, masked, into=None):
    depth, gate = gated.shape
    width = masked.shape[1]
    half = width // BLOCK // 2
    per = gate // width
    steps = gate // GROUP
    held = into[0].shape[1] if into else per
    assert held % per == 0

    def kernel(owner_ref, left, right, *refs):
        one, other, result = refs[-3:]
        step = pl.program_id(0)
        result[pl.ds(pl.multiple_of(step * GROUP, GROUP), GROUP)] = dot_first(left[...], right[...])

        @pl.when(step == steps - 1)
        def _():
            for at in range(half):
                for out, block in ((one, owner_ref[at]), (other, owner_ref[half + at])):
                    for part in range(per):
                        rows = pl.ds(pl.multiple_of((block * per + part) * BLOCK, BLOCK), BLOCK)
                        out[at, part] = result[rows].astype(BF16)

    spec = pl.BlockSpec((half, per, BLOCK, width), lambda g, *unused: (0, held // per - 1, 0, 0))
    return call(
        kernel,
        "out_weight_blocks",
        (steps,),
        [pl.BlockSpec((depth, GROUP), lambda g, *unused: (0, g)), whole((depth, width))]
        + anywhere(2 if into else 0),
        [((half, held, BLOCK, width), BF16)] * 2,
        [spec] * 2,
        [pltpu.VMEM((gate, width), F32)],
        2 * depth * width * gate,
        table=1,
        aliases={3: 0, 4: 1} if into else None,
    )(owner, gated, masked, *(into or ()))


class Tree:
    def __init__(self, devices):
        self.devices = devices
        self.far = devices // 8

    def swap(self, values, one, other=None):
        other = one if other is None else other
        pairs = [(i, i ^ (other if i % 2 else one)) for i in range(self.devices)]
        return lax.ppermute(values, AXES, pairs)

    def owners(self):
        me = lax.axis_index(AXES).astype(jnp.int32)
        odd = me % 2
        near, next_ = 2 + 2 * odd, 4 - 2 * odd
        side = jnp.arange(2, dtype=jnp.int32)[:, None, None, None]
        first = jnp.arange(2, dtype=jnp.int32)[None, :, None, None]
        second = jnp.arange(2, dtype=jnp.int32)[None, None, :, None]
        far = jnp.arange(self.far, dtype=jnp.int32)[None, None, None, :]
        one = jnp.where(side == 0, near, next_)
        two = jnp.where(side == 0, next_, near)
        return ((me ^ side) ^ (first * one) ^ (second * two) ^ (far * 8)).reshape(-1)

    def gather(self, own):
        column = jnp.stack([own] + [self.swap(own, 8 * m) for m in range(1, self.far)])
        first = self.swap(column, 2, 4)
        second = self.swap(column, 4, 2)
        both = self.swap(first, 4, 2)
        mine = [column, second, first, both]
        return mine + [self.swap(piece, 1) for piece in mine]

    def scatter(self, mine, theirs):
        far = self.far
        total = mine.astype(F32) + self.swap(theirs, 1).astype(F32)
        got = self.swap(total[2 * far :].astype(BF16), 2, 4)
        total = total[: 2 * far] + got.astype(F32)
        got = self.swap(total[far:].astype(BF16), 4, 2)
        total = total[:far] + got.astype(F32)
        last = total.astype(BF16)
        got = [self.swap(last[m], 8 * m) for m in range(1, far)]
        result = total[0]
        for part in got:
            result = result + part.astype(F32)
        return result

    def rows(self, block, groups):
        parts = []
        if groups:
            parts.append(block[:groups].transpose(1, 0, 2).reshape(BLOCK, -1))
        if groups < block.shape[0]:
            parts.append(block[groups:].reshape(-1, block.shape[2]))
        return parts

    def total(self, values):
        odd = lax.axis_index("narrow") % 2 == 1
        mine = jnp.where(odd, values[1], values[0])
        theirs = jnp.where(odd, values[0], values[1])
        mine = mine + self.swap(theirs, 1)
        mine = mine + self.swap(mine, 2, 4)
        mine = mine + self.swap(mine, 4, 2)
        bit = 8
        while bit < self.devices:
            mine = mine + self.swap(mine, bit)
            bit *= 2
        theirs = self.swap(mine, 1)
        return jnp.stack([jnp.where(odd, theirs, mine), jnp.where(odd, mine, theirs)])


class Plain:
    def __init__(self, width, gate):
        self.width, self.gate = width, gate
        self.blocks = width // BLOCK

    def owners(self):
        return jnp.arange(self.blocks, dtype=jnp.int32)

    def gather(self, own):
        w_in, w_out = (lax.all_gather(part, AXES, axis=0, tiled=True) for part in own)
        return [pack_blocks(w_in, w_out, self.blocks)]

    def scatter(self, mine, theirs):
        return jnp.concatenate([mine, theirs]).astype(F32)

    def rows(self, blocks, groups):
        parts = []
        if groups:
            parts.append(blocks[:, :groups].transpose(0, 2, 1, 3).reshape(self.width, -1))
        if groups < blocks.shape[1]:
            parts.append(blocks[:, groups:].reshape(self.gate, -1))
        return [lax.psum_scatter(part, AXES, scatter_dimension=0, tiled=True) for part in parts]

    def total(self, values):
        return lax.psum(values, AXES)


def pack_blocks(w_in, w_out, blocks):
    groups = w_in.shape[1] // GROUP
    inner = w_in.reshape(blocks, BLOCK, groups, GROUP).transpose(0, 2, 1, 3)
    outer = w_out.reshape(blocks, -1, BLOCK, GROUP)
    return jnp.concatenate([inner, outer], 1)


def bfloat_pair(values):
    top = lax.reduce_precision(values, 8, 7)
    return top.astype(BF16), lax.reduce_precision(values - top, 8, 7).astype(BF16)


def spatial_operands(valid, w_sp, b_sp, gain_two, bias_two, rows):
    images, slots = valid.shape
    gate = gain_two.shape[0]
    cut = slots // BLOCK * BLOCK
    spare = rows - slots
    masked = w_sp[None] * valid[:, None, :].astype(BF16)
    bias = jnp.broadcast_to(jnp.stack(bfloat_pair(b_sp), -1)[None], (images, slots, 2))
    mixer = jnp.concatenate([masked, bias], 2)
    mixer = jnp.pad(mixer, ((0, 0), (0, spare), (0, spare - 2)))
    column_sum = jnp.einsum("ir,pr->ip", valid.astype(BF16), w_sp, preferred_element_type=F32)
    back = jnp.concatenate([jnp.swapaxes(masked, 1, 2), jnp.stack(bfloat_pair(column_sum), 1)], 1)
    back = jnp.pad(back, ((0, 0), (0, spare - 2), (0, spare)))
    one = jnp.ones((gate,), BF16)
    pad = jnp.stack([one, one, *bfloat_pair(bias_two), *bfloat_pair(gain_two)])
    pad = jnp.pad(pad, ((slots - cut, rows - slots - 6), (0, 0))).astype(F32)
    return mixer, back, pad


def shards(
    tokens,
    mask,
    ln1_gain,
    ln1_bias,
    in_weight,
    in_bias,
    ln2_gain,
    ln2_bias,
    spatial_weight,
    spatial_bias,
    out_weight,
    out_bias,
    cotangent,
):
    devices = lax.axis_size(AXES)
    images, slots = mask.shape
    width = tokens.shape[1]
    hidden = in_weight.shape[2]
    gate = hidden // 2
    per = gate // width
    groups = hidden // GROUP
    rows = -(-(slots + 6) // BLOCK) * BLOCK
    spare = rows - slots
    pairwise = devices * BLOCK == width and devices >= 16 and devices & (devices - 1) == 0
    links = Tree(devices) if pairwise else Plain(width, gate)

    def blocks_of(layer):
        if pairwise:
            return pack_blocks(in_weight[layer], out_weight[layer], 1)[0]
        return in_weight[layer], out_weight[layer]

    owner = links.owners()
    pieces = [links.gather(blocks_of(layer)) for layer in range(2)]

    valid = mask.astype(F32)
    padded = lambda array: jnp.pad(array.reshape(images, slots, width), ((0, 0), (0, spare), (0, 0)))
    valid_column = jnp.pad(valid, ((0, 0), (0, spare)))[:, :, None]
    live = (jnp.arange(rows) < slots).astype(F32)[:, None]
    values = padded(tokens)
    layers, spatial = [], []
    for layer in range(2):
        layers.append(
            {
                "b_in": 0.5 * in_bias[layer][None],
                "gain_one": 0.5 * ln1_gain[layer][None],
                "bias_one": 0.5 * ln1_bias[layer][None],
                "gain_two": ln2_gain[layer][None],
                "bias_two": ln2_bias[layer][None],
                "b_out": out_bias[layer][None],
            }
        )
        spatial.append(
            spatial_operands(
                valid, spatial_weight[layer], spatial_bias[layer], ln2_gain[layer], ln2_bias[layer], rows
            )
        )
    flat = lambda array: array.reshape(images * rows, array.shape[2])
    mixer, back, pad = zip(*spatial)

    kept = forward_save(values, valid_column, live, mixer[0], pad[0], layers[0], owner, pieces[0], slots)
    last, last_sums = forward_backward(
        kept["values"], padded(cotangent), valid_column, live, mixer[1], back[1], pad[1], layers[1], owner, pieces[1], slots
    )

    def small_of(sums):
        cut = slots // BLOCK * BLOCK
        column = lambda name: sums[name].sum(0)
        at = slots - cut
        parts = (
            0.5 * column("gain_one"),
            0.5 * column("bias_one"),
            0.5 * column("b_in"),
            column("gain_two"),
            sums["bias_two"][at] + sums["bias_two"][at + 1],
            sums["spatial"][:slots, :slots].T.reshape(-1),
            sums["spatial"][slots, :slots],
            column("b_out"),
        )
        joined = jnp.concatenate(parts)
        size = joined.shape[0]
        full = -(-size // 2048) * 2048
        summed = links.total(jnp.pad(joined, (0, full - size)).reshape(2, -1, 128)).reshape(-1)
        ends, start = [], 0
        for part in parts:
            ends.append(summed[start : start + part.shape[0]])
            start += part.shape[0]
        ends[5] = ends[5].reshape(slots, slots)
        return ends

    mine, theirs = in_weight_blocks(owner, flat(last["normed"]), flat(last["hidden_grad"]), 0, groups, groups + per)
    mine, theirs = out_weight_blocks(owner, flat(last["gated"]), flat(last["masked"]), (mine, theirs))
    in_grad_one, out_grad_one = links.rows(links.scatter(mine, theirs), groups)
    small_one = small_of(last_sums)

    hidden_grad, masked, sums = backward_gate(
        last["upstream"], kept, valid_column, back[0], layers[0], owner, pieces[0], slots
    )
    mine, theirs = out_weight_blocks(owner, flat(kept["gated"]), flat(masked))
    (out_grad_zero,) = links.rows(links.scatter(mine, theirs), 0)
    mine, theirs = in_weight_blocks(owner, flat(kept["normed"]), flat(hidden_grad), 0, groups, groups)
    (in_grad_zero,) = links.rows(links.scatter(mine, theirs), groups)
    input_grad, sums["gain_one"], sums["bias_one"] = backward_first(
        values, hidden_grad, last["upstream"], layers[0], owner, pieces[0]
    )
    small_zero = small_of(sums)

    unpadded = lambda array: array[:, :slots].reshape(images * slots, width)
    small = [jnp.stack(pair) for pair in zip(small_zero, small_one)]
    return (
        unpadded(last["values"]),
        unpadded(input_grad),
        small[0],
        small[1],
        jnp.stack([in_grad_zero, in_grad_one]),
        small[2],
        small[3],
        small[4],
        small[5],
        small[6],
        jnp.stack([out_grad_zero, out_grad_one]),
        small[7],
    )


def solution(mesh):
    both = P(AXES, None)
    second = P(None, AXES, None)
    in_specs = (both, both, P(), P(), second, P(), P(), P(), P(), P(), second, P(), both)
    out_specs = (both, both, P(), P(), second, P(), P(), P(), P(), P(), second, P())
    return jax.shard_map(shards, mesh=mesh, in_specs=in_specs, out_specs=out_specs, check_vma=False)
```

time: 779 us -> 284 us (0.36); the launches traced: 768 us -> 282 us
  waiting for transfers between devices: 454 us -> 62.6 us
  Pallas kernels: 0 us -> 111 us
  matrix products: 96.6 us -> 0.94 us
  other arithmetic: 94 us -> 28.5 us
  starting transfers between devices: 0.28 us -> 56.3 us
  local copies, waits for them, and re-layouts: 66.8 us -> 21.5 us
  blocking collectives: 40.6 us -> 0 us
  between operations: 15.2 us -> 1.79 us
    reduce_scatter x2 -> x0, waiting for transfers between devices: 282 us -> none  [the longest x1 161 us: shards(): lax.psum_scatter(in_stack, ('wide', 'narrow'), scatter_dimension=1, tiled...]
    all_gather x4 -> x0, waiting for transfers between devices: 167 us -> none  [the longest x2 104 us: shards(): lax.all_gather(in_weight[layer_pos], ('wide', 'narrow'), axis=0, tiled=True)]
    pallas_call x0 -> x8, Pallas kernels: none -> 111 us  [the longest x1 29.4 us: forward_backward(): call(kernel, 'forward_backward', (images,), [image(rows, width)] * 2 + [i...]
    dot_general x18 -> x2, matrix products: 96.6 us -> 0.94 us  [spatial_operands(): jnp.einsum('ir,pr->ip', valid.astype(BF16), w_sp, preferred_element_type=...]
    ppermute x0 -> x50, waiting for transfers between devices: none -> 62.6 us  [swap(): return lax.ppermute(values, AXES, pairs)]
    ppermute x0 -> x50, starting transfers between devices: none -> 56.3 us  [swap(): return lax.ppermute(values, AXES, pairs)]
    psum x1 -> x0, blocking collectives: 40.6 us -> none  [shards(): lax.psum((small_stack[0], small_stack[1], small_stack[2], small_stack[3],...]
    reduce_sum x13 -> x10, other arithmetic: 42.1 us -> 1.68 us  [small_of(): column = lambda name: sums[name].sum(0)]
  transfers between devices with their start and end apart: 7 -> 50, of which waited for: 7 -> 15; matrix products, arithmetic and copies ran while one was open for 18% -> 15% of each run, Pallas kernels for 0% -> 19%
where the time goes in v1:
time: 284 us; the launch traced here: 282 us
  Pallas kernels  111 us (39%)
  waiting for transfers between devices  62.6 us (22%)
  starting transfers between devices  56.3 us (20%)
  other arithmetic  28.5 us (10%)
  local copies, waits for them, and re-layouts  21.5 us (8%)
    ppermute x50, waiting for transfers between devices, swap(): return lax.ppermute(values, AXES, pairs)  62.6 us
    ppermute x50, starting transfers between devices, swap(): return lax.ppermute(values, AXES, pairs)  56.3 us
    pallas_call x1, Pallas kernels, forward_backward(): call(kernel, 'forward_backward', (images,), [image(rows, width)] * 2 + [i...  29.4 us
    pallas_call x1, Pallas kernels, forward_save(): call(kernel, 'forward_save', (images,), [image(rows, width), image(rows,...  20.1 us
    pallas_call x2, Pallas kernels, in_weight_blocks(): call(kernel, 'in_weight_blocks', (count,), [whole((depth, width)), pl.Blo...  19.7 us
    pallas_call x1, Pallas kernels, backward_gate(): call(kernel, 'backward_gate', (images,), [image(rows, width), image(rows,...  16.4 us
    pallas_call x2, Pallas kernels, out_weight_blocks(): call(kernel, 'out_weight_blocks', (steps,), [pl.BlockSpec((depth, GROUP),...  13.1 us
    pallas_call x1, Pallas kernels, backward_first(): call(kernel, 'backward_first', (images,), [image(rows, width), image(rows...  12.2 us
  transfers between devices with their start and end apart: 50, of which 15 were waited for; matrix products, arithmetic and copies ran while one was open for 15% of the time, Pallas kernels for 19%

profile of v1, /device:TPU:0, one launch (start us, length us, event | category | flops | bytes accessed | tf_op | source)
XLA Modules:
  0.0 282.4 jit_solution(17638324733363153552)
XLA Ops:
  2.6 3.1 %collective-permute-start = (bf16[9,16,512]{2,1,0:T(8,128)(2,1)S(1)}, bf16[9,16,512]{2,1,0:T(8,128)(2,1)S(1)}, u32[]{:S(2)}, u32[]{:S(2)}) collective-permute-start(bf16[9,16,512]{2,1,0:T(8,128)(2,1)S(1)} %maximum_bitcast_fusion), channel_id=1, source_target_pairs={{0,8},{1,9},{2,10},{3,11},{4,12},{5,13},{6,14},{7,15},{8,0},{9,1},... | collective-permute-start | bytes 442376 | tf_op jit(solution)/shard_map/ppermute | solution.py:504
  5.7 2.6 collective-permute-start.1
  9.9 3.5 %collective-permute-start.11 = (bf16[9,16,512]{2,1,0:T(8,128)(2,1)}, bf16[9,16,512]{2,1,0:T(8,128)(2,1)S(1)}, u32[]{:S(2)}, u32[]{:S(2)}) collective-permute-start(bf16[9,16,512]{2,1,0:T(8,128)(2,1)} %maximum_bitcast_fusion.1), channel_id=1, source_target_pairs={{0,16},{1,17},{2,18},{3,19},{4,20},{5,21},{6,22},{7,23},{8,24},{9,... | collective-permute-start | bytes 442376 | tf_op jit(solution)/shard_map/ppermute | solution.py:504
  21.5 1.7 collective-permute-start.4
  24.9 1.5 collective-permute-start.3
  26.5 5.9 %collective-permute-done.11 = bf16[9,16,512]{2,1,0:T(8,128)(2,1)S(1)} collective-permute-done((bf16[9,16,512]{2,1,0:T(8,128)(2,1)}, bf16[9,16,512]{2,1,0:T(8,128)(2,1)S(1)}, u32[]{:S(2)}, u32[]{:S(2)}) %collective-permute-start.11) | collective-permute-done | bytes 147488 | tf_op jit(solution)/shard_map/ppermute | solution.py:504
  33.3 1.5 collective-permute-start.14
  34.8 2.8 collective-permute-done.4.refs_8_.refs_2_
  37.6 2.0 collective-permute-start.5
  41.2 1.3 reshape.283
  42.6 1.4 reshape.284
  45.0 1.1 pad.43.cot_ref
  50.2 2.0 collective-permute-start.15
  52.8 5.9 %collective-permute-done.13.refs_7_ = bf16[4,9,16,512]{3,2,1,0:T(8,128)(2,1)S(1)} collective-permute-done((bf16[4,9,16,512]{3,2,1,0:T(8,128)(2,1)}, bf16[4,9,16,512]{3,2,1,0:T(8,128)(2,1)S(1)}, u32[]{:S(2)}, u32[]{:S(2)}) %collective-permute-start.13) | collective-permute-done | bytes 589856 | tf_op jit(solution)/shard_map/ppermute | solution.py:504
  59.3 5.7 %collective-permute-done.15.refs_9_ = bf16[4,9,16,512]{3,2,1,0:T(8,128)(2,1)S(1)} collective-permute-done((bf16[4,9,16,512]{3,2,1,0:T(8,128)(2,1)}, bf16[4,9,16,512]{3,2,1,0:T(8,128)(2,1)S(1)}, u32[]{:S(2)}, u32[]{:S(2)}) %collective-permute-start.15) | collective-permute-done | bytes 589856 | tf_op jit(solution)/shard_map/ppermute | solution.py:504
  65.9 20.1 %forward_save.1 = (f32[5,208,512]{2,1,0:T(8,128)}, bf16[5,208,512]{2,1,0:T(8,128)(2,1)}, bf16[5,208,1536]{2,1,0:T(8,128)(2,1)}, bf16[5,208,1536]{2,1,0:T(8,128)(...) custom-call(s32[32]{0:T(128)} %xor.69.owner_ref, ...), custom_call_target="tpu_custom_call" | custom-call | flops 12000000000 | bytes 20000000 | tf_op jit(solution)/shard_map/forward_save/pallas_call | solution.py:273
  86.1 29.4 %forward_backward.1 = (bf16[5,208,512]{2,1,0:T(8,128)(2,1)}, bf16[5,208,512]{2,1,0:T(8,128)(2,1)}, bf16[5,208,1536]{2,1,0:T(8,128)(2,1)}, bf16[5,208,3072]{2,1,0...) custom-call(s32[32]{0:T(128)} %xor.69.owner_ref, ...), custom_call_target="tpu_custom_call" | custom-call | flops 24000000000 | bytes 20000000 | tf_op jit(solution)/shard_map/forward_backward/pallas_call | solution.py:333
  115.5 16.4 %backward_gate.1 = (bf16[5,208,3072]{2,1,0:T(8,128)(2,1)}, bf16[5,208,512]{2,1,0:T(8,128)(2,1)}, f32[8,512]{1,0:T(8,128)}, f32[8,3072]{1,0:T(8,128)}, f32[208,20...) custom-call(s32[32]{0:T(128)} %xor.69.owner_ref, f32[5,208,512]{2,1,0:T(8,128)} %get-tuple-element.54.up_ref, ...), custom_call_target="tpu_custom_call" | custom-call | flops 8999999488 | bytes 20000000 | tf_op jit(solution)/shard_map/backward_gate/pallas_call | solution.py:381
  133.6 12.2 %backward_first.1 = (f32[5,208,512]{2,1,0:T(8,128)}, f32[8,512]{1,0:T(8,128)}, f32[8,512]{1,0:T(8,128)}) custom-call(s32[32]{0:T(128)} %xor.69.owner_ref, bf16[5,208,512]{2,1,0:T(8,128)(2,1)} %pad.39.values_ref, bf16[5,208,3072]{2,1,0:T(8,128)(2,1)} %get-tuple-element.61.grad_ref, f32[5,208,512]{2,1,0:T(8,128)} %get-tuple-element.54.up_ref, ...), custom_call_target="tpu_custom_call" | custom-call | flops 6000000000 | bytes 20000000 | tf_op jit(solution)/shard_map/backward_first/pallas_call | solution.py:420
  151.1 6.6 %out_weight_blocks.3 = (bf16[16,3,16,512]{3,2,1,0:T(8,128)(2,1)}, bf16[16,3,16,512]{3,2,1,0:T(8,128)(2,1)}) custom-call(s32[32]{0:T(128)} %xor.69.owner_ref, bf16[1040,1536]{1,0:T(8,128)(2,1)} %bitcast.197, bf16[1040,512]{1,0:T(8,128)(2,1)} %bitcast.200), custom_call_target="tpu_custom_call" | custom-call | flops 1635778560 | bytes 20000000 | tf_op jit(solution)/shard_map/out_weight_blocks/pallas_call | solution.py:481
  158.1 1.6 collective-permute-start.21
  160.3 2.5 collective-permute-done.21
  162.9 1.5 collective-permute-done.27
  165.0 2.4 collective-permute-done.22
  167.5 4.9 %collective-permute-start.23 = (f32[184,128]{1,0:T(8,128)S(1)}, f32[184,128]{1,0:T(8,128)S(1)}, u32[]{:S(2)}, u32[]{:S(2)}) collective-permute-start(f32[184,128]{1,0:T(8,128)S(1)} %add.140), channel_id=1, source_target_pairs={{0,8},{1,9},{2,10},{3,11},{4,12},{5,13},{6,14},{7,15},{8,0},{9,1},... | collective-permute-start | bytes 282632 | tf_op jit(solution)/shard_map/ppermute | solution.py:504
  172.4 9.9 %in_weight_blocks.3 = (bf16[16,9,16,512]{3,2,1,0:T(8,128)(2,1)}, bf16[16,9,16,512]{3,2,1,0:T(8,128)(2,1)}) custom-call(s32[32]{0:T(128)} %xor.69.owner_ref, bf16[1040,512]{1,0:T(8,128)(2,1)} %bitcast.199, bf16[1040,3072]{1,0:T(8,128)(2,1)} %bitcast.196), custom_call_target="tpu_custom_call" | custom-call | flops 3271557120 | bytes 20000000 | tf_op jit(solution)/shard_map/in_weight_blocks/pallas_call | solution.py:445
  182.4 7.9 %collective-permute-start.24 = (f32[184,128]{1,0:T(8,128)S(1)}, f32[184,128]{1,0:T(8,128)S(1)}, u32[]{:S(2)}, u32[]{:S(2)}) collective-permute-start(f32[184,128]{1,0:T(8,128)S(1)} %add.141), channel_id=1, source_target_pairs={{0,16},{1,17},{2,18},{3,19},{4,20},{5,21},{6,22},{7,23},{8,24},{9,... | collective-permute-start | bytes 282632 | tf_op jit(solution)/shard_map/ppermute | solution.py:504
  190.3 6.5 %out_weight_blocks.2 = (bf16[16,9,16,512]{3,2,1,0:T(8,128)(2,1)}, bf16[16,9,16,512]{3,2,1,0:T(8,128)(2,1)}) custom-call(s32[32]{0:T(128)} %xor.69.owner_ref, bf16[1040,1536]{1,0:T(8,128)(2,1)} %bitcast.152, bf16[1040,512]{1,0:T(8,128)(2,1)} %bitcast.153, ...), custom_call_target="tpu_custom_call", output_to_operand_aliasing={{0}: (3, {}), {1}: (4, {})} | custom-call | flops 1635778560 | bytes 20000000 | tf_op jit(solution)/shard_map/out_weight_blocks/pallas_call | solution.py:481
  197.5 9.8 %in_weight_blocks.2 = (bf16[16,6,16,512]{3,2,1,0:T(8,128)(2,1)}, bf16[16,6,16,512]{3,2,1,0:T(8,128)(2,1)}) custom-call(s32[32]{0:T(128)} %xor.69.owner_ref, bf16[1040,512]{1,0:T(8,128)(2,1)} %bitcast.198, bf16[1040,3072]{1,0:T(8,128)(2,1)} %bitcast.195), custom_call_target="tpu_custom_call" | custom-call | flops 3271557120 | bytes 20000000 | tf_op jit(solution)/shard_map/in_weight_blocks/pallas_call | solution.py:445
  207.4 1.7 slice.287
  209.1 1.5 reshape.286
  210.7 1.1 reshape.285
  218.9 1.5 convert_add_fusion.2
  220.5 1.6 collective-permute-start.45
  222.1 2.2 convert_add_fusion.1
  225.0 2.7 convert_add_fusion
  227.9 1.6 collective-permute-start.39
  230.7 6.9 %collective-permute-done.46 = bf16[4,3,16,512]{3,2,1,0:T(8,128)(2,1)S(1)} collective-permute-done((bf16[4,3,16,512]{3,2,1,0:T(8,128)(2,1)S(1)}, bf16[4,3,16,512]{3,2,1,0:T(8,128)(2,1)S(1)}, u32[]{:S(2)}, u32[]{:S(2)}) %collective-permute-start.46) | collective-permute-done | bytes 196640 | tf_op jit(solution)/shard_map/ppermute | solution.py:504
  237.7 2.8 collective-permute-start.48
  240.6 1.6 collective-permute-start.49
  242.8 12.9 %collective-permute-done.39 = bf16[8,9,16,512]{3,2,1,0:T(8,128)(2,1)S(1)} collective-permute-done((bf16[8,9,16,512]{3,2,1,0:T(8,128)(2,1)S(1)}, bf16[8,9,16,512]{3,2,1,0:T(8,128)(2,1)S(1)}, u32[]{:S(2)}, u32[]{:S(2)}) %collective-permute-start.39) | collective-permute-done | bytes 1179680 | tf_op jit(solution)/shard_map/ppermute | solution.py:504
  257.0 2.8 collective-permute-start.36
  259.8 1.6 collective-permute-start.37
  261.3 4.8 %collective-permute-done.40 = bf16[4,9,16,512]{3,2,1,0:T(8,128)(2,1)S(1)} collective-permute-done((bf16[4,9,16,512]{3,2,1,0:T(8,128)(2,1)S(1)}, bf16[4,9,16,512]{3,2,1,0:T(8,128)(2,1)S(1)}, u32[]{:S(2)}, u32[]{:S(2)}) %collective-permute-start.40) | collective-permute-done | bytes 589856 | tf_op jit(solution)/shard_map/ppermute | solution.py:504
  266.5 2.8 collective-permute-start.42
  269.4 1.6 collective-permute-start.43
  271.2 2.3 collective-permute-done.41
  273.5 7.1 %collective-permute-done.42 = bf16[9,16,512]{2,1,0:T(8,128)(2,1)S(1)} collective-permute-done((bf16[9,16,512]{2,1,0:T(8,128)(2,1)S(1)}, bf16[9,16,512]{2,1,0:T(8,128)(2,1)S(1)}, u32[]{:S(2)}, u32[]{:S(2)}) %collective-permute-start.42) | collective-permute-done | bytes 147488 | tf_op jit(solution)/shard_map/ppermute | solution.py:504
  (292 shorter events, 46.1 us)
Async XLA Ops:
  2.6 17.1 %collective-permute-start = (bf16[9,16,512]{2,1,0:T(8,128)(2,1)S(1)}, bf16[9,16,512]{2,1,0:T(8,128)(2,1)S(1)}, u32[]{:S(2)}, u32[]{:S(2)}) collective-permute-start(bf16[9,16,512]{2,1,0:T(8,128)(2,1)S(1)} %maximum_bitcast_fusion), channel_id=1, source_target_pairs={{0,8},{1,9},{2,10},{3,11},{4,12},{5,13},{6,14},{7,15},{8,0},{9,1},... | collective-permute-start | bytes 442376 | tf_op jit(solution)/shard_map/ppermute | solution.py:504
  5.7 14.1 %collective-permute-start.1 = (bf16[9,16,512]{2,1,0:T(8,128)(2,1)S(1)}, bf16[9,16,512]{2,1,0:T(8,128)(2,1)}, u32[]{:S(2)}, u32[]{:S(2)}) collective-permute-start(bf16[9,16,512]{2,1,0:T(8,128)(2,1)S(1)} %maximum_bitcast_fusion), channel_id=1, source_target_pairs={{0,16},{1,17},{2,18},{3,19},{4,20},{5,21},{6,22},{7,23},{8,24},{9,... | collective-permute-start | bytes 442376 | tf_op jit(solution)/shard_map/ppermute | solution.py:504
  8.3 11.5 %collective-permute-start.2 = (bf16[9,16,512]{2,1,0:T(8,128)(2,1)S(1)}, bf16[9,16,512]{2,1,0:T(8,128)(2,1)S(1)}, u32[]{:S(2)}, u32[]{:S(2)}) collective-permute-start(bf16[9,16,512]{2,1,0:T(8,128)(2,1)S(1)} %maximum_bitcast_fusion), channel_id=1, source_target_pairs={{0,24},{1,25},{2,26},{3,27},{4,28},{5,29},{6,30},{7,31},{8,16},{9,... | collective-permute-start | bytes 442376 | tf_op jit(solution)/shard_map/ppermute | solution.py:504
  9.0 17.5 %collective-permute-start.10 = (bf16[9,16,512]{2,1,0:T(8,128)(2,1)}, bf16[9,16,512]{2,1,0:T(8,128)(2,1)S(1)}, u32[]{:S(2)}, u32[]{:S(2)}) collective-permute-start(bf16[9,16,512]{2,1,0:T(8,128)(2,1)} %maximum_bitcast_fusion.1), channel_id=1, source_target_pairs={{0,8},{1,9},{2,10},{3,11},{4,12},{5,13},{6,14},{7,15},{8,0},{9,1},... | collective-permute-start | bytes 442376 | tf_op jit(solution)/shard_map/ppermute | solution.py:504
  9.9 22.5 %collective-permute-start.11 = (bf16[9,16,512]{2,1,0:T(8,128)(2,1)}, bf16[9,16,512]{2,1,0:T(8,128)(2,1)S(1)}, u32[]{:S(2)}, u32[]{:S(2)}) collective-permute-start(bf16[9,16,512]{2,1,0:T(8,128)(2,1)} %maximum_bitcast_fusion.1), channel_id=1, source_target_pairs={{0,16},{1,17},{2,18},{3,19},{4,20},{5,21},{6,22},{7,23},{8,24},{9,... | collective-permute-start | bytes 442376 | tf_op jit(solution)/shard_map/ppermute | solution.py:504
  19.7 12.6 %collective-permute-start.12 = (bf16[9,16,512]{2,1,0:T(8,128)(2,1)}, bf16[9,16,512]{2,1,0:T(8,128)(2,1)S(1)}, u32[]{:S(2)}, u32[]{:S(2)}) collective-permute-start(bf16[9,16,512]{2,1,0:T(8,128)(2,1)} %maximum_bitcast_fusion.1), channel_id=1, source_target_pairs={{0,24},{1,25},{2,26},{3,27},{4,28},{5,29},{6,30},{7,31},{8,16},{9,... | collective-permute-start | bytes 442376 | tf_op jit(solution)/shard_map/ppermute | solution.py:504
  21.5 16.0 %collective-permute-start.4 = (bf16[4,9,16,512]{3,2,1,0:T(8,128)(2,1)S(1)}, bf16[4,9,16,512]{3,2,1,0:T(8,128)(2,1)}, u32[]{:S(2)}, u32[]{:S(2)}) collective-permute-start(bf16[4,9,16,512]{3,2,1,0:T(8,128)(2,1)S(1)} %pad_maximum_fusion.refs_6_.refs_0_), channel_id=1, source_target_pairs={{0,2},{1,5},{2,0},{3,7},{4,6},{5,1},{6,4},{7,3},{8,10},{9,13},{10,... | collective-permute-start | bytes 1769480 | tf_op jit(solution)/shard_map/ppermute | solution.py:504
  24.9 23.7 %collective-permute-start.3 = (bf16[4,9,16,512]{3,2,1,0:T(8,128)(2,1)S(1)}, bf16[4,9,16,512]{3,2,1,0:T(8,128)(2,1)}, u32[]{:S(2)}, u32[]{:S(2)}) collective-permute-start(bf16[4,9,16,512]{3,2,1,0:T(8,128)(2,1)S(1)} %pad_maximum_fusion.refs_6_.refs_0_), channel_id=1, source_target_pairs={{0,4},{1,3},{2,6},{3,1},{4,0},{5,7},{6,2},{7,5},{8,12},{9,11},{10,... | collective-permute-start | bytes 1769480 | tf_op jit(solution)/shard_map/ppermute | solution.py:504
  26.5 22.2 %collective-permute-start.6 = (bf16[4,9,16,512]{3,2,1,0:T(8,128)(2,1)S(1)}, bf16[4,9,16,512]{3,2,1,0:T(8,128)(2,1)}, u32[]{:S(2)}, u32[]{:S(2)}) collective-permute-start(bf16[4,9,16,512]{3,2,1,0:T(8,128)(2,1)S(1)} %pad_maximum_fusion.refs_6_.refs_0_), channel_id=1, source_target_pairs={{0,1},{1,0},{2,3},{3,2},{4,5},{5,4},{6,7},{7,6},{8,9},{9,8},{10,11... | collective-permute-start | bytes 1769480 | tf_op jit(solution)/shard_map/ppermute | solution.py:504
  33.3 16.9 %collective-permute-start.14 = (bf16[4,9,16,512]{3,2,1,0:T(8,128)(2,1)}, bf16[4,9,16,512]{3,2,1,0:T(8,128)(2,1)}, u32[]{:S(2)}, u32[]{:S(2)}) collective-permute-start(bf16[4,9,16,512]{3,2,1,0:T(8,128)(2,1)} %pad_maximum_fusion.1.refs_6_), channel_id=1, source_target_pairs={{0,2},{1,5},{2,0},{3,7},{4,6},{5,1},{6,4},{7,3},{8,10},{9,13},{10,... | collective-permute-start | bytes 1769480 | tf_op jit(solution)/shard_map/ppermute | solution.py:504
  37.6 14.6 %collective-permute-start.5 = (bf16[4,9,16,512]{3,2,1,0:T(8,128)(2,1)}, bf16[4,9,16,512]{3,2,1,0:T(8,128)(2,1)}, u32[]{:S(2)}, u32[]{:S(2)}) collective-permute-start(bf16[4,9,16,512]{3,2,1,0:T(8,128)(2,1)} %collective-permute-done.4.refs_8_.refs_2_), channel_id=1, source_target_pairs={{0,4},{1,3},{2,6},{3,1},{4,0},{5,7},{6,2},{7,5},{8,12},{9,11},{10,... | collective-permute-start | bytes 1769480 | tf_op jit(solution)/shard_map/ppermute | solution.py:504
  48.6 10.1 %collective-permute-start.13 = (bf16[4,9,16,512]{3,2,1,0:T(8,128)(2,1)}, bf16[4,9,16,512]{3,2,1,0:T(8,128)(2,1)S(1)}, u32[]{:S(2)}, u32[]{:S(2)}) collective-permute-start(bf16[4,9,16,512]{3,2,1,0:T(8,128)(2,1)} %pad_maximum_fusion.1.refs_6_), channel_id=1, source_target_pairs={{0,4},{1,3},{2,6},{3,1},{4,0},{5,7},{6,2},{7,5},{8,12},{9,11},{10,... | collective-permute-start | bytes 1769480 | tf_op jit(solution)/shard_map/ppermute | solution.py:504
  48.7 10.1 %collective-permute-start.8 = (bf16[4,9,16,512]{3,2,1,0:T(8,128)(2,1)}, bf16[4,9,16,512]{3,2,1,0:T(8,128)(2,1)S(1)}, u32[]{:S(2)}, u32[]{:S(2)}) collective-permute-start(bf16[4,9,16,512]{3,2,1,0:T(8,128)(2,1)} %collective-permute-done.4.refs_8_.refs_2_), channel_id=1, source_target_pairs={{0,1},{1,0},{2,3},{3,2},{4,5},{5,4},{6,7},{7,6},{8,9},{9,8},{10,11... | collective-permute-start | bytes 1769480 | tf_op jit(solution)/shard_map/ppermute | solution.py:504
  48.7 10.6 %collective-permute-start.7 = (bf16[4,9,16,512]{3,2,1,0:T(8,128)(2,1)}, bf16[4,9,16,512]{3,2,1,0:T(8,128)(2,1)S(1)}, u32[]{:S(2)}, u32[]{:S(2)}) collective-permute-start(bf16[4,9,16,512]{3,2,1,0:T(8,128)(2,1)} %collective-permute-done.3.refs_7_.refs_1_), channel_id=1, source_target_pairs={{0,1},{1,0},{2,3},{3,2},{4,5},{5,4},{6,7},{7,6},{8,9},{9,8},{10,11... | collective-permute-start | bytes 1769480 | tf_op jit(solution)/shard_map/ppermute | solution.py:504
  50.2 14.8 %collective-permute-start.15 = (bf16[4,9,16,512]{3,2,1,0:T(8,128)(2,1)}, bf16[4,9,16,512]{3,2,1,0:T(8,128)(2,1)S(1)}, u32[]{:S(2)}, u32[]{:S(2)}) collective-permute-start(bf16[4,9,16,512]{3,2,1,0:T(8,128)(2,1)} %collective-permute-done.14.refs_8_), channel_id=1, source_target_pairs={{0,4},{1,3},{2,6},{3,1},{4,0},{5,7},{6,2},{7,5},{8,12},{9,11},{10,... | collective-permute-start | bytes 1769480 | tf_op jit(solution)/shard_map/ppermute | solution.py:504
  52.2 12.9 %collective-permute-start.9 = (bf16[4,9,16,512]{3,2,1,0:T(8,128)(2,1)}, bf16[4,9,16,512]{3,2,1,0:T(8,128)(2,1)S(1)}, u32[]{:S(2)}, u32[]{:S(2)}) collective-permute-start(bf16[4,9,16,512]{3,2,1,0:T(8,128)(2,1)} %collective-permute-done.5.refs_9_.refs_3_), channel_id=1, source_target_pairs={{0,1},{1,0},{2,3},{3,2},{4,5},{5,4},{6,7},{7,6},{8,9},{9,8},{10,11... | collective-permute-start | bytes 1769480 | tf_op jit(solution)/shard_map/ppermute | solution.py:504
  58.7 27.3 %collective-permute-start.16 = (bf16[4,9,16,512]{3,2,1,0:T(8,128)(2,1)}, bf16[4,9,16,512]{3,2,1,0:T(8,128)(2,1)}, u32[]{:S(2)}, u32[]{:S(2)}) collective-permute-start(bf16[4,9,16,512]{3,2,1,0:T(8,128)(2,1)} %pad_maximum_fusion.1.refs_6_), channel_id=1, source_target_pairs={{0,1},{1,0},{2,3},{3,2},{4,5},{5,4},{6,7},{7,6},{8,9},{9,8},{10,11... | collective-permute-start | bytes 1769480 | tf_op jit(solution)/shard_map/ppermute | solution.py:504
  58.7 27.3 %collective-permute-start.18 = (bf16[4,9,16,512]{3,2,1,0:T(8,128)(2,1)}, bf16[4,9,16,512]{3,2,1,0:T(8,128)(2,1)}, u32[]{:S(2)}, u32[]{:S(2)}) collective-permute-start(bf16[4,9,16,512]{3,2,1,0:T(8,128)(2,1)} %collective-permute-done.14.refs_8_), channel_id=1, source_target_pairs={{0,1},{1,0},{2,3},{3,2},{4,5},{5,4},{6,7},{7,6},{8,9},{9,8},{10,11... | collective-permute-start | bytes 1769480 | tf_op jit(solution)/shard_map/ppermute | solution.py:504
  59.2 26.8 %collective-permute-start.17 = (bf16[4,9,16,512]{3,2,1,0:T(8,128)(2,1)S(1)}, bf16[4,9,16,512]{3,2,1,0:T(8,128)(2,1)}, u32[]{:S(2)}, u32[]{:S(2)}) collective-permute-start(bf16[4,9,16,512]{3,2,1,0:T(8,128)(2,1)S(1)} %collective-permute-done.13.refs_7_), channel_id=1, source_target_pairs={{0,1},{1,0},{2,3},{3,2},{4,5},{5,4},{6,7},{7,6},{8,9},{9,8},{10,11... | collective-permute-start | bytes 1769480 | tf_op jit(solution)/shard_map/ppermute | solution.py:504
  65.0 21.0 %collective-permute-start.19 = (bf16[4,9,16,512]{3,2,1,0:T(8,128)(2,1)S(1)}, bf16[4,9,16,512]{3,2,1,0:T(8,128)(2,1)}, u32[]{:S(2)}, u32[]{:S(2)}) collective-permute-start(bf16[4,9,16,512]{3,2,1,0:T(8,128)(2,1)S(1)} %collective-permute-done.15.refs_9_), channel_id=1, source_target_pairs={{0,1},{1,0},{2,3},{3,2},{4,5},{5,4},{6,7},{7,6},{8,9},{9,8},{10,11... | collective-permute-start | bytes 1769480 | tf_op jit(solution)/shard_map/ppermute | solution.py:504
  148.9 9.3 %collective-permute-start.20 = (f32[184,128]{1,0:T(8,128)S(1)}, f32[184,128]{1,0:T(8,128)S(1)}, u32[]{:S(2)}, u32[]{:S(2)}) collective-permute-start(f32[184,128]{1,0:T(8,128)S(1)} %select_bitcast_fusion.5), channel_id=1, source_target_pairs={{0,1},{1,0},{2,3},{3,2},{4,5},{5,4},{6,7},{7,6},{8,9},{9,8},{10,11... | collective-permute-start | bytes 282632 | tf_op jit(solution)/shard_map/ppermute | solution.py:504
  151.0 8.7 %collective-permute-start.26 = (f32[184,128]{1,0:T(8,128)S(1)}, f32[184,128]{1,0:T(8,128)S(1)}, u32[]{:S(2)}, u32[]{:S(2)}) collective-permute-start(f32[184,128]{1,0:T(8,128)S(1)} %select_bitcast_fusion.2), channel_id=1, source_target_pairs={{0,1},{1,0},{2,3},{3,2},{4,5},{5,4},{6,7},{7,6},{8,9},{9,8},{10,11... | collective-permute-start | bytes 282632 | tf_op jit(solution)/shard_map/ppermute | solution.py:504
  157.7 61.2 %collective-permute-start.44 = (bf16[16,3,16,512]{3,2,1,0:T(8,128)(2,1)}, bf16[16,3,16,512]{3,2,1,0:T(8,128)(2,1)}, u32[]{:S(2)}, u32[]{:S(2)}) collective-permute-start(bf16[16,3,16,512]{3,2,1,0:T(8,128)(2,1)} %get-tuple-element.91), channel_id=1, source_target_pairs={{0,1},{1,0},{2,3},{3,2},{4,5},{5,4},{6,7},{7,6},{8,9},{9,8},{10,11... | collective-permute-start | bytes 2359304 | tf_op jit(solution)/shard_map/ppermute | solution.py:504
  158.1 4.6 %collective-permute-start.21 = (f32[184,128]{1,0:T(8,128)S(1)}, f32[184,128]{1,0:T(8,128)S(1)}, u32[]{:S(2)}, u32[]{:S(2)}) collective-permute-start(f32[184,128]{1,0:T(8,128)S(1)} %bitcast_add_fusion.1), channel_id=1, source_target_pairs={{0,2},{1,5},{2,0},{3,7},{4,6},{5,1},{6,4},{7,3},{8,10},{9,13},{10,... | collective-permute-start | bytes 282632 | tf_op jit(solution)/shard_map/ppermute | solution.py:504
  159.7 4.6 %collective-permute-start.27 = (f32[184,128]{1,0:T(8,128)S(1)}, f32[184,128]{1,0:T(8,128)S(1)}, u32[]{:S(2)}, u32[]{:S(2)}) collective-permute-start(f32[184,128]{1,0:T(8,128)S(1)} %bitcast_add_fusion), channel_id=1, source_target_pairs={{0,2},{1,5},{2,0},{3,7},{4,6},{5,1},{6,4},{7,3},{8,10},{9,13},{10,... | collective-permute-start | bytes 282632 | tf_op jit(solution)/shard_map/ppermute | solution.py:504
  164.4 17.8 %collective-permute-start.28 = (f32[184,128]{1,0:T(8,128)S(1)}, f32[184,128]{1,0:T(8,128)S(1)}, u32[]{:S(2)}, u32[]{:S(2)}) collective-permute-start(f32[184,128]{1,0:T(8,128)S(1)} %fusion.77), channel_id=1, source_target_pairs={{0,4},{1,3},{2,6},{3,1},{4,0},{5,7},{6,2},{7,5},{8,12},{9,11},{10,... | collective-permute-start | bytes 282632 | tf_op jit(solution)/shard_map/ppermute | solution.py:504
  167.5 14.9 %collective-permute-start.23 = (f32[184,128]{1,0:T(8,128)S(1)}, f32[184,128]{1,0:T(8,128)S(1)}, u32[]{:S(2)}, u32[]{:S(2)}) collective-permute-start(f32[184,128]{1,0:T(8,128)S(1)} %add.140), channel_id=1, source_target_pairs={{0,8},{1,9},{2,10},{3,11},{4,12},{5,13},{6,14},{7,15},{8,0},{9,1},... | collective-permute-start | bytes 282632 | tf_op jit(solution)/shard_map/ppermute | solution.py:504
  182.3 14.6 %collective-permute-start.29 = (f32[184,128]{1,0:T(8,128)S(1)}, f32[184,128]{1,0:T(8,128)S(1)}, u32[]{:S(2)}, u32[]{:S(2)}) collective-permute-start(f32[184,128]{1,0:T(8,128)S(1)} %add.147), channel_id=1, source_target_pairs={{0,8},{1,9},{2,10},{3,11},{4,12},{5,13},{6,14},{7,15},{8,0},{9,1},... | collective-permute-start | bytes 282632 | tf_op jit(solution)/shard_map/ppermute | solution.py:504
  182.4 14.6 %collective-permute-start.24 = (f32[184,128]{1,0:T(8,128)S(1)}, f32[184,128]{1,0:T(8,128)S(1)}, u32[]{:S(2)}, u32[]{:S(2)}) collective-permute-start(f32[184,128]{1,0:T(8,128)S(1)} %add.141), channel_id=1, source_target_pairs={{0,16},{1,17},{2,18},{3,19},{4,20},{5,21},{6,22},{7,23},{8,24},{9,... | collective-permute-start | bytes 282632 | tf_op jit(solution)/shard_map/ppermute | solution.py:504
  196.8 28.2 %collective-permute-start.38 = (bf16[16,9,16,512]{3,2,1,0:T(8,128)(2,1)}, bf16[16,9,16,512]{3,2,1,0:T(8,128)(2,1)}, u32[]{:S(2)}, u32[]{:S(2)}) collective-permute-start(bf16[16,9,16,512]{3,2,1,0:T(8,128)(2,1)} %get-tuple-element.87), channel_id=1, source_target_pairs={{0,1},{1,0},{2,3},{3,2},{4,5},{5,4},{6,7},{7,6},{8,9},{9,8},{10,11... | collective-permute-start | bytes 7077896 | tf_op jit(solution)/shard_map/ppermute | solution.py:504
  196.8 15.0 %collective-permute-start.30 = (f32[184,128]{1,0:T(8,128)S(1)}, f32[184,128]{1,0:T(8,128)S(1)}, u32[]{:S(2)}, u32[]{:S(2)}) collective-permute-start(f32[184,128]{1,0:T(8,128)S(1)} %add.148), channel_id=1, source_target_pairs={{0,16},{1,17},{2,18},{3,19},{4,20},{5,21},{6,22},{7,23},{8,24},{9,... | collective-permute-start | bytes 282632 | tf_op jit(solution)/shard_map/ppermute | solution.py:504
  197.0 15.4 %collective-permute-start.25 = (f32[184,128]{1,0:T(8,128)S(1)}, f32[184,128]{1,0:T(8,128)S(1)}, u32[]{:S(2)}, u32[]{:S(2)}) collective-permute-start(f32[184,128]{1,0:T(8,128)S(1)} %add.142), channel_id=1, source_target_pairs={{0,1},{1,0},{2,3},{3,2},{4,5},{5,4},{6,7},{7,6},{8,9},{9,8},{10,11... | collective-permute-start | bytes 282632 | tf_op jit(solution)/shard_map/ppermute | solution.py:504
  207.4 14.7 %collective-permute-start.32 = (bf16[16,6,16,512]{3,2,1,0:T(8,128)(2,1)}, bf16[16,6,16,512]{3,2,1,0:T(8,128)(2,1)}, u32[]{:S(2)}, u32[]{:S(2)}) collective-permute-start(bf16[16,6,16,512]{3,2,1,0:T(8,128)(2,1)} %get-tuple-element.79), channel_id=1, source_target_pairs={{0,1},{1,0},{2,3},{3,2},{4,5},{5,4},{6,7},{7,6},{8,9},{9,8},{10,11... | collective-permute-start | bytes 4718600 | tf_op jit(solution)/shard_map/ppermute | solution.py:504
  220.5 9.0 %collective-permute-start.45 = (bf16[8,3,16,512]{3,2,1,0:T(8,128)(2,1)S(1)}, bf16[8,3,16,512]{3,2,1,0:T(8,128)(2,1)S(1)}, u32[]{:S(2)}, u32[]{:S(2)}) collective-permute-start(bf16[8,3,16,512]{3,2,1,0:T(8,128)(2,1)S(1)} %slice.472), channel_id=1, source_target_pairs={{0,2},{1,5},{2,0},{3,7},{4,6},{5,1},{6,4},{7,3},{8,10},{9,13},{10,... | collective-permute-start | bytes 1179656 | tf_op jit(solution)/shard_map/ppermute | solution.py:504
  224.4 17.7 %collective-permute-start.33 = (bf16[8,6,16,512]{3,2,1,0:T(8,128)(2,1)S(1)}, bf16[8,6,16,512]{3,2,1,0:T(8,128)(2,1)S(1)}, u32[]{:S(2)}, u32[]{:S(2)}) collective-permute-start(bf16[8,6,16,512]{3,2,1,0:T(8,128)(2,1)S(1)} %slice.470), channel_id=1, source_target_pairs={{0,2},{1,5},{2,0},{3,7},{4,6},{5,1},{6,4},{7,3},{8,10},{9,13},{10,... | collective-permute-start | bytes 2359304 | tf_op jit(solution)/shard_map/ppermute | solution.py:504
  227.9 27.8 %collective-permute-start.39 = (bf16[8,9,16,512]{3,2,1,0:T(8,128)(2,1)S(1)}, bf16[8,9,16,512]{3,2,1,0:T(8,128)(2,1)S(1)}, u32[]{:S(2)}, u32[]{:S(2)}) collective-permute-start(bf16[8,9,16,512]{3,2,1,0:T(8,128)(2,1)S(1)} %slice.469), channel_id=1, source_target_pairs={{0,2},{1,5},{2,0},{3,7},{4,6},{5,1},{6,4},{7,3},{8,10},{9,13},{10,... | collective-permute-start | bytes 3538952 | tf_op jit(solution)/shard_map/ppermute | solution.py:504
  229.7 7.9 %collective-permute-start.46 = (bf16[4,3,16,512]{3,2,1,0:T(8,128)(2,1)S(1)}, bf16[4,3,16,512]{3,2,1,0:T(8,128)(2,1)S(1)}, u32[]{:S(2)}, u32[]{:S(2)}) collective-permute-start(bf16[4,3,16,512]{3,2,1,0:T(8,128)(2,1)S(1)} %slice.474), channel_id=1, source_target_pairs={{0,4},{1,3},{2,6},{3,1},{4,0},{5,7},{6,2},{7,5},{8,12},{9,11},{10,... | collective-permute-start | bytes 589832 | tf_op jit(solution)/shard_map/ppermute | solution.py:504
  237.7 19.0 %collective-permute-start.47 = (bf16[3,16,512]{2,1,0:T(8,128)(2,1)S(1)}, bf16[3,16,512]{2,1,0:T(8,128)(2,1)S(1)}, u32[]{:S(2)}, u32[]{:S(2)}) collective-permute-start(bf16[3,16,512]{2,1,0:T(8,128)(2,1)S(1)} %get-tuple-element.130), channel_id=1, source_target_pairs={{0,8},{1,9},{2,10},{3,11},{4,12},{5,13},{6,14},{7,15},{8,0},{9,1},... | collective-permute-start | bytes 147464 | tf_op jit(solution)/shard_map/ppermute | solution.py:504
  237.7 18.9 %collective-permute-start.48 = (bf16[3,16,512]{2,1,0:T(8,128)(2,1)S(1)}, bf16[3,16,512]{2,1,0:T(8,128)(2,1)S(1)}, u32[]{:S(2)}, u32[]{:S(2)}) collective-permute-start(bf16[3,16,512]{2,1,0:T(8,128)(2,1)S(1)} %get-tuple-element.132), channel_id=1, source_target_pairs={{0,16},{1,17},{2,18},{3,19},{4,20},{5,21},{6,22},{7,23},{8,24},{9,... | collective-permute-start | bytes 147464 | tf_op jit(solution)/shard_map/ppermute | solution.py:504
  240.6 16.1 %collective-permute-start.49 = (bf16[3,16,512]{2,1,0:T(8,128)(2,1)S(1)}, bf16[3,16,512]{2,1,0:T(8,128)(2,1)S(1)}, u32[]{:S(2)}, u32[]{:S(2)}) collective-permute-start(bf16[3,16,512]{2,1,0:T(8,128)(2,1)S(1)} %get-tuple-element.131), channel_id=1, source_target_pairs={{0,24},{1,25},{2,26},{3,27},{4,28},{5,29},{6,30},{7,31},{8,16},{9,... | collective-permute-start | bytes 147464 | tf_op jit(solution)/shard_map/ppermute | solution.py:504
  242.4 14.3 %collective-permute-start.34 = (bf16[4,6,16,512]{3,2,1,0:T(8,128)(2,1)S(1)}, bf16[4,6,16,512]{3,2,1,0:T(8,128)(2,1)S(1)}, u32[]{:S(2)}, u32[]{:S(2)}) collective-permute-start(bf16[4,6,16,512]{3,2,1,0:T(8,128)(2,1)S(1)} %slice.473), channel_id=1, source_target_pairs={{0,4},{1,3},{2,6},{3,1},{4,0},{5,7},{6,2},{7,5},{8,12},{9,11},{10,... | collective-permute-start | bytes 1179656 | tf_op jit(solution)/shard_map/ppermute | solution.py:504
  256.2 9.9 %collective-permute-start.40 = (bf16[4,9,16,512]{3,2,1,0:T(8,128)(2,1)S(1)}, bf16[4,9,16,512]{3,2,1,0:T(8,128)(2,1)S(1)}, u32[]{:S(2)}, u32[]{:S(2)}) collective-permute-start(bf16[4,9,16,512]{3,2,1,0:T(8,128)(2,1)S(1)} %slice.471), channel_id=1, source_target_pairs={{0,4},{1,3},{2,6},{3,1},{4,0},{5,7},{6,2},{7,5},{8,12},{9,11},{10,... | collective-permute-start | bytes 1769480 | tf_op jit(solution)/shard_map/ppermute | solution.py:504
  256.9 12.5 %collective-permute-start.35 = (bf16[6,16,512]{2,1,0:T(8,128)(2,1)S(1)}, bf16[6,16,512]{2,1,0:T(8,128)(2,1)S(1)}, u32[]{:S(2)}, u32[]{:S(2)}) collective-permute-start(bf16[6,16,512]{2,1,0:T(8,128)(2,1)S(1)} %get-tuple-element.125), channel_id=1, source_target_pairs={{0,8},{1,9},{2,10},{3,11},{4,12},{5,13},{6,14},{7,15},{8,0},{9,1},... | collective-permute-start | bytes 294920 | tf_op jit(solution)/shard_map/ppermute | solution.py:504
  257.0 13.9 %collective-permute-start.36 = (bf16[6,16,512]{2,1,0:T(8,128)(2,1)S(1)}, bf16[6,16,512]{2,1,0:T(8,128)(2,1)S(1)}, u32[]{:S(2)}, u32[]{:S(2)}) collective-permute-start(bf16[6,16,512]{2,1,0:T(8,128)(2,1)S(1)} %get-tuple-element.127), channel_id=1, source_target_pairs={{0,16},{1,17},{2,18},{3,19},{4,20},{5,21},{6,22},{7,23},{8,24},{9,... | collective-permute-start | bytes 294920 | tf_op jit(solution)/shard_map/ppermute | solution.py:504
  259.8 11.1 %collective-permute-start.37 = (bf16[6,16,512]{2,1,0:T(8,128)(2,1)S(1)}, bf16[6,16,512]{2,1,0:T(8,128)(2,1)S(1)}, u32[]{:S(2)}, u32[]{:S(2)}) collective-permute-start(bf16[6,16,512]{2,1,0:T(8,128)(2,1)S(1)} %get-tuple-element.126), channel_id=1, source_target_pairs={{0,24},{1,25},{2,26},{3,27},{4,28},{5,29},{6,30},{7,31},{8,16},{9,... | collective-permute-start | bytes 294920 | tf_op jit(solution)/shard_map/ppermute | solution.py:504
  266.5 7.1 %collective-permute-start.41 = (bf16[9,16,512]{2,1,0:T(8,128)(2,1)S(1)}, bf16[9,16,512]{2,1,0:T(8,128)(2,1)S(1)}, u32[]{:S(2)}, u32[]{:S(2)}) collective-permute-start(bf16[9,16,512]{2,1,0:T(8,128)(2,1)S(1)} %get-tuple-element.122), channel_id=1, source_target_pairs={{0,8},{1,9},{2,10},{3,11},{4,12},{5,13},{6,14},{7,15},{8,0},{9,1},... | collective-permute-start | bytes 442376 | tf_op jit(solution)/shard_map/ppermute | solution.py:504
  266.5 14.1 %collective-permute-start.42 = (bf16[9,16,512]{2,1,0:T(8,128)(2,1)S(1)}, bf16[9,16,512]{2,1,0:T(8,128)(2,1)S(1)}, u32[]{:S(2)}, u32[]{:S(2)}) collective-permute-start(bf16[9,16,512]{2,1,0:T(8,128)(2,1)S(1)} %get-tuple-element.124), channel_id=1, source_target_pairs={{0,16},{1,17},{2,18},{3,19},{4,20},{5,21},{6,22},{7,23},{8,24},{9,... | collective-permute-start | bytes 442376 | tf_op jit(solution)/shard_map/ppermute | solution.py:504
  269.4 11.3 %collective-permute-start.43 = (bf16[9,16,512]{2,1,0:T(8,128)(2,1)S(1)}, bf16[9,16,512]{2,1,0:T(8,128)(2,1)S(1)}, u32[]{:S(2)}, u32[]{:S(2)}) collective-permute-start(bf16[9,16,512]{2,1,0:T(8,128)(2,1)S(1)} %get-tuple-element.123), channel_id=1, source_target_pairs={{0,24},{1,25},{2,26},{3,27},{4,28},{5,29},{6,30},{7,31},{8,16},{9,... | collective-permute-start | bytes 442376 | tf_op jit(solution)/shard_map/ppermute | solution.py:504
  (36 other events, 276.8 us)

commit v2 on v1

v2 whole, which is shorter than its diff:
```python
import jax
import jax.numpy as jnp
import numpy as np
from jax import lax
from jax.experimental import pallas as pl
from jax.experimental.pallas import tpu as pltpu
from jax.sharding import PartitionSpec as P

EPS = 1e-05
AXES = ("wide", "narrow")
F32 = jnp.float32
BF16 = jnp.bfloat16
TANH_ONE = 2 * 0.7978845608028654
TANH_THREE = 8 * 0.7978845608028654 * 0.044715
COLUMNS = 256
BLOCK = 16
GROUP = 512
STRIP = 256
WEIGHTS = ("b_in", "gain_one", "bias_one", "gain_two", "bias_two")
SUMS = ("b_out", "b_left", "b_right", "spatial", "gain_two", "bias_two", "gain_one", "bias_one")


def dot(a, b):
    return jnp.dot(a, b, preferred_element_type=F32)


def dot_last(a, b):
    return lax.dot_general(a, b, (((1,), (1,)), ((), ())), preferred_element_type=F32)


def dot_first(a, b):
    return lax.dot_general(a, b, (((0,), (0,)), ((), ())), preferred_element_type=F32)


def gelu_pair(half):
    square = half * half
    tanh = jnp.tanh(half * (TANH_ONE + TANH_THREE * square))
    upper = 1.0 + tanh
    value = half * upper
    slope = upper + value * (1.0 - tanh) * (TANH_ONE + (3 * TANH_THREE) * square)
    return value, slope


def fold_rows(values):
    total = values[:8]
    for row in range(8, values.shape[0], 8):
        total = total + values[row : row + 8]
    return total


def fold_columns(values):
    total = values[:, :128]
    for column in range(128, values.shape[1], 128):
        total = total + values[:, column : column + 128]
    return total


def white_of(values):
    centred = values - jnp.mean(values, -1, keepdims=True)
    inverse = lax.rsqrt(jnp.mean(centred * centred, -1, keepdims=True) + EPS)
    return centred * inverse, inverse


def cuts(width):
    return [slice(c, c + COLUMNS) for c in range(0, width, COLUMNS)]


def in_columns(w_in, start):
    at = start % GROUP
    return w_in[start // GROUP, :, at : at + COLUMNS]


def forward_image(values, live, mixer, slot_pad, w, t, slots):
    rows = values.shape[0]
    half_width = t["white"].shape[1]
    cut = slots // BLOCK * BLOCK
    white_one, unused_inverse = white_of(values)
    t["normed"][...] = (white_one * w["gain_one"][...] + w["bias_one"][...]).astype(BF16)
    total = None
    for sl in cuts(half_width):
        at = half_width + sl.start
        half = dot(t["normed"][...], in_columns(w["w_in"], at)) + w["b_in"][:, at : at + COLUMNS]
        value, slope = gelu_pair(half)
        t["right"][:, sl] = value
        t["right_slope"][:, sl] = slope.astype(BF16)
        part = fold_columns(value)
        total = part if total is None else total + part
    average = jnp.sum(total, -1, keepdims=True) * (1.0 / half_width)
    total = None
    for sl in cuts(half_width):
        centred = t["right"][:, sl] - average
        part = fold_columns(centred * centred)
        total = part if total is None else total + part
    spread = jnp.sum(total, -1, keepdims=True) * (1.0 / half_width)
    inverse = lax.rsqrt(spread + EPS) * live
    row = lax.broadcasted_iota(jnp.int32, (rows - cut, COLUMNS), 0)
    for sl in cuts(half_width):
        white = (t["right"][:, sl] - average) * inverse
        t["white"][:, sl] = white.astype(BF16)
        slot_in = white * w["gain_two"][:, sl] + w["bias_two"][:, sl]
        t["slot_in"][:cut, sl] = slot_in[:cut].astype(BF16)
        last = jnp.where(row < slots - cut, slot_in[cut:], slot_pad[:, sl])
        t["slot_in"][cut:, sl] = last.astype(BF16)
    for sl in cuts(half_width):
        half = dot(t["normed"][...], in_columns(w["w_in"], sl.start)) + w["b_in"][:, sl]
        left, slope = gelu_pair(half)
        mixed = dot(mixer, t["slot_in"][:, sl])
        t["gated"][:, sl] = (left * mixed).astype(BF16)
        t["left"][:, sl] = left.astype(BF16)
        t["left_slope"][:, sl] = (mixed * slope).astype(BF16)
    return inverse


def add_branch(values, gated, valid, w_out, b_out):
    branch = dot(gated, w_out[...].reshape(gated.shape[1], -1)) * valid
    return values + (branch + b_out[...])


def backward_left(upstream, w_out, left, left_slope, mixed_grad, hidden_grad, b_in_sum):
    for sl in cuts(mixed_grad.shape[1]):
        blocks = slice(sl.start // BLOCK, sl.stop // BLOCK)
        gated_grad = dot_last(upstream, w_out[blocks].reshape(COLUMNS, -1))
        mixed_grad[:, sl] = (gated_grad * left[:, sl].astype(F32)).astype(BF16)
        left_grad = gated_grad * left_slope[:, sl].astype(F32)
        hidden_grad[:, sl] = left_grad.astype(BF16)
        b_in_sum[:, sl] += fold_rows(left_grad)


def backward_right(valid, mixer_back, inverse, gain_two, t, hidden_grad, b_in_sum, sums, slots):
    rows = valid.shape[0]
    half_width = t["white"].shape[1]
    cut = slots // BLOCK * BLOCK
    outer = dot_last(t["slot_in"][...], t["mixed_grad"][...])
    is_slot = lax.broadcasted_iota(jnp.int32, (rows, 1), 0) < slots
    sums["spatial"][:rows, :rows] += outer * jnp.where(is_slot, valid, 1.0)
    back = mixer_back.astype(F32)
    by_bias = outer[slots + 2 : slots + 3] + outer[slots + 3 : slots + 4]
    by_gain = outer[slots + 4 : slots + 5] + outer[slots + 5 : slots + 6]
    mean_scaled = jnp.sum(back * by_gain, -1, keepdims=True) * (1.0 / half_width)
    mean_white = jnp.sum(back * (outer - by_bias), -1, keepdims=True) * (1.0 / half_width)
    for sl in cuts(half_width):
        slot_grad = dot(mixer_back, t["mixed_grad"][:, sl])
        white = t["white"][:, sl].astype(F32)
        sums["gain_two"][:, sl] += fold_rows(slot_grad * white)
        sums["bias_two"][:, sl] += slot_grad[cut:]
        scaled = slot_grad * gain_two[:, sl] - mean_scaled - white * mean_white
        right_grad = scaled * inverse * t["right_slope"][:, sl].astype(F32)
        hidden_grad[:, sl] = right_grad.astype(BF16)
        b_in_sum[:, sl] += fold_rows(right_grad)


def backward_norm(values, halves, upstream, w, sums):
    white, inverse = white_of(values)
    normed_grad = None
    per_half = w["w_in"].shape[0] // 2
    for group in range(2 * per_half):
        at = group % per_half * GROUP
        part = dot_last(halves[group // per_half][:, at : at + GROUP], w["w_in"][group])
        normed_grad = part if normed_grad is None else normed_grad + part
    sums["gain_one"][...] += fold_rows(normed_grad * white)
    sums["bias_one"][...] += fold_rows(normed_grad)
    scaled = normed_grad * w["gain_one"][...]
    mean = jnp.mean(scaled, -1, keepdims=True)
    mean_white = jnp.mean(scaled * white, -1, keepdims=True)
    return upstream + inverse * (scaled - mean - white * mean_white)


def load_blocks(owner, pieces, places, sem):
    position = 0
    for piece in pieces:
        blocks = piece.shape[0]

        def start(at, carry, piece=piece, position=position):
            block = owner[position + at]
            for first, ref in places:
                if ref.shape[1] == BLOCK:
                    count = ref.shape[0] * BLOCK // ref.shape[2]
                    target = ref.at[pl.ds(block * count, count)]
                else:
                    count = ref.shape[0]
                    target = ref.at[:, pl.ds(pl.multiple_of(block * BLOCK, BLOCK), BLOCK)]
                pltpu.make_async_copy(piece.at[at, first : first + count], target, sem).start()
            return carry

        lax.fori_loop(0, blocks, start, 0)
        position += blocks
    for unused, ref in places:
        pltpu.make_async_copy(ref, ref, sem).wait()


def put_weight_grads(owner, jobs, result, stage, outs, sem):
    half = stage.shape[1]

    def send(group, rows):
        for side in range(2):
            for at in range(half):
                stage[side, at, group] = result[rows(owner[side * half + at])]
            pltpu.make_async_copy(stage.at[side, :, group], outs[side].at[:, group], sem).start()

    for left, right, place in jobs:
        if left.shape[1] > right.shape[1]:
            for start in range(0, left.shape[1], GROUP):
                stop = start + GROUP
                result[start:stop] = dot_first(left[:, start:stop], right[...]).astype(BF16)
            per = left.shape[1] // right.shape[1]
            for part in range(per):
                spot = lambda block: pl.ds(pl.multiple_of((block * per + part) * BLOCK, BLOCK), BLOCK)
                send(place + part, spot)
        else:
            for group in range(right.shape[1] // GROUP):
                columns = slice(group * GROUP, (group + 1) * GROUP)
                result[: left.shape[1]] = dot_first(left[...], right[:, columns]).astype(BF16)
                send(place + group, lambda block: pl.ds(pl.multiple_of(block * BLOCK, BLOCK), BLOCK))
    for side in range(2):
        pltpu.make_async_copy(stage.at[side], outs[side], sem).wait()


def zero(refs):
    for ref in refs:
        ref[...] = jnp.zeros_like(ref)


def whole(shape):
    return pl.BlockSpec(shape, lambda *i: (0,) * len(shape))


def image(rows, columns):
    return pl.BlockSpec((1, rows, columns), lambda i, *unused: (i, 0, 0))


def anywhere(count):
    return [pl.BlockSpec(memory_space=pl.ANY)] * count


def call(kernel, name, grid, in_specs, outs, out_specs, scratch, flops, megabytes, table=0, aliases=None):
    return pl.pallas_call(
        kernel,
        grid_spec=pltpu.PrefetchScalarGridSpec(
            num_scalar_prefetch=table,
            grid=grid,
            in_specs=in_specs,
            out_specs=out_specs,
            scratch_shapes=scratch,
        ),
        out_shape=[jax.ShapeDtypeStruct(shape, dtype) for shape, dtype in outs],
        input_output_aliases=aliases or {},
        compiler_params=pltpu.CompilerParams(vmem_limit_bytes=megabytes << 20),
        cost_estimate=pl.CostEstimate(flops=flops, bytes_accessed=20_000_000, transcendentals=0),
        name=name,
    )


def in_scratch(width, hidden):
    return pltpu.VMEM((hidden // GROUP, width, GROUP), BF16)


def out_scratch(width, hidden):
    return pltpu.VMEM((hidden // 2 // BLOCK, BLOCK, width), BF16)


def strips_of(rows, gate):
    strips = gate // STRIP
    return strips, -(-rows // strips // 8) * 8


def sum_shapes(rows, width, hidden, slots):
    strips, high = strips_of(rows, hidden // 2)
    return {
        "b_out": (8, width),
        "b_left": (8, hidden // 2),
        "b_right": (8, hidden // 2),
        "spatial": (strips * high, STRIP),
        "gain_two": (8, hidden // 2),
        "bias_two": (rows - slots // BLOCK * BLOCK, hidden // 2),
        "gain_one": (8, width),
        "bias_one": (8, width),
    }


def forward_save(values, live, mixer, slot_pad, w, owner, pieces, place, slots, first, count, into=()):
    images, rows, width = values.shape
    hidden = w["b_in"].shape[1]
    gate = hidden // 2
    outs = {name: (gate, BF16) for name in KEPT[:6]}
    outs["normed"] = (width, BF16)
    outs["inverse"] = (1, F32)
    n_w, n_p, n_o, n_i = len(WEIGHTS), len(pieces), len(outs), len(into)

    def kernel(owner_ref, values_ref, live_ref, mixer_ref, pad_ref, *refs):
        weights = dict(zip(WEIGHTS, refs[:n_w]))
        rest = refs[n_w + n_p + n_i :]
        out = dict(zip(outs, rest[:n_o]))
        right, weights["w_in"], sem = rest[n_o:]

        @pl.when(pl.program_id(0) == 0)
        def _():
            load_blocks(owner_ref, refs[n_w : n_w + n_p], [(place, weights["w_in"])], sem)

        kept = {name: ref.at[0] for name, ref in out.items()}
        kept["right"] = right
        here = values_ref[0].astype(F32)
        out["inverse"][0] = forward_image(here, live_ref[...], mixer_ref[0], pad_ref, weights, kept, slots)

    some = lambda columns: pl.BlockSpec((1, rows, columns), lambda i, *unused: (first + i, 0, 0))
    results = call(
        kernel,
        "forward_save",
        (count,),
        [some(width), whole((rows, 1)), some(rows), whole(slot_pad.shape)]
        + [whole(w[name].shape) for name in WEIGHTS]
        + anywhere(n_p + n_i),
        [((images, rows, columns), dtype) for columns, dtype in outs.values()],
        [some(columns) for columns, unused in outs.values()],
        [pltpu.VMEM((rows, gate), F32), in_scratch(width, hidden), pltpu.SemaphoreType.DMA],
        2_000_000_000 * count,
        60,
        table=1,
        aliases={5 + n_w + n_p + at: at for at in range(n_i)},
    )(owner, values, live, mixer, slot_pad, *[w[name] for name in WEIGHTS], *pieces, *into)
    return results


KEPT = ("left", "left_slope", "white", "right_slope", "slot_in", "gated", "normed", "inverse")


def forward_backward(
    values, kept_before, b_out, cotangent, valid, live, mixer, mixer_back, slot_pad, w, owner, pieces, places, slots
):
    images, rows, width = values.shape
    hidden = w["b_in"].shape[1]
    gate = hidden // 2
    groups, per, half = hidden // GROUP, gate // width, width // BLOCK // 2
    outs = {
        "values": (width, BF16),
        "upstream": (width, F32),
        "left_grad_before": (gate, BF16),
        "mixed_grad_before": (gate, BF16),
    }
    shapes = sum_shapes(rows, width, hidden, slots)
    shapes = {name: shapes[name] for name in SUMS} | {
        "b_out_before": shapes["b_out"],
        "b_left_before": shapes["b_left"],
    }
    image_scratch = {"right": F32} | dict.fromkeys(
        ("left", "left_slope", "white", "right_slope", "slot_in", "mixed_grad"), BF16
    )
    all_scratch = {
        "normed": width,
        "gated": gate,
        "hidden_grad": hidden,
        "masked": width,
        "normed_before": width,
        "gated_before": gate,
        "left_grad_before": gate,
        "masked_before": width,
    }
    reads = ("gated", "left", "left_slope", "normed")
    last_shape = (half, groups + per, BLOCK, GROUP)
    before_shape = (half, groups // 2 + per, BLOCK, GROUP)
    n_w, n_p, n_o, n_s, n_r = len(WEIGHTS), len(pieces), len(outs), len(shapes), len(reads)

    def kernel(owner_ref, values_ref, b_out_ref, cot_ref, valid_ref, live_ref, mixer_ref, back_ref, pad_ref, *refs):
        before = {name: ref.at[0] for name, ref in zip(reads, refs)}
        refs = refs[n_r:]
        weights = dict(zip(WEIGHTS, refs[:n_w]))
        rest = refs[n_w + n_p :]
        out = {name: ref.at[0] for name, ref in zip(outs, rest)}
        sums = dict(zip(shapes, rest[n_o:]))
        last_outs, before_outs = rest[n_o + n_s :][:2], rest[n_o + n_s + 2 :][:2]
        rest = rest[n_o + n_s + 4 :]
        kept = dict(zip(image_scratch, rest))
        rest = rest[len(image_scratch) :]
        every = dict(zip(all_scratch, rest))
        w_out_before, weights["w_in"], weights["w_out"], result, last_stage, before_stage, sem, out_sem = rest[len(every) :]
        step = pl.program_id(0)

        @pl.when(step == 0)
        def _():
            targets = (w_out_before, weights["w_in"], weights["w_out"])
            load_blocks(owner_ref, refs[n_w : n_w + n_p], list(zip(places, targets)), sem)
            zero(sums.values())

        mine = pl.ds(pl.multiple_of(step * rows, BLOCK), rows)
        here = {name: ref.at[mine] for name, ref in every.items()}
        kept["normed"], kept["gated"] = here["normed"], here["gated"]
        left_grad, right_grad = (here["hidden_grad"].at[:, at : at + gate] for at in (0, gate))
        here["normed_before"][...] = before["normed"][...]
        here["gated_before"][...] = before["gated"][...]
        valid_column = valid_ref[0]
        inputs = add_branch(values_ref[0].astype(F32), before["gated"][...], valid_column, w_out_before, b_out_ref.at[:1])
        inverse = forward_image(inputs, live_ref[...], mixer_ref[0], pad_ref, weights, kept, slots)
        outputs = add_branch(inputs, kept["gated"][...], valid_column, weights["w_out"], b_out_ref.at[1:])
        out["values"][...] = outputs.astype(BF16)
        upstream = cot_ref[0].astype(F32)
        sums["b_out"][...] += fold_rows(upstream)
        masked = (upstream * valid_column).astype(BF16)
        here["masked"][...] = masked
        backward_left(
            masked, weights["w_out"], kept["left"], kept["left_slope"], kept["mixed_grad"], left_grad, sums["b_left"]
        )
        backward_right(
            valid_column, back_ref[0], inverse, weights["gain_two"], kept, right_grad, sums["b_right"], sums, slots
        )
        upstream = backward_norm(inputs, (left_grad, right_grad), upstream, weights, sums)
        out["upstream"][...] = upstream
        branch_grad = upstream.astype(BF16).astype(F32)
        sums["b_out_before"][...] += fold_rows(branch_grad)
        masked = (branch_grad * valid_column).astype(BF16)
        here["masked_before"][...] = masked
        backward_left(
            masked,
            w_out_before,
            before["left"],
            before["left_slope"],
            out["mixed_grad_before"],
            here["left_grad_before"],
            sums["b_left_before"],
        )
        out["left_grad_before"][...] = here["left_grad_before"][...]

        @pl.when(step == images - 1)
        def _():
            jobs = [(every["normed"], every["hidden_grad"], 0), (every["gated"], every["masked"], groups)]
            put_weight_grads(owner_ref, jobs, result, last_stage, last_outs, out_sem.at[0])
            jobs = [
                (every["normed_before"], every["left_grad_before"], 0),
                (every["gated_before"], every["masked_before"], groups // 2),
            ]
            put_weight_grads(owner_ref, jobs, result, before_stage, before_outs, out_sem.at[1])

    results = call(
        kernel,
        "forward_backward",
        (images,),
        [image(rows, width), whole(b_out.shape), image(rows, width), image(rows, 1), whole((rows, 1))]
        + [image(rows, rows), image(rows, rows), whole(slot_pad.shape)]
        + [image(rows, kept_before[name].shape[2]) for name in reads]
        + [whole(w[name].shape) for name in WEIGHTS]
        + anywhere(n_p),
        [((images, rows, columns), dtype) for columns, dtype in outs.values()]
        + [(shape, F32) for shape in shapes.values()]
        + [(last_shape, BF16)] * 2
        + [(before_shape, BF16)] * 2,
        [image(rows, columns) for columns, unused in outs.values()]
        + [whole(shape) for shape in shapes.values()]
        + anywhere(4),
        [pltpu.VMEM((rows, gate), dtype) for dtype in image_scratch.values()]
        + [pltpu.VMEM((images * rows, columns), BF16) for columns in all_scratch.values()]
        + [out_scratch(width, hidden), in_scratch(width, hidden), out_scratch(width, hidden)]
        + [pltpu.VMEM((gate, GROUP), BF16), pltpu.VMEM((2,) + last_shape, BF16), pltpu.VMEM((2,) + before_shape, BF16)]
        + [pltpu.SemaphoreType.DMA, pltpu.SemaphoreType.DMA((2,))],
        40_000_000_000,
        60,
        table=1,
    )(
        owner,
        values,
        b_out,
        cotangent,
        valid,
        live,
        mixer,
        mixer_back,
        slot_pad,
        *[kept_before[name] for name in reads],
        *[w[name] for name in WEIGHTS],
        *pieces,
    )
    blocks = results[n_o + n_s :]
    return dict(zip(outs, results)), dict(zip(shapes, results[n_o:])), blocks[:2], blocks[2:]


def backward_slots(kept, mixed_grad, valid, mixer_back, w, owner, slots):
    images, rows, gate = mixed_grad.shape
    width = w["gain_one"].shape[1]
    half = width // BLOCK // 2
    shapes = sum_shapes(rows, width, 2 * gate, slots)
    names = ("b_right", "spatial", "gain_two", "bias_two")
    reads = ("white", "right_slope", "slot_in", "inverse", "normed")
    block_shape = (half, gate // GROUP, BLOCK, GROUP)
    n_r, n_s = len(reads), len(names)

    def kernel(owner_ref, mixed_ref, valid_ref, back_ref, gain_two, *refs):
        t = {name: ref.at[0] for name, ref in zip(reads, refs)}
        t["mixed_grad"] = mixed_ref.at[0]
        out, sums, outs = refs[n_r], dict(zip(names, refs[n_r + 1 :])), refs[n_r + 1 + n_s :][:2]
        normed, right_grad, result, stage, out_sem = refs[n_r + 3 + n_s :]
        step = pl.program_id(0)

        @pl.when(step == 0)
        def _():
            zero(sums.values())

        mine = pl.ds(pl.multiple_of(step * rows, BLOCK), rows)
        normed[mine] = t["normed"][...]
        here = right_grad.at[mine]
        backward_right(valid_ref[0], back_ref[0], t["inverse"][...], gain_two, t, here, sums["b_right"], sums, slots)
        out[0] = here[...]

        @pl.when(step == images - 1)
        def _():
            put_weight_grads(owner_ref, [(normed, right_grad, 0)], result, stage, outs, out_sem)

    results = call(
        kernel,
        "backward_slots",
        (images,),
        [image(rows, gate), image(rows, 1), image(rows, rows), whole((1, gate))]
        + [image(rows, kept[name].shape[2]) for name in reads],
        [((images, rows, gate), BF16)] + [(shapes[name], F32) for name in names] + [(block_shape, BF16)] * 2,
        [image(rows, gate)] + [whole(shapes[name]) for name in names] + anywhere(2),
        [pltpu.VMEM((images * rows, width), BF16), pltpu.VMEM((images * rows, gate), BF16)]
        + [pltpu.VMEM((width, GROUP), BF16), pltpu.VMEM((2,) + block_shape, BF16), pltpu.SemaphoreType.DMA],
        9_000_000_000,
        60,
        table=1,
    )(owner, mixed_grad, valid, mixer_back, w["gain_two"], *[kept[name] for name in reads])
    return results[0], dict(zip(names, results[1:])), results[1 + n_s :]


def backward_first(values, left_grad, right_grad, upstream, w, owner, pieces, place):
    images, rows, width = values.shape
    gate = left_grad.shape[2]
    n_p = len(pieces)

    def kernel(owner_ref, values_ref, left_ref, right_ref, up_ref, gain_ref, *refs):
        out, line, gain_sum, bias_sum, w_in, sem = refs[n_p:]
        step = pl.program_id(0)

        @pl.when(step == 0)
        def _():
            load_blocks(owner_ref, refs[:n_p], [(place, w_in)], sem)
            zero((gain_sum, bias_sum))

        weights = {"w_in": w_in, "gain_one": gain_ref}
        sums = {"gain_one": gain_sum, "bias_one": bias_sum}
        out[0] = backward_norm(values_ref[0].astype(F32), (left_ref.at[0], right_ref.at[0]), up_ref[0], weights, sums)

        @pl.when(step == images - 1)
        def _():
            line[...] = jnp.zeros_like(line)
            for at, ref in enumerate((gain_sum, bias_sum)):
                line[5:6, (1 + at) * width : (2 + at) * width] = 0.5 * jnp.sum(ref[...], 0, keepdims=True)

    return call(
        kernel,
        "backward_first",
        (images,),
        [image(rows, width), image(rows, gate), image(rows, gate), image(rows, width), whole((1, width))]
        + anywhere(n_p),
        [((images, rows, width), F32), ((8, gate), F32)],
        [image(rows, width), whole((8, gate))],
        [pltpu.VMEM((8, width), F32)] * 2 + [in_scratch(width, 2 * gate), pltpu.SemaphoreType.DMA],
        6_000_000_000,
        60,
        table=1,
    )(owner, values, left_grad, right_grad, upstream, w["gain_one"], *pieces)


def pack_sums(both, slots):
    gate = both[0]["gain_two"].shape[1]
    rows = slots // BLOCK * BLOCK + both[0]["bias_two"].shape[0]
    strips, high = strips_of(rows, gate)
    at = slots % BLOCK
    flat = [(block, name) for block in range(2) for name in SUMS if name in both[block]]

    def kernel(*refs):
        out = refs[-1]
        row = lax.broadcasted_iota(jnp.int32, (8, gate), 0)
        for block in range(2):
            sums = {name: ref for (at_block, name), ref in zip(flat, refs) if at_block == block}
            out[block, :high] = jnp.concatenate(
                [sums["spatial"][strip * high : (strip + 1) * high] for strip in range(strips)], 1
            )
            one = lambda name: jnp.sum(sums[name][...], 0, keepdims=True)
            narrow = one("b_out")
            if "gain_one" in sums:
                narrow = jnp.concatenate([narrow, 0.5 * one("gain_one"), 0.5 * one("bias_one")], 1)
            bias_two = sums["bias_two"][at : at + 1] + sums["bias_two"][at + 1 : at + 2]
            lines = [0.5 * one("b_left"), 0.5 * one("b_right"), one("gain_two"), bias_two]
            total = jnp.zeros((8, gate), F32)
            for place, line in enumerate(lines):
                total = jnp.where(row == place, line, total)
            out[block, high:] = total
            out[block, high + 4 : high + 5, : narrow.shape[1]] = narrow

    return pl.pallas_call(
        kernel,
        out_shape=jax.ShapeDtypeStruct((2, high + 8, gate), F32),
        compiler_params=pltpu.CompilerParams(vmem_limit_bytes=60 << 20),
        name="pack_sums",
    )(*[both[block][name] for block, name in flat])


def unpack_sums(odd, mine, theirs, slots, width):
    gate = mine.shape[1]
    high = mine.shape[0] - 8
    strips = gate // STRIP

    def kernel(odd_ref, mine_ref, theirs_ref, gain_one, bias_one, b_in, gain_two, bias_two, spatial, b_sp, b_out):
        is_odd = odd_ref[0] == 1
        held = mine_ref[...].astype(F32), theirs_ref[...].astype(F32)
        for block in range(2):
            value = jnp.where(is_odd, held[1 - block], held[block])
            square = [value[:high, strip * STRIP : (strip + 1) * STRIP] for strip in range(strips)]
            square = jnp.concatenate(square + [jnp.zeros((STRIP, STRIP), F32)], 0)[:STRIP]
            b_sp[block : block + 1] = square[slots : slots + 1, :slots]
            spatial[:, block, :] = square.T[:slots, :slots]
            line = lambda place: value[high + place : high + place + 1]
            b_in[block : block + 1, :gate] = line(0)
            b_in[block : block + 1, gate:] = line(1)
            gain_two[block : block + 1] = line(2)
            bias_two[block : block + 1] = line(3)
            narrow = line(4)
            if block == 0:
                narrow = narrow + (held[0][high + 5 : high + 6] + held[1][high + 5 : high + 6])
            for place, out in enumerate((b_out, gain_one, bias_one)):
                out[block : block + 1] = narrow[:, place * width : (place + 1) * width]

    shapes = [(2, width), (2, width), (2, 2 * gate), (2, gate), (2, gate), (slots, 2, slots), (2, slots), (2, width)]
    results = pl.pallas_call(
        kernel,
        in_specs=[pl.BlockSpec(memory_space=pltpu.SMEM)] + [pl.BlockSpec(memory_space=pltpu.VMEM)] * 2,
        out_shape=[jax.ShapeDtypeStruct(shape, F32) for shape in shapes],
        compiler_params=pltpu.CompilerParams(vmem_limit_bytes=60 << 20),
        name="unpack_sums",
    )(odd, mine, theirs)
    return [*results[:5], results[5].transpose(1, 0, 2), *results[6:]]


def add_blocks(chains, places, groups, per):
    counts = [len(chain) for chain in chains]
    flat = [array for chain in chains for array in chain]
    width = flat[0].shape[-1]

    def kernel(*refs):
        in_out, out_out = refs[-2:]
        start = 0
        for count, spots in zip(counts, places):
            for at, (block, group) in enumerate(spots):
                total = None
                for ref in refs[start : start + count]:
                    part = (ref[0, at] if len(ref.shape) == 4 else ref[at]).astype(F32)
                    total = part if total is None else total + part
                if group < groups:
                    in_out[block, :, group * GROUP : (group + 1) * GROUP] = total
                else:
                    first = (group - groups) * BLOCK
                    out_out[block, first : first + BLOCK] = total
            start += count

    def spec(array):
        if array.ndim == 4:
            return pl.BlockSpec((1,) + array.shape[1:], lambda i: (0, 0, 0, 0))
        return pl.BlockSpec(array.shape, lambda i: (0, 0, 0))

    shapes = [(2, BLOCK, groups * GROUP), (2, per * BLOCK, width)]
    return pl.pallas_call(
        kernel,
        grid=(1,),
        in_specs=[spec(array) for array in flat],
        out_specs=[whole(shape) for shape in shapes],
        out_shape=[jax.ShapeDtypeStruct(shape, F32) for shape in shapes],
        compiler_params=pltpu.CompilerParams(vmem_limit_bytes=60 << 20),
        name="add_blocks",
    )(*flat)


class Tree:
    def __init__(self, devices):
        self.devices = devices
        far = [1 << bit for bit in range(3, devices.bit_length() - 1)]
        self.bits = far + [2, 4], far[::-1] + [4, 2]
        self.steps = len(far) + 2

    def swap(self, values, *steps):
        bits = [sum(bits[step] for step in steps) or 1 for bits in self.bits]
        return lax.ppermute(values, AXES, [(i, i ^ bits[i % 2]) for i in range(self.devices)])

    def owners(self):
        offsets = np.zeros((2, 1 << self.steps), np.int32)
        for core in range(2):
            for step in range(self.steps):
                offsets[core] ^= (np.arange(1 << self.steps, dtype=np.int32) >> step & 1) * self.bits[core][step]
        me = lax.axis_index(AXES).astype(jnp.int32)
        odd = me % 2 == 1
        mine = me ^ jnp.where(odd, offsets[1], offsets[0])
        theirs = (me ^ 1) ^ jnp.where(odd, offsets[0], offsets[1])
        return jnp.concatenate([mine, theirs])

    def gather(self, own):
        held = pack_blocks(own, 1)
        far = self.steps - 2
        got = [
            self.swap(held, *[step for step in range(far) if index >> step & 1]) for index in range(1, 1 << far)
        ]
        wait = yield held, got
        held = jnp.concatenate(after([held, *got], wait))
        first, second = self.swap(held, far), self.swap(held, far + 1)
        wait = yield held, (first, second)
        last = self.swap(after(first, wait), far + 1)
        pieces = [held, first, second]
        others = [self.swap(piece) for piece in pieces]
        wait = yield held, last
        last = after(last, wait)
        yield [*pieces, last, *others, self.swap(last)]

    def scatter(self, mine, theirs):
        parts = [mine, self.swap(theirs)]
        wait = yield theirs, parts[1]
        for step in reversed(range(self.steps)):
            keep = 1 << step
            sent = self.add(after(parts, wait), slice(keep, 2 * keep)).astype(BF16)
            parts.append(self.swap(sent, step))
            wait = yield sent, parts[-1]
        yield parts

    def add(self, parts, at):
        total = parts[0][at].astype(F32)
        for part in parts[1:]:
            total = total + part[at].astype(F32)
        return total

    def finish(self, chains, places, groups, per):
        return add_blocks(chains, places, groups, per)

    def total(self, values):
        odd = lax.axis_index("narrow") % 2
        mine = jnp.where(odd == 1, values[1], values[0]).astype(BF16)
        theirs = jnp.where(odd == 1, values[0], values[1]).astype(BF16)
        got = self.swap(theirs)
        late = yield theirs, got
        wait = None
        for step in [*reversed(range(self.steps)), -1]:
            got = after(got, wait)
            mine = mine.astype(F32) + got.astype(F32)
            if step == self.steps - 1:
                mine = mine + jnp.pad(late, ((mine.shape[0] - late.shape[0], 0), (0, 0)))
            mine = mine.astype(BF16)
            got = self.swap(mine, *([step] if step >= 0 else []))
            wait = yield mine, got
        yield odd, mine, got


class Plain:
    def __init__(self, width, gate):
        self.width, self.gate = width, gate
        self.steps = 4
        self.blocks = width // BLOCK

    def owners(self):
        return jnp.arange(self.blocks, dtype=jnp.int32)

    def gather(self, own):
        gathered = [lax.all_gather(part, AXES, axis=0, tiled=True) for part in own]
        for unused in range(3):
            yield gathered, gathered
        yield [pack_blocks(gathered, self.blocks)]

    def scatter(self, mine, theirs):
        for unused in range(self.steps + 1):
            yield theirs, mine
        yield jnp.concatenate([mine, theirs]).astype(F32)

    def finish(self, chains, places, groups, per):
        spots = {spot: chain[:, at] for chain, place in zip(chains, places) for at, spot in enumerate(place)}
        in_grad, out_grad = [], []
        for block in range(2):
            inner = jnp.concatenate([spots[block, group] for group in range(groups)], 2)
            outer = jnp.concatenate([spots[block, groups + part] for part in range(per)], 1)
            in_grad.append(inner.reshape(self.width, -1))
            out_grad.append(outer.reshape(self.gate, -1))
        return [
            lax.psum_scatter(jnp.stack(grad), AXES, scatter_dimension=1, tiled=True) for grad in (in_grad, out_grad)
        ]

    def total(self, values):
        late = yield values, values
        late = jnp.pad(late, ((values.shape[1] - late.shape[0], 0), (0, 0)))
        values = lax.psum(jnp.stack([values[0] + late, values[1]]), AXES)
        for unused in range(self.steps + 1):
            yield values, values
        yield jnp.int32(0), values[0], values[1]


def pack_blocks(parts, blocks):
    packed = []
    for part in parts:
        if part.shape[1] > GROUP:
            packed.append(part.reshape(blocks, BLOCK, -1, GROUP).transpose(0, 2, 1, 3))
        else:
            packed.append(part.reshape(blocks, -1, BLOCK, GROUP))
    return jnp.concatenate(packed, 1)


def after(values, *others):
    return lax.optimization_barrier((values, others))[0] if others != (None,) else values


def bfloat_pair(values):
    top = lax.reduce_precision(values, 8, 7)
    return top.astype(BF16), lax.reduce_precision(values - top, 8, 7).astype(BF16)


def spatial_operands(valid, w_sp, b_sp, gain_two, bias_two, rows):
    images, slots = valid.shape
    gate = gain_two.shape[0]
    cut = slots // BLOCK * BLOCK
    spare = rows - slots
    masked = w_sp[None] * valid[:, None, :].astype(BF16)
    bias = jnp.broadcast_to(jnp.stack(bfloat_pair(b_sp), -1)[None], (images, slots, 2))
    mixer = jnp.concatenate([masked, bias], 2)
    mixer = jnp.pad(mixer, ((0, 0), (0, spare), (0, spare - 2)))
    column_sum = jnp.einsum("ir,pr->ip", valid.astype(BF16), w_sp, preferred_element_type=F32)
    back = jnp.concatenate([jnp.swapaxes(masked, 1, 2), jnp.stack(bfloat_pair(column_sum), 1)], 1)
    back = jnp.pad(back, ((0, 0), (0, spare - 2), (0, spare)))
    one = jnp.ones((gate,), BF16)
    pad = jnp.stack([one, one, *bfloat_pair(bias_two), *bfloat_pair(gain_two)])
    pad = jnp.pad(pad, ((slots - cut, rows - slots - 6), (0, 0))).astype(F32)
    return mixer, back, pad


def shards(
    tokens,
    mask,
    ln1_gain,
    ln1_bias,
    in_weight,
    in_bias,
    ln2_gain,
    ln2_bias,
    spatial_weight,
    spatial_bias,
    out_weight,
    out_bias,
    cotangent,
):
    devices = lax.axis_size(AXES)
    images, slots = mask.shape
    width = tokens.shape[1]
    hidden = in_weight.shape[2]
    gate = hidden // 2
    per = gate // width
    groups = hidden // GROUP
    rows = -(-(slots + 6) // BLOCK) * BLOCK
    spare = rows - slots
    pairwise = devices * BLOCK == width and devices >= 16 and devices & (devices - 1) == 0
    links = Tree(devices) if pairwise else Plain(width, gate)

    owner = links.owners()
    gather_one = links.gather([in_weight[0]])
    unused, got = next(gather_one)
    gather_rest = links.gather(after([out_weight[0], in_weight[1], out_weight[1]], got))
    unused, got = next(gather_rest)
    next(gather_one)
    gather_one.send(got)
    pieces_one = gather_one.send(None)
    column_rest, got_rest = gather_rest.send(None)

    valid = mask.astype(F32)
    padded = lambda array: jnp.pad(array.reshape(images, slots, width), ((0, 0), (0, spare), (0, 0)))
    valid_column = jnp.pad(valid, ((0, 0), (0, spare)))[:, :, None]
    live = (jnp.arange(rows) < slots).astype(F32)[:, None]
    values = padded(tokens)
    layers, spatial = [], []
    for layer in range(2):
        layers.append(
            {
                "b_in": 0.5 * in_bias[layer][None],
                "gain_one": 0.5 * ln1_gain[layer][None],
                "bias_one": 0.5 * ln1_bias[layer][None],
                "gain_two": ln2_gain[layer][None],
                "bias_two": ln2_bias[layer][None],
                "b_out": out_bias[layer][None],
            }
        )
        spatial.append(
            spatial_operands(
                valid, spatial_weight[layer], spatial_bias[layer], ln2_gain[layer], ln2_bias[layer], rows
            )
        )
    cot = padded(cotangent)
    mixer, back, pad = zip(*spatial)

    halfway = images * 2 // 5
    save = lambda array, start, count, into: forward_save(
        array, live, mixer[0], pad[0], layers[0], owner, pieces_one, 0, slots, start, count, into
    )
    kept = save(after(values, column_rest), 0, halfway, ())
    gather_rest.send(kept[0])
    ahead = got_rest[0], valid_column, cot, mixer[1], back, pad[1]
    kept = save(after(values, ahead), halfway, images - halfway, kept)
    pieces_rest = gather_rest.send(kept[0])
    kept = dict(zip(KEPT, kept))
    last, last_sums, last_blocks, before_blocks = forward_backward(
        values,
        kept,
        out_bias,
        cot,
        valid_column,
        live,
        mixer[1],
        back[1],
        pad[1],
        layers[1],
        owner,
        pieces_rest,
        (0, per, per + groups),
        slots,
    )

    one = links.scatter(*last_blocks)
    sent, got_one = next(one)
    left = links.scatter(before_blocks[0], after(before_blocks[1], sent))
    sent, got_left = next(left)
    sent, got_one = one.send(sent)
    right_grad, sums, blocks = backward_slots(
        kept, after(last["mixed_grad_before"], sent), valid_column, back[0], layers[0], owner, slots
    )
    sums["b_out"], sums["b_left"] = last_sums["b_out_before"], last_sums["b_left_before"]
    right = links.scatter(*after(blocks, got_one, got_left))
    sent, got_right = next(right)
    sent, got_left = left.send(sent)
    sent, got_one = one.send(sent)
    small = links.total(pack_sums((sums, last_sums), slots))
    sent_small, got_small = next(small)
    input_grad, late = after(
        backward_first(
            values,
            last["left_grad_before"],
            right_grad,
            after(last["upstream"], sent, sent_small),
            layers[0],
            owner,
            pieces_one,
            0,
        ),
        got_right,
        got_left,
        got_one,
        got_small,
    )
    sent = input_grad
    for turn in range(links.steps):
        for chain, turns in ((right, 0), (left, 1), (one, 2)):
            if turn + turns < links.steps:
                sent, unused = chain.send(sent)
        unused, sent_small = small.send(late if turn == 0 else sent)
    small.send(None)
    small_sent = small.send(None)
    chains = [next(chain) for chain in (one, left, right)]
    odd, *summed = small_sent
    steps = groups // 2
    places = (
        [(1, group) for group in range(groups + per)],
        [(0, group) for group in range(steps)] + [(0, groups + part) for part in range(per)],
        [(0, steps + group) for group in range(steps)],
    )
    in_grad, out_grad = links.finish(chains, places, groups, per)
    gain_one, bias_one, b_in, gain_two, bias_two, spatial_grad, b_sp, b_out = unpack_sums(
        odd.reshape(1), *summed, slots, width
    )

    unpadded = lambda array: array[:, :slots].reshape(images * slots, width)
    return (
        unpadded(last["values"]),
        unpadded(input_grad),
        gain_one,
        bias_one,
        in_grad,
        b_in,
        gain_two,
        bias_two,
        spatial_grad,
        b_sp,
        out_grad,
        b_out,
    )


def solution(mesh):
    both = P(AXES, None)
    second = P(None, AXES, None)
    in_specs = (both, both, P(), P(), second, P(), P(), P(), P(), P(), second, P(), both)
    out_specs = (both, both, P(), P(), second, P(), P(), P(), P(), P(), second, P())
    return jax.shard_map(shards, mesh=mesh, in_specs=in_specs, out_specs=out_specs, check_vma=False)
```

time: 284 us -> 237 us (0.83)
  waiting for transfers between devices: 62.6 us -> 37.6 us
  starting transfers between devices: 56.3 us -> 44.9 us
  local copies, waits for them, and re-layouts: 21.5 us -> 14.6 us
  Pallas kernels: 111 us -> 106 us
    ppermute x50 -> x41, waiting for transfers between devices: 62.6 us -> 37.6 us  [swap(): lax.ppermute(values, AXES, [(i, i ^ bits[i % 2]) for i in range(self.devi...]
    convert_element_type x3 -> x18, other arithmetic: 0.48 us -> 20.6 us  [the longest x12 20.4 us: scatter(): sent = self.add(after(parts, wait), slice(keep, 2 * keep)).astype(BF16)]
    ppermute x50 -> x41, starting transfers between devices: 56.3 us -> 44.9 us  [swap(): lax.ppermute(values, AXES, [(i, i ^ bits[i % 2]) for i in range(self.devi...]
    add x20 -> x0, other arithmetic: 9.33 us -> none  [the longest x3 6.51 us: scatter(): total = mine.astype(F32) + self.swap(theirs, 1).astype(F32)]
    another operation x16 -> x0, other arithmetic: 7.79 us -> none  [the longest x8 4.28 us: shards(): small = [jnp.stack(pair) for pair in zip(small_zero, small_one)]]
    pallas_call x7, Pallas kernels: 98.7 us -> 94.2 us  [the longest x1 50 us: forward_backward(): call(kernel, 'forward_backward', (images,), [image(rows, width), whole(b_...]
    slice x22 -> x1, local copies, waits for them, and re-layouts: 4 us -> 0.95 us  [shards(): gather_one = links.gather([in_weight[0]])]
  transfers between devices with their start and end apart: 50 -> 41, of which waited for: 15 -> 13; matrix products, arithmetic and copies ran while one was open for 15% -> 17% of each run, Pallas kernels for 19% -> 23%
where the time goes in v2:
time: 237 us; the launch traced here: 235 us
  Pallas kernels  106 us (45%)
  starting transfers between devices  44.9 us (19%)
  waiting for transfers between devices  37.6 us (16%)
  other arithmetic  30.3 us (13%)
  local copies, waits for them, and re-layouts  14.6 us (6%)
    pallas_call x1, Pallas kernels, forward_backward(): call(kernel, 'forward_backward', (images,), [image(rows, width), whole(b_...  50 us
    ppermute x41, starting transfers between devices, swap(): lax.ppermute(values, AXES, [(i, i ^ bits[i % 2]) for i in range(self.devi...  44.9 us
    ppermute x41, waiting for transfers between devices, swap(): lax.ppermute(values, AXES, [(i, i ^ bits[i % 2]) for i in range(self.devi...  37.6 us
    pallas_call x2, Pallas kernels, forward_save(): call(kernel, 'forward_save', (count,), [some(width), whole((rows, 1)), so...  23.1 us
    convert_element_type x12, other arithmetic, scatter(): sent = self.add(after(parts, wait), slice(keep, 2 * keep)).astype(BF16)  20.4 us
    pallas_call x1, Pallas kernels, backward_slots(): call(kernel, 'backward_slots', (images,), [image(rows, gate), image(rows,...  14.6 us
    pallas_call x1, Pallas kernels, backward_first(): call(kernel, 'backward_first', (images,), [image(rows, width), image(rows...  11.9 us
  transfers between devices with their start and end apart: 41, of which 13 were waited for; matrix products, arithmetic and copies ran while one was open for 17% of the time, Pallas kernels for 23%

profile of v2, /device:TPU:0, one launch (start us, length us, event | category | flops | bytes accessed | tf_op | source)
XLA Modules:
  0.0 235.1 jit_solution(4044379792966036338)
XLA Ops:
  1.7 3.1 %collective-permute-start = (bf16[1,6,16,512]{3,2,1,0:T(8,128)(2,1)S(1)}, bf16[1,6,16,512]{3,2,1,0:T(8,128)(2,1)S(1)}, u32[]{:S(2)}, u32[]{:S(2)}) collective-permute-start(bf16[1,6,16,512]{3,2,1,0:T(8,128)(2,1)S(1)} %bitcast.65), channel_id=1, source_target_pairs={{0,8},{1,17},{2,10},{3,19},{4,12},{5,21},{6,14},{7,23},{8,0},{9,25... | collective-permute-start | bytes 294920 | tf_op jit(solution)/shard_map/ppermute | solution.py:678
  4.8 2.6 %collective-permute-start.1 = (bf16[1,6,16,512]{3,2,1,0:T(8,128)(2,1)S(1)}, bf16[1,6,16,512]{3,2,1,0:T(8,128)(2,1)S(1)}, u32[]{:S(2)}, u32[]{:S(2)}) collective-permute-start(bf16[1,6,16,512]{3,2,1,0:T(8,128)(2,1)S(1)} %bitcast.66), channel_id=1, source_target_pairs={{0,16},{1,9},{2,18},{3,11},{4,20},{5,13},{6,22},{7,15},{8,24},{9,1... | collective-permute-start | bytes 294920 | tf_op jit(solution)/shard_map/ppermute | solution.py:678
  7.4 1.4 fusion.55
  14.5 1.6 collective-permute-start.7
  16.4 1.7 collective-permute-start.3
  18.1 2.4 %collective-permute-start.4 = (bf16[1,12,16,512]{3,2,1,0:T(8,128)(2,1)S(1)}, bf16[1,12,16,512]{3,2,1,0:T(8,128)(2,1)S(1)}, u32[]{:S(2)}, u32[]{:S(2)}) collective-permute-start(bf16[1,12,16,512]{3,2,1,0:T(8,128)(2,1)S(1)} %pad_maximum_fusion.2), channel_id=1, source_target_pairs={{0,16},{1,9},{2,18},{3,11},{4,20},{5,13},{6,22},{7,15},{8,24},{9,1... | collective-permute-start | bytes 589832 | tf_op jit(solution)/shard_map/ppermute | solution.py:678
  21.1 1.6 collective-permute-start.8
  22.7 6.0 %collective-permute-done.3 = bf16[1,12,16,512]{3,2,1,0:T(8,128)(2,1)S(1)} collective-permute-done((bf16[1,12,16,512]{3,2,1,0:T(8,128)(2,1)S(1)}, bf16[1,12,16,512]{3,2,1,0:T(8,128)(2,1)S(1)}, u32[]{:S(2)}, u32[]{:S(2)}) %collective-permute-start.3) | collective-permute-done | bytes 196640 | tf_op jit(solution)/shard_map/ppermute | solution.py:678
  28.6 4.6 %collective-permute-done.4 = bf16[1,12,16,512]{3,2,1,0:T(8,128)(2,1)S(1)} collective-permute-done((bf16[1,12,16,512]{3,2,1,0:T(8,128)(2,1)S(1)}, bf16[1,12,16,512]{3,2,1,0:T(8,128)(2,1)S(1)}, u32[]{:S(2)}, u32[]{:S(2)}) %collective-permute-start.4) | collective-permute-done | bytes 196640 | tf_op jit(solution)/shard_map/ppermute | solution.py:678
  33.2 1.5 collective-permute-start.9
  38.5 3.0 %collective-permute-done.9.refs_8_.refs_3_ = bf16[4,6,16,512]{3,2,1,0:T(8,128)(2,1)} collective-permute-done((bf16[4,6,16,512]{3,2,1,0:T(8,128)(2,1)S(1)}, bf16[4,6,16,512]{3,2,1,0:T(8,128)(2,1)}, u32[]{:S(2)}, u32[]{:S(2)}) %collective-permute-start.9) | collective-permute-done | bytes 393248 | tf_op jit(solution)/shard_map/ppermute | solution.py:678
  42.2 1.4 reshape.135
  46.8 2.4 %collective-permute-start.14 = (bf16[4,12,16,512]{3,2,1,0:T(8,128)(2,1)}, bf16[4,12,16,512]{3,2,1,0:T(8,128)(2,1)S(1)}, u32[]{:S(2)}, u32[]{:S(2)}) collective-permute-start(bf16[4,12,16,512]{3,2,1,0:T(8,128)(2,1)} %pad_maximum_fusion.refs_9_), channel_id=1, source_target_pairs={{0,4},{1,3},{2,6},{3,1},{4,0},{5,7},{6,2},{7,5},{8,12},{9,11},{10,... | collective-permute-start | bytes 2359304 | tf_op jit(solution)/shard_map/ppermute | solution.py:678
  49.8 10.3 %forward_save.2 = (bf16[5,208,1536]{2,1,0:T(8,128)(2,1)}, bf16[5,208,1536]{2,1,0:T(8,128)(2,1)}, bf16[5,208,1536]{2,1,0:T(8,128)(2,1)}, bf16[5,208,1536]{2,1,0:T...) custom-call(s32[32]{0:T(128)} %pad_add_fusion.owner_ref, ...), custom_call_target="tpu_custom_call" | custom-call | flops 4000000000 | bytes 20000000 | tf_op jit(solution)/shard_map/forward_save/pallas_call | solution.py:305
  61.4 12.8 %forward_save.3 = (bf16[5,208,1536]{2,1,0:T(8,128)(2,1)}, bf16[5,208,1536]{2,1,0:T(8,128)(2,1)}, bf16[5,208,1536]{2,1,0:T(8,128)(2,1)}, bf16[5,208,1536]{2,1,0:T...) custom-call(s32[32]{0:T(128)} %pad_add_fusion.owner_ref, ...), custom_call_target="tpu_custom_call", output_to_operand_aliasing={{0}: (18, {}), {1}: (19, {}), {2}: (20, {}), {3}: (21, {}),... | custom-call | flops 6000000000 | bytes 20000000 | tf_op jit(solution)/shard_map/forward_save/pallas_call | solution.py:305
  76.9 50.0 %forward_backward.1 = (bf16[5,208,512]{2,1,0:T(8,128)(2,1)}, f32[5,208,512]{2,1,0:T(8,128)}, bf16[5,208,1536]{2,1,0:T(8,128)(2,1)}, bf16[5,208,1536]{2,1,0:T(8,1...) custom-call(s32[32]{0:T(128)} %pad_add_fusion.owner_ref, ...), custom_call_target="tpu_custom_call" | custom-call | flops 40000000000 | bytes 20000000 | tf_op jit(solution)/shard_map/forward_backward/pallas_call | solution.py:431
  127.4 5.9 %collective-permute-done.20.refs_1_ = bf16[16,9,16,512]{3,2,1,0:T(8,128)(2,1)S(1)} collective-permute-done((bf16[16,9,16,512]{3,2,1,0:T(8,128)(2,1)}, bf16[16,9,16,512]{3,2,1,0:T(8,128)(2,1)S(1)}, u32[]{:S(2)}, u32[]{:S(2)}) %collective-permute-start.20) | collective-permute-done | bytes 2359328 | tf_op jit(solution)/shard_map/ppermute | solution.py:678
  133.3 3.7 %add_convert_fusion = bf16[8,9,16,512]{3,2,1,0:T(8,128)(2,1)} fusion(bf16[16,9,16,512]{3,2,1,0:T(8,128)(2,1)S(1)} %collective-permute-done.20.refs_1_, bf16[16,9,16,512]{3,2,1,0:T(8,128)(2,1)} %get-tuple-element.206.refs_0_), kind=kLoop, calls=%fused_computation | loop fusion | flops 2359296 | bytes 3538944 | tf_op jit(solution)/shard_map/convert_element_type | solution.py:713
  137.0 2.0 collective-permute-start.21
  139.0 14.6 %backward_slots.1 = (bf16[5,208,1536]{2,1,0:T(8,128)(2,1)}, f32[8,1536]{1,0:T(8,128)}, f32[240,256]{1,0:T(8,128)}, f32[8,1536]{1,0:T(8,128)}, f32[16,1536]{1,0:T...) custom-call(s32[32]{0:T(128)} %pad_add_fusion.owner_ref, ...), custom_call_target="tpu_custom_call" | custom-call | flops 8999999488 | bytes 20000000 | tf_op jit(solution)/shard_map/backward_slots/pallas_call | solution.py:504
  153.6 2.2 pack_sums.1
  155.9 2.9 %add_convert_fusion.1 = bf16[8,6,16,512]{3,2,1,0:T(8,128)(2,1)} fusion(bf16[16,6,16,512]{3,2,1,0:T(8,128)(2,1)} %collective-permute-done.22.refs_7_, bf16[16,6,16,512]{3,2,1,0:T(8,128)(2,1)} %get-tuple-element.216.refs_6_), kind=kLoop, calls=%fused_computation.1 | loop fusion | flops 1572864 | bytes 2359296 | tf_op jit(solution)/shard_map/convert_element_type | solution.py:713
  159.0 2.2 add_convert_fusion.2
  161.2 1.5 collective-permute-start.25
  162.8 11.9 %backward_first.1 = (f32[5,208,512]{2,1,0:T(8,128)}, f32[8,1536]{1,0:T(8,128)}) custom-call(s32[32]{0:T(128)} %pad_add_fusion.owner_ref, bf16[5,208,512]{2,1,0:T(8,128)(2,1)} %pad.36.values_ref, bf16[5,208,1536]{2,1,0:T(8,128)(2,1)} %get-tuple-element.146.left_ref, bf16[5,208,1536]{2,1,0:T(8,128)(2,1)} %get-tuple-element.159.right_ref, ...), custom_call_target="tpu_custom_call" | custom-call | flops 6000000000 | bytes 20000000 | tf_op jit(solution)/shard_map/backward_first/pallas_call | solution.py:545
  174.8 1.8 collective-permute-done.25.refs_3_
  177.4 1.2 add_convert_fusion.4
  178.8 1.5 add_convert_fusion.3
  180.3 1.8 collective-permute-start.29
  182.0 1.2 add_convert_fusion.5
  183.3 5.3 %collective-permute-start.28 = (bf16[2,9,16,512]{3,2,1,0:T(8,128)(2,1)S(1)}, bf16[2,9,16,512]{3,2,1,0:T(8,128)(2,1)S(1)}, u32[]{:S(2)}, u32[]{:S(2)}) collective-permute-start(bf16[2,9,16,512]{3,2,1,0:T(8,128)(2,1)S(1)} %add_convert_fusion.5), channel_id=1, source_target_pairs={{0,16},{1,9},{2,18},{3,11},{4,20},{5,13},{6,22},{7,15},{8,24},{9,1... | collective-permute-start | bytes 884744 | tf_op jit(solution)/shard_map/ppermute | solution.py:678
  188.7 1.5 collective-permute-done.30.refs_14_
  190.2 1.3 add_convert_fusion.7
  191.8 1.4 add_convert_fusion.6
  193.1 4.5 %collective-permute-start.32 = (bf16[2,6,16,512]{3,2,1,0:T(8,128)(2,1)S(1)}, bf16[2,6,16,512]{3,2,1,0:T(8,128)(2,1)S(1)}, u32[]{:S(2)}, u32[]{:S(2)}) collective-permute-start(bf16[2,6,16,512]{3,2,1,0:T(8,128)(2,1)S(1)} %add_convert_fusion.6), channel_id=1, source_target_pairs={{0,16},{1,9},{2,18},{3,11},{4,20},{5,13},{6,22},{7,15},{8,24},{9,1... | collective-permute-start | bytes 589832 | tf_op jit(solution)/shard_map/ppermute | solution.py:678
  197.7 1.9 add_convert_fusion.12
  199.6 2.1 collective-permute-start.31
  203.0 1.2 add_convert_fusion.13
  204.8 2.2 collective-permute-start.34
  207.0 1.3 collective-permute-done.35.refs_16_
  209.2 7.6 %collective-permute-done.34 = bf16[48,1536]{1,0:T(8,128)(2,1)S(1)} collective-permute-done((bf16[48,1536]{1,0:T(8,128)(2,1)S(1)}, bf16[48,1536]{1,0:T(8,128)(2,1)S(1)}, u32[]{:S(2)}, u32[]{:S(2)}) %collective-permute-start.34) | collective-permute-done | bytes 147488 | tf_op jit(solution)/shard_map/ppermute | solution.py:678
  216.9 2.0 collective-permute-start.38
  218.9 3.1 %collective-permute-done.36 = bf16[48,1536]{1,0:T(8,128)(2,1)S(1)} collective-permute-done((bf16[48,1536]{1,0:T(8,128)(2,1)S(1)}, bf16[48,1536]{1,0:T(8,128)(2,1)S(1)}, u32[]{:S(2)}, u32[]{:S(2)}) %collective-permute-start.36) | collective-permute-done | bytes 147488 | tf_op jit(solution)/shard_map/ppermute | solution.py:678
  222.3 2.0 collective-permute-start.40
  225.5 1.7 slice.226
  227.2 1.5 reshape.140
  230.0 2.4 %add_blocks.1 = (f32[2,16,3072]{2,1,0:T(8,128)}, f32[2,48,512]{2,1,0:T(8,128)}) custom-call(bf16[16,9,16,512]{3,2,1,0:T(8,128)(2,1)} %get-tuple-element.206.refs_0_, bf16[16,9,16,512]{3,2,1,0:T(8,128)(2,1)} %copy-done, bf16[8,9,16,512]{3,2,1,0:T(8,128)(2,1)} %copy-done.1, bf16[4,9,16,512]{3,2,1,0:T(8,128)(2,1)} %collective-permute-done.25.refs_3_, ...), custom_call_target="tpu_custom_call" | custom-call | tf_op jit(solution)/shard_map/add_blocks/pallas_call | solution.py:658
  233.1 2.0 unpack_sums.1
  (179 shorter events, 28.5 us)
Async XLA Ops:
  1.7 12.3 %collective-permute-start = (bf16[1,6,16,512]{3,2,1,0:T(8,128)(2,1)S(1)}, bf16[1,6,16,512]{3,2,1,0:T(8,128)(2,1)S(1)}, u32[]{:S(2)}, u32[]{:S(2)}) collective-permute-start(bf16[1,6,16,512]{3,2,1,0:T(8,128)(2,1)S(1)} %bitcast.65), channel_id=1, source_target_pairs={{0,8},{1,17},{2,10},{3,19},{4,12},{5,21},{6,14},{7,23},{8,0},{9,25... | collective-permute-start | bytes 294920 | tf_op jit(solution)/shard_map/ppermute | solution.py:678
  4.8 9.6 %collective-permute-start.1 = (bf16[1,6,16,512]{3,2,1,0:T(8,128)(2,1)S(1)}, bf16[1,6,16,512]{3,2,1,0:T(8,128)(2,1)S(1)}, u32[]{:S(2)}, u32[]{:S(2)}) collective-permute-start(bf16[1,6,16,512]{3,2,1,0:T(8,128)(2,1)S(1)} %bitcast.66), channel_id=1, source_target_pairs={{0,16},{1,9},{2,18},{3,11},{4,20},{5,13},{6,22},{7,15},{8,24},{9,1... | collective-permute-start | bytes 294920 | tf_op jit(solution)/shard_map/ppermute | solution.py:678
  7.4 7.0 %collective-permute-start.2 = (bf16[1,6,16,512]{3,2,1,0:T(8,128)(2,1)S(1)}, bf16[1,6,16,512]{3,2,1,0:T(8,128)(2,1)S(1)}, u32[]{:S(2)}, u32[]{:S(2)}) collective-permute-start(bf16[1,6,16,512]{3,2,1,0:T(8,128)(2,1)S(1)} %bitcast.67), channel_id=1, source_target_pairs={{0,24},{1,25},{2,26},{3,27},{4,28},{5,29},{6,30},{7,31},{8,16},{9,... | collective-permute-start | bytes 294920 | tf_op jit(solution)/shard_map/ppermute | solution.py:678
  14.4 22.9 %copy-start.4 = (bf16[4,6,16,512]{3,2,1,0:T(8,128)(2,1)}, bf16[4,6,16,512]{3,2,1,0:T(8,128)(2,1)S(1)}, u32[]{:S(2)}) copy-start(bf16[4,6,16,512]{3,2,1,0:T(8,128)(2,1)S(1)} %pad_maximum_fusion.1.refs_5_.refs_0_) | copy-start | bytes 1179652
  14.5 18.7 %collective-permute-start.7 = (bf16[4,6,16,512]{3,2,1,0:T(8,128)(2,1)S(1)}, bf16[4,6,16,512]{3,2,1,0:T(8,128)(2,1)S(1)}, u32[]{:S(2)}, u32[]{:S(2)}) collective-permute-start(bf16[4,6,16,512]{3,2,1,0:T(8,128)(2,1)S(1)} %pad_maximum_fusion.1.refs_5_.refs_0_), channel_id=1, source_target_pairs={{0,2},{1,5},{2,0},{3,7},{4,6},{5,1},{6,4},{7,3},{8,10},{9,13},{10,... | collective-permute-start | bytes 1179656 | tf_op jit(solution)/shard_map/ppermute | solution.py:678
  16.4 12.2 %collective-permute-start.3 = (bf16[1,12,16,512]{3,2,1,0:T(8,128)(2,1)S(1)}, bf16[1,12,16,512]{3,2,1,0:T(8,128)(2,1)S(1)}, u32[]{:S(2)}, u32[]{:S(2)}) collective-permute-start(bf16[1,12,16,512]{3,2,1,0:T(8,128)(2,1)S(1)} %pad_maximum_fusion.2), channel_id=1, source_target_pairs={{0,8},{1,17},{2,10},{3,19},{4,12},{5,21},{6,14},{7,23},{8,0},{9,25... | collective-permute-start | bytes 589832 | tf_op jit(solution)/shard_map/ppermute | solution.py:678
  18.1 15.1 %collective-permute-start.4 = (bf16[1,12,16,512]{3,2,1,0:T(8,128)(2,1)S(1)}, bf16[1,12,16,512]{3,2,1,0:T(8,128)(2,1)S(1)}, u32[]{:S(2)}, u32[]{:S(2)}) collective-permute-start(bf16[1,12,16,512]{3,2,1,0:T(8,128)(2,1)S(1)} %pad_maximum_fusion.2), channel_id=1, source_target_pairs={{0,16},{1,9},{2,18},{3,11},{4,20},{5,13},{6,22},{7,15},{8,24},{9,1... | collective-permute-start | bytes 589832 | tf_op jit(solution)/shard_map/ppermute | solution.py:678
  20.5 12.7 %collective-permute-start.5 = (bf16[1,12,16,512]{3,2,1,0:T(8,128)(2,1)S(1)}, bf16[1,12,16,512]{3,2,1,0:T(8,128)(2,1)S(1)}, u32[]{:S(2)}, u32[]{:S(2)}) collective-permute-start(bf16[1,12,16,512]{3,2,1,0:T(8,128)(2,1)S(1)} %pad_maximum_fusion.2), channel_id=1, source_target_pairs={{0,24},{1,25},{2,26},{3,27},{4,28},{5,29},{6,30},{7,31},{8,16},{9,... | collective-permute-start | bytes 589832 | tf_op jit(solution)/shard_map/ppermute | solution.py:678
  21.1 17.1 %collective-permute-start.8 = (bf16[4,6,16,512]{3,2,1,0:T(8,128)(2,1)S(1)}, bf16[4,6,16,512]{3,2,1,0:T(8,128)(2,1)}, u32[]{:S(2)}, u32[]{:S(2)}) collective-permute-start(bf16[4,6,16,512]{3,2,1,0:T(8,128)(2,1)S(1)} %pad_maximum_fusion.1.refs_5_.refs_0_), channel_id=1, source_target_pairs={{0,4},{1,3},{2,6},{3,1},{4,0},{5,7},{6,2},{7,5},{8,12},{9,11},{10,... | collective-permute-start | bytes 1179656 | tf_op jit(solution)/shard_map/ppermute | solution.py:678
  33.2 8.2 %collective-permute-start.9 = (bf16[4,6,16,512]{3,2,1,0:T(8,128)(2,1)S(1)}, bf16[4,6,16,512]{3,2,1,0:T(8,128)(2,1)}, u32[]{:S(2)}, u32[]{:S(2)}) collective-permute-start(bf16[4,6,16,512]{3,2,1,0:T(8,128)(2,1)S(1)} %collective-permute-done.7.refs_6_.refs_1_), channel_id=1, source_target_pairs={{0,4},{1,3},{2,6},{3,1},{4,0},{5,7},{6,2},{7,5},{8,12},{9,11},{10,... | collective-permute-start | bytes 1179656 | tf_op jit(solution)/shard_map/ppermute | solution.py:678
  36.4 10.4 %collective-permute-start.10 = (bf16[4,6,16,512]{3,2,1,0:T(8,128)(2,1)S(1)}, bf16[4,6,16,512]{3,2,1,0:T(8,128)(2,1)}, u32[]{:S(2)}, u32[]{:S(2)}) collective-permute-start(bf16[4,6,16,512]{3,2,1,0:T(8,128)(2,1)S(1)} %pad_maximum_fusion.1.refs_5_.refs_0_), channel_id=1, source_target_pairs={{0,1},{1,0},{2,3},{3,2},{4,5},{5,4},{6,7},{7,6},{8,9},{9,8},{10,11... | collective-permute-start | bytes 1179656 | tf_op jit(solution)/shard_map/ppermute | solution.py:678
  37.4 22.7 %collective-permute-start.6 = (bf16[4,12,16,512]{3,2,1,0:T(8,128)(2,1)}, bf16[4,12,16,512]{3,2,1,0:T(8,128)(2,1)}, u32[]{:S(2)}, u32[]{:S(2)}) collective-permute-start(bf16[4,12,16,512]{3,2,1,0:T(8,128)(2,1)} %pad_maximum_fusion.refs_9_), channel_id=1, source_target_pairs={{0,2},{1,5},{2,0},{3,7},{4,6},{5,1},{6,4},{7,3},{8,10},{9,13},{10,... | collective-permute-start | bytes 2359304 | tf_op jit(solution)/shard_map/ppermute | solution.py:678
  38.0 11.8 %collective-permute-start.11 = (bf16[4,6,16,512]{3,2,1,0:T(8,128)(2,1)S(1)}, bf16[4,6,16,512]{3,2,1,0:T(8,128)(2,1)}, u32[]{:S(2)}, u32[]{:S(2)}) collective-permute-start(bf16[4,6,16,512]{3,2,1,0:T(8,128)(2,1)S(1)} %collective-permute-done.7.refs_6_.refs_1_), channel_id=1, source_target_pairs={{0,1},{1,0},{2,3},{3,2},{4,5},{5,4},{6,7},{7,6},{8,9},{9,8},{10,11... | collective-permute-start | bytes 1179656 | tf_op jit(solution)/shard_map/ppermute | solution.py:678
  38.2 11.6 %collective-permute-start.12 = (bf16[4,6,16,512]{3,2,1,0:T(8,128)(2,1)}, bf16[4,6,16,512]{3,2,1,0:T(8,128)(2,1)}, u32[]{:S(2)}, u32[]{:S(2)}) collective-permute-start(bf16[4,6,16,512]{3,2,1,0:T(8,128)(2,1)} %collective-permute-done.8.refs_7_.refs_2_), channel_id=1, source_target_pairs={{0,1},{1,0},{2,3},{3,2},{4,5},{5,4},{6,7},{7,6},{8,9},{9,8},{10,11... | collective-permute-start | bytes 1179656 | tf_op jit(solution)/shard_map/ppermute | solution.py:678
  41.4 8.3 %collective-permute-start.13 = (bf16[4,6,16,512]{3,2,1,0:T(8,128)(2,1)}, bf16[4,6,16,512]{3,2,1,0:T(8,128)(2,1)}, u32[]{:S(2)}, u32[]{:S(2)}) collective-permute-start(bf16[4,6,16,512]{3,2,1,0:T(8,128)(2,1)} %collective-permute-done.9.refs_8_.refs_3_), channel_id=1, source_target_pairs={{0,1},{1,0},{2,3},{3,2},{4,5},{5,4},{6,7},{7,6},{8,9},{9,8},{10,11... | collective-permute-start | bytes 1179656 | tf_op jit(solution)/shard_map/ppermute | solution.py:678
  46.8 14.6 %collective-permute-start.14 = (bf16[4,12,16,512]{3,2,1,0:T(8,128)(2,1)}, bf16[4,12,16,512]{3,2,1,0:T(8,128)(2,1)S(1)}, u32[]{:S(2)}, u32[]{:S(2)}) collective-permute-start(bf16[4,12,16,512]{3,2,1,0:T(8,128)(2,1)} %pad_maximum_fusion.refs_9_), channel_id=1, source_target_pairs={{0,4},{1,3},{2,6},{3,1},{4,0},{5,7},{6,2},{7,5},{8,12},{9,11},{10,... | collective-permute-start | bytes 2359304 | tf_op jit(solution)/shard_map/ppermute | solution.py:678
  60.1 14.1 %collective-permute-start.15 = (bf16[4,12,16,512]{3,2,1,0:T(8,128)(2,1)}, bf16[4,12,16,512]{3,2,1,0:T(8,128)(2,1)S(1)}, u32[]{:S(2)}, u32[]{:S(2)}) collective-permute-start(bf16[4,12,16,512]{3,2,1,0:T(8,128)(2,1)} %collective-permute-done.6.refs_10_), channel_id=1, source_target_pairs={{0,4},{1,3},{2,6},{3,1},{4,0},{5,7},{6,2},{7,5},{8,12},{9,11},{10,... | collective-permute-start | bytes 2359304 | tf_op jit(solution)/shard_map/ppermute | solution.py:678
  60.8 14.9 %collective-permute-start.16 = (bf16[4,12,16,512]{3,2,1,0:T(8,128)(2,1)}, bf16[4,12,16,512]{3,2,1,0:T(8,128)(2,1)S(1)}, u32[]{:S(2)}, u32[]{:S(2)}) collective-permute-start(bf16[4,12,16,512]{3,2,1,0:T(8,128)(2,1)} %pad_maximum_fusion.refs_9_), channel_id=1, source_target_pairs={{0,1},{1,0},{2,3},{3,2},{4,5},{5,4},{6,7},{7,6},{8,9},{9,8},{10,11... | collective-permute-start | bytes 2359304 | tf_op jit(solution)/shard_map/ppermute | solution.py:678
  60.8 14.9 %collective-permute-start.17 = (bf16[4,12,16,512]{3,2,1,0:T(8,128)(2,1)}, bf16[4,12,16,512]{3,2,1,0:T(8,128)(2,1)S(1)}, u32[]{:S(2)}, u32[]{:S(2)}) collective-permute-start(bf16[4,12,16,512]{3,2,1,0:T(8,128)(2,1)} %collective-permute-done.6.refs_10_), channel_id=1, source_target_pairs={{0,1},{1,0},{2,3},{3,2},{4,5},{5,4},{6,7},{7,6},{8,9},{9,8},{10,11... | collective-permute-start | bytes 2359304 | tf_op jit(solution)/shard_map/ppermute | solution.py:678
  61.3 14.4 %collective-permute-start.18 = (bf16[4,12,16,512]{3,2,1,0:T(8,128)(2,1)S(1)}, bf16[4,12,16,512]{3,2,1,0:T(8,128)(2,1)}, u32[]{:S(2)}, u32[]{:S(2)}) collective-permute-start(bf16[4,12,16,512]{3,2,1,0:T(8,128)(2,1)S(1)} %collective-permute-done.14.refs_11_), channel_id=1, source_target_pairs={{0,1},{1,0},{2,3},{3,2},{4,5},{5,4},{6,7},{7,6},{8,9},{9,8},{10,11... | collective-permute-start | bytes 2359304 | tf_op jit(solution)/shard_map/ppermute | solution.py:678
  74.2 2.5 %collective-permute-start.19 = (bf16[4,12,16,512]{3,2,1,0:T(8,128)(2,1)S(1)}, bf16[4,12,16,512]{3,2,1,0:T(8,128)(2,1)}, u32[]{:S(2)}, u32[]{:S(2)}) collective-permute-start(bf16[4,12,16,512]{3,2,1,0:T(8,128)(2,1)S(1)} %collective-permute-done.15.refs_12_), channel_id=1, source_target_pairs={{0,1},{1,0},{2,3},{3,2},{4,5},{5,4},{6,7},{7,6},{8,9},{9,8},{10,11... | collective-permute-start | bytes 2359304 | tf_op jit(solution)/shard_map/ppermute | solution.py:678
  126.8 6.5 %collective-permute-start.20 = (bf16[16,9,16,512]{3,2,1,0:T(8,128)(2,1)}, bf16[16,9,16,512]{3,2,1,0:T(8,128)(2,1)S(1)}, u32[]{:S(2)}, u32[]{:S(2)}) collective-permute-start(bf16[16,9,16,512]{3,2,1,0:T(8,128)(2,1)} %get-tuple-element.149), channel_id=1, source_target_pairs={{0,1},{1,0},{2,3},{3,2},{4,5},{5,4},{6,7},{7,6},{8,9},{9,8},{10,11... | collective-permute-start | bytes 7077896 | tf_op jit(solution)/shard_map/ppermute | solution.py:678
  127.2 28.5 %collective-permute-start.22 = (bf16[16,6,16,512]{3,2,1,0:T(8,128)(2,1)}, bf16[16,6,16,512]{3,2,1,0:T(8,128)(2,1)}, u32[]{:S(2)}, u32[]{:S(2)}) collective-permute-start(bf16[16,6,16,512]{3,2,1,0:T(8,128)(2,1)} %get-tuple-element.151), channel_id=1, source_target_pairs={{0,1},{1,0},{2,3},{3,2},{4,5},{5,4},{6,7},{7,6},{8,9},{9,8},{10,11... | collective-permute-start | bytes 4718600 | tf_op jit(solution)/shard_map/ppermute | solution.py:678
  133.3 64.4 %copy-start = (bf16[16,9,16,512]{3,2,1,0:T(8,128)(2,1)}, bf16[16,9,16,512]{3,2,1,0:T(8,128)(2,1)S(1)}, u32[]{:S(2)}) copy-start(bf16[16,9,16,512]{3,2,1,0:T(8,128)(2,1)S(1)} %collective-permute-done.20.refs_1_) | copy-start | bytes 7077892
  137.0 18.8 %collective-permute-start.21 = (bf16[8,9,16,512]{3,2,1,0:T(8,128)(2,1)}, bf16[8,9,16,512]{3,2,1,0:T(8,128)(2,1)S(1)}, u32[]{:S(2)}, u32[]{:S(2)}) collective-permute-start(bf16[8,9,16,512]{3,2,1,0:T(8,128)(2,1)} %add_convert_fusion), channel_id=1, source_target_pairs={{0,4},{1,3},{2,6},{3,1},{4,0},{5,7},{6,2},{7,5},{8,12},{9,11},{10,... | collective-permute-start | bytes 3538952 | tf_op jit(solution)/shard_map/ppermute | solution.py:678
  155.8 41.9 %copy-start.1 = (bf16[8,9,16,512]{3,2,1,0:T(8,128)(2,1)}, bf16[8,9,16,512]{3,2,1,0:T(8,128)(2,1)S(1)}, u32[]{:S(2)}) copy-start(bf16[8,9,16,512]{3,2,1,0:T(8,128)(2,1)S(1)} %collective-permute-done.21.refs_2_) | copy-start | bytes 3538948
  155.8 21.6 %collective-permute-start.23 = (bf16[16,3,16,512]{3,2,1,0:T(8,128)(2,1)}, bf16[16,3,16,512]{3,2,1,0:T(8,128)(2,1)}, u32[]{:S(2)}, u32[]{:S(2)}) collective-permute-start(bf16[16,3,16,512]{3,2,1,0:T(8,128)(2,1)} %get-tuple-element.164), channel_id=1, source_target_pairs={{0,1},{1,0},{2,3},{3,2},{4,5},{5,4},{6,7},{7,6},{8,9},{9,8},{10,11... | collective-permute-start | bytes 2359304 | tf_op jit(solution)/shard_map/ppermute | solution.py:678
  158.8 18.6 %collective-permute-start.24 = (bf16[8,6,16,512]{3,2,1,0:T(8,128)(2,1)}, bf16[8,6,16,512]{3,2,1,0:T(8,128)(2,1)}, u32[]{:S(2)}, u32[]{:S(2)}) collective-permute-start(bf16[8,6,16,512]{3,2,1,0:T(8,128)(2,1)} %add_convert_fusion.1), channel_id=1, source_target_pairs={{0,4},{1,3},{2,6},{3,1},{4,0},{5,7},{6,2},{7,5},{8,12},{9,11},{10,... | collective-permute-start | bytes 2359304 | tf_op jit(solution)/shard_map/ppermute | solution.py:678
  161.2 15.4 %collective-permute-start.25 = (bf16[4,9,16,512]{3,2,1,0:T(8,128)(2,1)}, bf16[4,9,16,512]{3,2,1,0:T(8,128)(2,1)}, u32[]{:S(2)}, u32[]{:S(2)}) collective-permute-start(bf16[4,9,16,512]{3,2,1,0:T(8,128)(2,1)} %add_convert_fusion.2), channel_id=1, source_target_pairs={{0,2},{1,5},{2,0},{3,7},{4,6},{5,1},{6,4},{7,3},{8,10},{9,13},{10,... | collective-permute-start | bytes 1769480 | tf_op jit(solution)/shard_map/ppermute | solution.py:678
  162.8 12.0 %collective-permute-start.26 = (bf16[48,1536]{1,0:T(8,128)(2,1)S(1)}, bf16[48,1536]{1,0:T(8,128)(2,1)S(1)}, u32[]{:S(2)}, u32[]{:S(2)}) collective-permute-start(bf16[48,1536]{1,0:T(8,128)(2,1)S(1)} %fusion.30), channel_id=1, source_target_pairs={{0,1},{1,0},{2,3},{3,2},{4,5},{5,4},{6,7},{7,6},{8,9},{9,8},{10,11... | collective-permute-start | bytes 442376 | tf_op jit(solution)/shard_map/ppermute | solution.py:678
  178.7 11.5 %collective-permute-start.30 = (bf16[8,3,16,512]{3,2,1,0:T(8,128)(2,1)S(1)}, bf16[8,3,16,512]{3,2,1,0:T(8,128)(2,1)S(1)}, u32[]{:S(2)}, u32[]{:S(2)}) collective-permute-start(bf16[8,3,16,512]{3,2,1,0:T(8,128)(2,1)S(1)} %add_convert_fusion.4), channel_id=1, source_target_pairs={{0,4},{1,3},{2,6},{3,1},{4,0},{5,7},{6,2},{7,5},{8,12},{9,11},{10,... | collective-permute-start | bytes 1179656 | tf_op jit(solution)/shard_map/ppermute | solution.py:678
  180.3 11.5 %collective-permute-start.29 = (bf16[4,6,16,512]{3,2,1,0:T(8,128)(2,1)S(1)}, bf16[4,6,16,512]{3,2,1,0:T(8,128)(2,1)S(1)}, u32[]{:S(2)}, u32[]{:S(2)}) collective-permute-start(bf16[4,6,16,512]{3,2,1,0:T(8,128)(2,1)S(1)} %add_convert_fusion.3), channel_id=1, source_target_pairs={{0,2},{1,5},{2,0},{3,7},{4,6},{5,1},{6,4},{7,3},{8,10},{9,13},{10,... | collective-permute-start | bytes 1179656 | tf_op jit(solution)/shard_map/ppermute | solution.py:678
  183.3 14.4 %collective-permute-start.28 = (bf16[2,9,16,512]{3,2,1,0:T(8,128)(2,1)S(1)}, bf16[2,9,16,512]{3,2,1,0:T(8,128)(2,1)S(1)}, u32[]{:S(2)}, u32[]{:S(2)}) collective-permute-start(bf16[2,9,16,512]{3,2,1,0:T(8,128)(2,1)S(1)} %add_convert_fusion.5), channel_id=1, source_target_pairs={{0,16},{1,9},{2,18},{3,11},{4,20},{5,13},{6,22},{7,15},{8,24},{9,1... | collective-permute-start | bytes 884744 | tf_op jit(solution)/shard_map/ppermute | solution.py:678
  188.6 10.9 %collective-permute-start.27 = (bf16[48,1536]{1,0:T(8,128)(2,1)S(1)}, bf16[48,1536]{1,0:T(8,128)(2,1)S(1)}, u32[]{:S(2)}, u32[]{:S(2)}) collective-permute-start(bf16[48,1536]{1,0:T(8,128)(2,1)S(1)} %fusion.29), channel_id=1, source_target_pairs={{0,4},{1,3},{2,6},{3,1},{4,0},{5,7},{6,2},{7,5},{8,12},{9,11},{10,... | collective-permute-start | bytes 442376 | tf_op jit(solution)/shard_map/ppermute | solution.py:678
  190.2 18.1 %copy-start.5 = (bf16[8,3,16,512]{3,2,1,0:T(8,128)(2,1)}, bf16[8,3,16,512]{3,2,1,0:T(8,128)(2,1)S(1)}, u32[]{:S(2)}) copy-start(bf16[8,3,16,512]{3,2,1,0:T(8,128)(2,1)S(1)} %collective-permute-done.30.refs_14_) | copy-start | bytes 1179652
  191.5 10.2 %collective-permute-start.33 = (bf16[4,3,16,512]{3,2,1,0:T(8,128)(2,1)S(1)}, bf16[4,3,16,512]{3,2,1,0:T(8,128)(2,1)S(1)}, u32[]{:S(2)}, u32[]{:S(2)}) collective-permute-start(bf16[4,3,16,512]{3,2,1,0:T(8,128)(2,1)S(1)} %add_convert_fusion.7), channel_id=1, source_target_pairs={{0,2},{1,5},{2,0},{3,7},{4,6},{5,1},{6,4},{7,3},{8,10},{9,13},{10,... | collective-permute-start | bytes 589832 | tf_op jit(solution)/shard_map/ppermute | solution.py:678
  193.1 9.9 %collective-permute-start.32 = (bf16[2,6,16,512]{3,2,1,0:T(8,128)(2,1)S(1)}, bf16[2,6,16,512]{3,2,1,0:T(8,128)(2,1)S(1)}, u32[]{:S(2)}, u32[]{:S(2)}) collective-permute-start(bf16[2,6,16,512]{3,2,1,0:T(8,128)(2,1)S(1)} %add_convert_fusion.6), channel_id=1, source_target_pairs={{0,16},{1,9},{2,18},{3,11},{4,20},{5,13},{6,22},{7,15},{8,24},{9,1... | collective-permute-start | bytes 589832 | tf_op jit(solution)/shard_map/ppermute | solution.py:678
  199.6 5.2 %collective-permute-start.31 = (bf16[48,1536]{1,0:T(8,128)(2,1)S(1)}, bf16[48,1536]{1,0:T(8,128)(2,1)S(1)}, u32[]{:S(2)}, u32[]{:S(2)}) collective-permute-start(bf16[48,1536]{1,0:T(8,128)(2,1)S(1)} %add_convert_fusion.11), channel_id=1, source_target_pairs={{0,2},{1,5},{2,0},{3,7},{4,6},{5,1},{6,4},{7,3},{8,10},{9,13},{10,... | collective-permute-start | bytes 442376 | tf_op jit(solution)/shard_map/ppermute | solution.py:678
  201.7 20.5 %copy-start.10 = (bf16[4,3,16,512]{3,2,1,0:T(8,128)(2,1)}, bf16[4,3,16,512]{3,2,1,0:T(8,128)(2,1)S(1)}, u32[]{:S(2)}) copy-start(bf16[4,3,16,512]{3,2,1,0:T(8,128)(2,1)S(1)} %collective-permute-done.33.refs_15_) | copy-start | bytes 589828
  202.7 21.6 %copy-start.8 = (bf16[5,208,512]{2,1,0:T(8,128)(2,1)S(1)}, bf16[5,208,512]{2,1,0:T(8,128)(2,1)}, u32[]{:S(2)}) copy-start(bf16[5,208,512]{2,1,0:T(8,128)(2,1)} %get-tuple-element.145) | copy-start | bytes 3194884
  202.7 5.6 %collective-permute-start.35 = (bf16[2,3,16,512]{3,2,1,0:T(8,128)(2,1)S(1)}, bf16[2,3,16,512]{3,2,1,0:T(8,128)(2,1)S(1)}, u32[]{:S(2)}, u32[]{:S(2)}) collective-permute-start(bf16[2,3,16,512]{3,2,1,0:T(8,128)(2,1)S(1)} %add_convert_fusion.14), channel_id=1, source_target_pairs={{0,16},{1,9},{2,18},{3,11},{4,20},{5,13},{6,22},{7,15},{8,24},{9,1... | collective-permute-start | bytes 294920 | tf_op jit(solution)/shard_map/ppermute | solution.py:678
  203.0 21.3 %copy-start.12 = (bf16[2,6,16,512]{3,2,1,0:T(8,128)(2,1)}, bf16[2,6,16,512]{3,2,1,0:T(8,128)(2,1)S(1)}, u32[]{:S(2)}) copy-start(bf16[2,6,16,512]{3,2,1,0:T(8,128)(2,1)S(1)} %collective-permute-done.32.refs_10_) | copy-start | bytes 589828
  204.8 12.0 %collective-permute-start.34 = (bf16[48,1536]{1,0:T(8,128)(2,1)S(1)}, bf16[48,1536]{1,0:T(8,128)(2,1)S(1)}, u32[]{:S(2)}, u32[]{:S(2)}) collective-permute-start(bf16[48,1536]{1,0:T(8,128)(2,1)S(1)} %add_convert_fusion.10), channel_id=1, source_target_pairs={{0,16},{1,9},{2,18},{3,11},{4,20},{5,13},{6,22},{7,15},{8,24},{9,1... | collective-permute-start | bytes 442376 | tf_op jit(solution)/shard_map/ppermute | solution.py:678
  216.9 5.2 %collective-permute-start.36 = (bf16[48,1536]{1,0:T(8,128)(2,1)S(1)}, bf16[48,1536]{1,0:T(8,128)(2,1)S(1)}, u32[]{:S(2)}, u32[]{:S(2)}) collective-permute-start(bf16[48,1536]{1,0:T(8,128)(2,1)S(1)} %add_convert_fusion.9), channel_id=1, source_target_pairs={{0,8},{1,17},{2,10},{3,19},{4,12},{5,21},{6,14},{7,23},{8,0},{9,25... | collective-permute-start | bytes 442376 | tf_op jit(solution)/shard_map/ppermute | solution.py:678
  216.9 11.8 %collective-permute-start.38 = (bf16[1,9,16,512]{3,2,1,0:T(8,128)(2,1)}, bf16[1,9,16,512]{3,2,1,0:T(8,128)(2,1)S(1)}, u32[]{:S(2)}, u32[]{:S(2)}) collective-permute-start(bf16[1,9,16,512]{3,2,1,0:T(8,128)(2,1)} %add_convert_fusion.12), channel_id=1, source_target_pairs={{0,8},{1,17},{2,10},{3,19},{4,12},{5,21},{6,14},{7,23},{8,0},{9,25... | collective-permute-start | bytes 442376 | tf_op jit(solution)/shard_map/ppermute | solution.py:678
  222.1 10.4 %collective-permute-start.37 = (bf16[48,1536]{1,0:T(8,128)(2,1)S(1)}, bf16[48,1536]{1,0:T(8,128)(2,1)S(1)}, u32[]{:S(2)}, u32[]{:S(2)}) collective-permute-start(bf16[48,1536]{1,0:T(8,128)(2,1)S(1)} %add_convert_fusion.8.mine_ref), channel_id=1, source_target_pairs={{0,1},{1,0},{2,3},{3,2},{4,5},{5,4},{6,7},{7,6},{8,9},{9,8},{10,11... | collective-permute-start | bytes 442376 | tf_op jit(solution)/shard_map/ppermute | solution.py:678
  222.2 6.5 %collective-permute-start.39 = (bf16[1,6,16,512]{3,2,1,0:T(8,128)(2,1)S(1)}, bf16[1,6,16,512]{3,2,1,0:T(8,128)(2,1)S(1)}, u32[]{:S(2)}, u32[]{:S(2)}) collective-permute-start(bf16[1,6,16,512]{3,2,1,0:T(8,128)(2,1)S(1)} %add_convert_fusion.13), channel_id=1, source_target_pairs={{0,8},{1,17},{2,10},{3,19},{4,12},{5,21},{6,14},{7,23},{8,0},{9,25... | collective-permute-start | bytes 294920 | tf_op jit(solution)/shard_map/ppermute | solution.py:678
  222.3 6.5 %collective-permute-start.40 = (bf16[1,3,16,512]{3,2,1,0:T(8,128)(2,1)S(1)}, bf16[1,3,16,512]{3,2,1,0:T(8,128)(2,1)S(1)}, u32[]{:S(2)}, u32[]{:S(2)}) collective-permute-start(bf16[1,3,16,512]{3,2,1,0:T(8,128)(2,1)S(1)} %add_convert_fusion.15), channel_id=1, source_target_pairs={{0,8},{1,17},{2,10},{3,19},{4,12},{5,21},{6,14},{7,23},{8,0},{9,25... | collective-permute-start | bytes 147464 | tf_op jit(solution)/shard_map/ppermute | solution.py:678
  (27 other events, 162.0 us)

commit v3 on v2

--- a/solution.py
+++ b/solution.py
@@ -213,6 +213,33 @@
                 send(place + group, lambda block: pl.ds(pl.multiple_of(block * BLOCK, BLOCK), BLOCK))
     for side in range(2):
         pltpu.make_async_copy(stage.at[side], outs[side], sem).wait()
+
+
+def put_sums(both, slots, outs, odd):
+    gate = both[0]["gain_two"].shape[1]
+    rows = slots // BLOCK * BLOCK + both[0]["bias_two"].shape[0]
+    strips, high = strips_of(rows, gate)
+    at = slots % BLOCK
+    row = lax.broadcasted_iota(jnp.int32, (8, gate), 0)
+    packed = []
+    for sums in both:
+        one = lambda name: jnp.sum(sums[name][...], 0, keepdims=True)
+        bias_two = sums["bias_two"][at : at + 1] + sums["bias_two"][at + 1 : at + 2]
+        narrow = [one("b_out")]
+        if "gain_one" in sums:
+            narrow += [0.5 * one("gain_one"), 0.5 * one("bias_one")]
+        filled = sum(part.shape[1] for part in narrow)
+        if filled < gate:
+            narrow.append(jnp.zeros((1, gate - filled), F32))
+        narrow = jnp.concatenate(narrow, 1)
+        lines = [0.5 * one("b_left"), 0.5 * one("b_right"), one("gain_two"), bias_two, narrow]
+        total = jnp.zeros((8, gate), F32)
+        for place, line in enumerate(lines):
+            total = jnp.where(row == place, line, total)
+        square = [sums["spatial"][strip * high : (strip + 1) * high] for strip in range(strips)]
+        packed.append(jnp.concatenate([jnp.concatenate(square, 1), total], 0).astype(BF16))
+    outs[0][...] = jnp.where(odd, packed[1], packed[0])
+    outs[1][...] = jnp.where(odd, packed[0], packed[1])
 
 
 def zero(refs):
@@ -470,7 +497,7 @@
     return dict(zip(outs, results)), dict(zip(shapes, results[n_o:])), blocks[:2], blocks[2:]
 
 
-def backward_slots(kept, mixed_grad, valid, mixer_back, w, owner, slots):
+def backward_slots(kept, mixed_grad, valid, mixer_back, w, owner, both, slots):
     images, rows, gate = mixed_grad.shape
     width = w["gain_one"].shape[1]
     half = width // BLOCK // 2
@@ -478,47 +505,66 @@
     names = ("b_right", "spatial", "gain_two", "bias_two")
     reads = ("white", "right_slope", "slot_in", "inverse", "normed")
     block_shape = (half, gate // GROUP, BLOCK, GROUP)
-    n_r, n_s = len(reads), len(names)
+    high = strips_of(rows, gate)[1]
+    flat = [(block, name) for block in range(2) for name in both[block]]
+    n_r, n_f, n_s = len(reads), len(flat), len(names)
 
     def kernel(owner_ref, mixed_ref, valid_ref, back_ref, gain_two, *refs):
         t = {name: ref.at[0] for name, ref in zip(reads, refs)}
         t["mixed_grad"] = mixed_ref.at[0]
-        out, sums, outs = refs[n_r], dict(zip(names, refs[n_r + 1 :])), refs[n_r + 1 + n_s :][:2]
-        normed, right_grad, result, stage, out_sem = refs[n_r + 3 + n_s :]
+        out, *outs = refs[n_r + n_f :][:5]
+        rest = refs[n_r + n_f + 5 :]
+        own = dict(zip(names, rest))
+        normed, right_grad, result, stage, out_sem = rest[n_s:]
         step = pl.program_id(0)
 
         @pl.when(step == 0)
         def _():
-            zero(sums.values())
+            zero(own.values())
 
         mine = pl.ds(pl.multiple_of(step * rows, BLOCK), rows)
         normed[mine] = t["normed"][...]
         here = right_grad.at[mine]
-        backward_right(valid_ref[0], back_ref[0], t["inverse"][...], gain_two, t, here, sums["b_right"], sums, slots)
+        backward_right(valid_ref[0], back_ref[0], t["inverse"][...], gain_two, t, here, own["b_right"], own, slots)
         out[0] = here[...]
 
         @pl.when(step == images - 1)
         def _():
-            put_weight_grads(owner_ref, [(normed, right_grad, 0)], result, stage, outs, out_sem)
+            put_weight_grads(owner_ref, [(normed, right_grad, 0)], result, stage, outs[:2], out_sem)
+            sums = {}, {}
+            for (block, name), ref in zip(flat, refs[n_r:]):
+                sums[block][name] = ref
+            sums[0].update(own)
+            put_sums(sums, slots, outs[2:], owner_ref[0] % 2 == 1)
 
     results = call(
         kernel,
         "backward_slots",
         (images,),
         [image(rows, gate), image(rows, 1), image(rows, rows), whole((1, gate))]
-        + [image(rows, kept[name].shape[2]) for name in reads],
-        [((images, rows, gate), BF16)] + [(shapes[name], F32) for name in names] + [(block_shape, BF16)] * 2,
-        [image(rows, gate)] + [whole(shapes[name]) for name in names] + anywhere(2),
-        [pltpu.VMEM((images * rows, width), BF16), pltpu.VMEM((images * rows, gate), BF16)]
+        + [image(rows, kept[name].shape[2]) for name in reads]
+        + [whole(both[block][name].shape) for block, name in flat],
+        [((images, rows, gate), BF16)] + [(block_shape, BF16)] * 2 + [((high + 8, gate), BF16)] * 2,
+        [image(rows, gate)] + anywhere(2) + [whole((high + 8, gate))] * 2,
+        [pltpu.VMEM(shapes[name], F32) for name in names]
+        + [pltpu.VMEM((images * rows, width), BF16), pltpu.VMEM((images * rows, gate), BF16)]
         + [pltpu.VMEM((width, GROUP), BF16), pltpu.VMEM((2,) + block_shape, BF16), pltpu.SemaphoreType.DMA],
         9_000_000_000,
         60,
         table=1,
-    )(owner, mixed_grad, valid, mixer_back, w["gain_two"], *[kept[name] for name in reads])
-    return results[0], dict(zip(names, results[1:])), results[1 + n_s :]
-
-
-def backward_first(values, left_grad, right_grad, upstream, w, owner, pieces, place):
+    )(
+        owner,
+        mixed_grad,
+        valid,
+        mixer_back,
+        w["gain_two"],
+        *[kept[name] for name in reads],
+        *[both[block][name] for block, name in flat],
+    )
+    return results[0], results[1:3], results[3:]
+
+
+def backward_first(values, left_grad, right_grad, upstream, w, owner, pieces, place, slots):
     images, rows, width = values.shape
     gate = left_grad.shape[2]
     n_p = len(pieces)
@@ -533,12 +579,18 @@
             zero((gain_sum, bias_sum))
 
         weights = {"w_in": w_in, "gain_one": gain_ref}
-        sums = {"gain_one": gain_sum, "bias_one": bias_sum}
-        out[0] = backward_norm(values_ref[0].astype(F32), (left_ref.at[0], right_ref.at[0]), up_ref[0], weights, sums)
+        own = {"gain_one": gain_sum, "bias_one": bias_sum}
+        halves = left_ref.at[0], right_ref.at[0]
+        result = backward_norm(values_ref[0].astype(F32), halves, up_ref[0], weights, own)
+        for at in range(images):
+
+            @pl.when(step == at)
+            def _(at=at):
+                out[at * slots : (at + 1) * slots] = result[:slots]
 
         @pl.when(step == images - 1)
         def _():
-            line[...] = jnp.zeros_like(line)
+            zero((line,))
             for at, ref in enumerate((gain_sum, bias_sum)):
                 line[5:6, (1 + at) * width : (2 + at) * width] = 0.5 * jnp.sum(ref[...], 0, keepdims=True)
 
@@ -548,48 +600,13 @@
         (images,),
         [image(rows, width), image(rows, gate), image(rows, gate), image(rows, width), whole((1, width))]
         + anywhere(n_p),
-        [((images, rows, width), F32), ((8, gate), F32)],
-        [image(rows, width), whole((8, gate))],
+        [((images * slots, width), F32), ((8, gate), F32)],
+        [whole((images * slots, width)), whole((8, gate))],
         [pltpu.VMEM((8, width), F32)] * 2 + [in_scratch(width, 2 * gate), pltpu.SemaphoreType.DMA],
         6_000_000_000,
         60,
         table=1,
     )(owner, values, left_grad, right_grad, upstream, w["gain_one"], *pieces)
-
-
-def pack_sums(both, slots):
-    gate = both[0]["gain_two"].shape[1]
-    rows = slots // BLOCK * BLOCK + both[0]["bias_two"].shape[0]
-    strips, high = strips_of(rows, gate)
-    at = slots % BLOCK
-    flat = [(block, name) for block in range(2) for name in SUMS if name in both[block]]
-
-    def kernel(*refs):
-        out = refs[-1]
-        row = lax.broadcasted_iota(jnp.int32, (8, gate), 0)
-        for block in range(2):
-            sums = {name: ref for (at_block, name), ref in zip(flat, refs) if at_block == block}
-            out[block, :high] = jnp.concatenate(
-                [sums["spatial"][strip * high : (strip + 1) * high] for strip in range(strips)], 1
-            )
-            one = lambda name: jnp.sum(sums[name][...], 0, keepdims=True)
-            narrow = one("b_out")
-            if "gain_one" in sums:
-                narrow = jnp.concatenate([narrow, 0.5 * one("gain_one"), 0.5 * one("bias_one")], 1)
-            bias_two = sums["bias_two"][at : at + 1] + sums["bias_two"][at + 1 : at + 2]
-            lines = [0.5 * one("b_left"), 0.5 * one("b_right"), one("gain_two"), bias_two]
-            total = jnp.zeros((8, gate), F32)
-            for place, line in enumerate(lines):
-                total = jnp.where(row == place, line, total)
-            out[block, high:] = total
-            out[block, high + 4 : high + 5, : narrow.shape[1]] = narrow
-
-    return pl.pallas_call(
-        kernel,
-        out_shape=jax.ShapeDtypeStruct((2, high + 8, gate), F32),
-        compiler_params=pltpu.CompilerParams(vmem_limit_bytes=60 << 20),
-        name="pack_sums",
-    )(*[both[block][name] for block, name in flat])
 
 
 def unpack_sums(odd, mine, theirs, slots, width):
@@ -628,42 +645,36 @@
     return [*results[:5], results[5].transpose(1, 0, 2), *results[6:]]
 
 
-def add_blocks(chains, places, groups, per):
-    counts = [len(chain) for chain in chains]
-    flat = [array for chain in chains for array in chain]
-    width = flat[0].shape[-1]
+def add_blocks(terms, groups, per):
+    arrays = []
+    for pairs in terms.values():
+        arrays += [array for array, unused in pairs if not any(array is other for other in arrays)]
+    index = {id(array): at for at, array in enumerate(arrays)}
+    width = arrays[0].shape[-1]
 
     def kernel(*refs):
         in_out, out_out = refs[-2:]
-        start = 0
-        for count, spots in zip(counts, places):
-            for at, (block, group) in enumerate(spots):
-                total = None
-                for ref in refs[start : start + count]:
-                    part = (ref[0, at] if len(ref.shape) == 4 else ref[at]).astype(F32)
-                    total = part if total is None else total + part
-                if group < groups:
-                    in_out[block, :, group * GROUP : (group + 1) * GROUP] = total
-                else:
-                    first = (group - groups) * BLOCK
-                    out_out[block, first : first + BLOCK] = total
-            start += count
-
-    def spec(array):
-        if array.ndim == 4:
-            return pl.BlockSpec((1,) + array.shape[1:], lambda i: (0, 0, 0, 0))
-        return pl.BlockSpec(array.shape, lambda i: (0, 0, 0))
+        for (block, group), pairs in terms.items():
+            total = None
+            for array, at in pairs:
+                part = refs[index[id(array)]][0, at].astype(F32)
+                total = part if total is None else total + part
+            if group < groups:
+                in_out[block, :, group * GROUP : (group + 1) * GROUP] = total
+            else:
+                first = (group - groups) * BLOCK
+                out_out[block, first : first + BLOCK] = total
 
     shapes = [(2, BLOCK, groups * GROUP), (2, per * BLOCK, width)]
     return pl.pallas_call(
         kernel,
         grid=(1,),
-        in_specs=[spec(array) for array in flat],
+        in_specs=[pl.BlockSpec((1,) + array.shape[1:], lambda i: (0, 0, 0, 0)) for array in arrays],
         out_specs=[whole(shape) for shape in shapes],
         out_shape=[jax.ShapeDtypeStruct(shape, F32) for shape in shapes],
         compiler_params=pltpu.CompilerParams(vmem_limit_bytes=60 << 20),
         name="add_blocks",
-    )(*flat)
+    )(*arrays)
 
 
 class Tree:
@@ -705,41 +716,86 @@
         last = after(last, wait)
         yield [*pieces, last, *others, self.swap(last)]
 
-    def scatter(self, mine, theirs):
-        parts = [mine, self.swap(theirs)]
-        wait = yield theirs, parts[1]
-        for step in reversed(range(self.steps)):
-            keep = 1 << step
-            sent = self.add(after(parts, wait), slice(keep, 2 * keep)).astype(BF16)
-            parts.append(self.swap(sent, step))
-            wait = yield sent, parts[-1]
-        yield parts
-
-    def add(self, parts, at):
-        total = parts[0][at].astype(F32)
-        for part in parts[1:]:
+    def sum(self, mine, theirs):
+        return TreeSum(self, mine, theirs)
+
+    def finish(self, terms, groups, per):
+        return add_blocks(terms, groups, per)
+
+    def total(self, mine, theirs):
+        far = self.steps - 2
+        order = [*reversed(range(far)), far, far + 1]
+        add = lambda one, other: (one.astype(F32) + other.astype(F32)).astype(BF16)
+        got = self.swap(theirs)
+        wait = yield theirs
+        mine = add(mine, after(got, wait))
+        got = self.swap(mine, order[0])
+        late = yield mine
+        late = late.astype(BF16)
+        late_got = self.swap(late, order[0])
+        wait = yield late
+        late = late.astype(F32) + late_got.astype(F32)
+        mine = mine.astype(F32) + after(got, wait).astype(F32)
+        mine = (mine + jnp.pad(late, ((mine.shape[0] - late.shape[0], 0), (0, 0)))).astype(BF16)
+        for step in order[1:]:
+            got = self.swap(mine, step)
+            wait = yield mine
+            mine = add(mine, after(got, wait))
+        yield lax.axis_index("narrow") % 2, mine, self.swap(mine)
+
+
+class TreeSum:
+    def __init__(self, links, mine, theirs):
+        self.links, self.step = links, links.steps
+        self.sent, self.got = theirs, links.swap(theirs)
+        self.columns, self.shared = [[mine, self.got]], []
+
+    def add(self, at):
+        total = []
+        for column in self.columns:
+            total.append(column[0][at].astype(F32))
+            for part in column[1:]:
+                total[-1] = total[-1] + part[at].astype(F32)
+        total = jnp.concatenate(total, 1) if len(total) > 1 else total[0]
+        for part in self.shared:
             total = total + part[at].astype(F32)
         return total
 
-    def finish(self, chains, places, groups, per):
-        return add_blocks(chains, places, groups, per)
-
-    def total(self, values):
-        odd = lax.axis_index("narrow") % 2
-        mine = jnp.where(odd == 1, values[1], values[0]).astype(BF16)
-        theirs = jnp.where(odd == 1, values[0], values[1]).astype(BF16)
-        got = self.swap(theirs)
-        late = yield theirs, got
-        wait = None
-        for step in [*reversed(range(self.steps)), -1]:
-            got = after(got, wait)
-            mine = mine.astype(F32) + got.astype(F32)
-            if step == self.steps - 1:
-                mine = mine + jnp.pad(late, ((mine.shape[0] - late.shape[0], 0), (0, 0)))
-            mine = mine.astype(BF16)
-            got = self.swap(mine, *([step] if step >= 0 else []))
-            wait = yield mine, got
-        yield odd, mine, got
+    def send(self, wait):
+        self.columns, self.shared = after((self.columns, self.shared), wait)
+        self.step -= 1
+        keep = 1 << self.step
+        self.sent = self.add(slice(keep, 2 * keep)).astype(BF16)
+        self.got = self.links.swap(self.sent, self.step)
+        (self.columns[0] if len(self.columns) == 1 else self.shared).append(self.got)
+        return self.sent
+
+    def join(self, other):
+        self.columns = self.columns + other.columns
+        return self
+
+    def terms(self):
+        terms = []
+        for column in self.columns:
+            for at in range(column[0].shape[1]):
+                terms.append([(part, at) for part in column] + [(part, len(terms)) for part in self.shared])
+        return terms
+
+
+class PlainSum:
+    def __init__(self, mine, theirs):
+        self.blocks = jnp.concatenate([mine, theirs]).astype(F32)
+        self.sent = self.got = theirs
+
+    def send(self, wait):
+        return self.sent
+
+    def join(self, other):
+        self.blocks = jnp.concatenate([self.blocks, other.blocks], 1)
+        return self
+
+    def terms(self):
+        return [self.blocks[:, at] for at in range(self.blocks.shape[1])]
 
 
 class Plain:
@@ -757,30 +813,28 @@
             yield gathered, gathered
         yield [pack_blocks(gathered, self.blocks)]
 
-    def scatter(self, mine, theirs):
-        for unused in range(self.steps + 1):
-            yield theirs, mine
-        yield jnp.concatenate([mine, theirs]).astype(F32)
-
-    def finish(self, chains, places, groups, per):
-        spots = {spot: chain[:, at] for chain, place in zip(chains, places) for at, spot in enumerate(place)}
+    def sum(self, mine, theirs):
+        return PlainSum(mine, theirs)
+
+    def finish(self, terms, groups, per):
         in_grad, out_grad = [], []
         for block in range(2):
-            inner = jnp.concatenate([spots[block, group] for group in range(groups)], 2)
-            outer = jnp.concatenate([spots[block, groups + part] for part in range(per)], 1)
+            inner = jnp.concatenate([terms[block, group] for group in range(groups)], 2)
+            outer = jnp.concatenate([terms[block, groups + part] for part in range(per)], 1)
             in_grad.append(inner.reshape(self.width, -1))
             out_grad.append(outer.reshape(self.gate, -1))
         return [
             lax.psum_scatter(jnp.stack(grad), AXES, scatter_dimension=1, tiled=True) for grad in (in_grad, out_grad)
         ]
 
-    def total(self, values):
-        late = yield values, values
-        late = jnp.pad(late, ((values.shape[1] - late.shape[0], 0), (0, 0)))
-        values = lax.psum(jnp.stack([values[0] + late, values[1]]), AXES)
-        for unused in range(self.steps + 1):
-            yield values, values
-        yield jnp.int32(0), values[0], values[1]
+    def total(self, mine, theirs):
+        yield mine
+        late = yield mine
+        mine = mine.astype(F32) + jnp.pad(late, ((mine.shape[0] - late.shape[0], 0), (0, 0)))
+        yield late
+        for unused in range(self.steps - 1):
+            yield mine
+        yield jnp.int32(0), *lax.psum((mine, theirs.astype(F32)), AXES)
 
 
 def pack_blocks(parts, blocks):
@@ -909,62 +963,57 @@
         slots,
     )
 
-    one = links.scatter(*last_blocks)
-    sent, got_one = next(one)
-    left = links.scatter(before_blocks[0], after(before_blocks[1], sent))
-    sent, got_left = next(left)
-    sent, got_one = one.send(sent)
-    right_grad, sums, blocks = backward_slots(
-        kept, after(last["mixed_grad_before"], sent), valid_column, back[0], layers[0], owner, slots
+    unpadded = lambda array: array[:, :slots].reshape(images * slots, width)
+    one = links.sum(*last_blocks)
+    left = links.sum(before_blocks[0], after(before_blocks[1], one.sent))
+    layer_out = unpadded(after(last["values"], left.sent))
+    sent = one.send((left.sent, layer_out))
+    sums = {"b_out": last_sums.pop("b_out_before"), "b_left": last_sums.pop("b_left_before")}
+    right_grad, blocks, packed = backward_slots(
+        kept,
+        after(last["mixed_grad_before"], sent),
+        valid_column,
+        back[0],
+        layers[0],
+        owner,
+        (sums, last_sums),
+        slots,
     )
-    sums["b_out"], sums["b_left"] = last_sums["b_out_before"], last_sums["b_left_before"]
-    right = links.scatter(*after(blocks, got_one, got_left))
-    sent, got_right = next(right)
-    sent, got_left = left.send(sent)
-    sent, got_one = one.send(sent)
-    small = links.total(pack_sums((sums, last_sums), slots))
-    sent_small, got_small = next(small)
-    input_grad, late = after(
-        backward_first(
-            values,
-            last["left_grad_before"],
-            right_grad,
-            after(last["upstream"], sent, sent_small),
-            layers[0],
-            owner,
-            pieces_one,
-            0,
-        ),
-        got_right,
-        got_left,
-        got_one,
-        got_small,
+    right = links.sum(*after(blocks, one.got, left.got))
+    small = links.total(*packed)
+    sent = next(small)
+    sent = left.send((sent, right.sent))
+    sent = one.send(sent)
+    sent = right.send(sent)
+    sent = small.send(sent)
+    input_grad, line = backward_first(
+        values, last["left_grad_before"], right_grad, after(last["upstream"], sent), layers[0], owner, pieces_one, 0, slots
     )
-    sent = input_grad
-    for turn in range(links.steps):
-        for chain, turns in ((right, 0), (left, 1), (one, 2)):
-            if turn + turns < links.steps:
-                sent, unused = chain.send(sent)
-        unused, sent_small = small.send(late if turn == 0 else sent)
-    small.send(None)
-    small_sent = small.send(None)
-    chains = [next(chain) for chain in (one, left, right)]
-    odd, *summed = small_sent
+    line = after(line, left.got, one.got, right.got)
+    sent = small.send(line)
+    both = left.join(right)
+    sent = both.send(sent)
+    for step in range(links.steps - 2):
+        sent = one.send(sent)
+        sent = small.send(sent)
+        sent = both.send(sent)
+    for unused in range(2):
+        small_end = small.send(sent)
+    odd, *summed = small_end
     steps = groups // 2
-    places = (
-        [(1, group) for group in range(groups + per)],
-        [(0, group) for group in range(steps)] + [(0, groups + part) for part in range(per)],
-        [(0, steps + group) for group in range(steps)],
-    )
-    in_grad, out_grad = links.finish(chains, places, groups, per)
+    spots = [(1, group) for group in range(groups + per)]
+    terms = dict(zip(spots, one.terms()))
+    spots = [(0, group) for group in range(steps)] + [(0, groups + part) for part in range(per)]
+    spots += [(0, steps + group) for group in range(steps)]
+    terms |= zip(spots, both.terms())
+    in_grad, out_grad = links.finish(terms, groups, per)
     gain_one, bias_one, b_in, gain_two, bias_two, spatial_grad, b_sp, b_out = unpack_sums(
         odd.reshape(1), *summed, slots, width
     )
 
-    unpadded = lambda array: array[:, :slots].reshape(images * slots, width)
     return (
-        unpadded(last["values"]),
-        unpadded(input_grad),
+        layer_out,
+        input_grad,
         gain_one,
         bias_one,
         in_grad,

time: 237 us -> 226 us (0.954)
  waiting for transfers between devices: 37.6 us -> 32.6 us
  starting transfers between devices: 44.9 us -> 42.3 us
    convert_element_type x18 -> x14, other arithmetic: 20.6 us -> 13.9 us  [the longest x8 11.9 us: send(): self.sent = self.add(slice(keep, 2 * keep)).astype(BF16)]
    ppermute x41 -> x39, waiting for transfers between devices: 37.6 us -> 32.6 us  [swap(): lax.ppermute(values, AXES, [(i, i ^ bits[i % 2]) for i in range(self.devi...]
    add x0 -> x5, other arithmetic: none -> 4.37 us  [the longest x4 4.36 us: add(): total[-1] = total[-1] + part[at].astype(F32)]
    ppermute x41 -> x39, starting transfers between devices: 44.9 us -> 42.3 us  [swap(): lax.ppermute(values, AXES, [(i, i ^ bits[i % 2]) for i in range(self.devi...]
    another operation x0 -> x2, other arithmetic: none -> 2.55 us
  transfers between devices with their start and end apart: 41 -> 39, of which waited for: 13 -> 12; matrix products, arithmetic and copies ran while one was open for 17% -> 18% of each run, Pallas kernels for 23% -> 23%
where the time goes in v3:
time: 226 us; the launch traced here: 225 us
  Pallas kernels  105 us (46%)
  starting transfers between devices  42.3 us (19%)
  waiting for transfers between devices  32.6 us (14%)
  other arithmetic  30.5 us (13%)
  local copies, waits for them, and re-layouts  12.8 us (6%)
    pallas_call x1, Pallas kernels, forward_backward(): call(kernel, 'forward_backward', (images,), [image(rows, width), whole(b_...  50 us
    ppermute x39, starting transfers between devices, swap(): lax.ppermute(values, AXES, [(i, i ^ bits[i % 2]) for i in range(self.devi...  42.3 us
    ppermute x39, waiting for transfers between devices, swap(): lax.ppermute(values, AXES, [(i, i ^ bits[i % 2]) for i in range(self.devi...  32.6 us
    pallas_call x2, Pallas kernels, forward_save(): call(kernel, 'forward_save', (count,), [some(width), whole((rows, 1)), so...  23.2 us
    pallas_call x1, Pallas kernels, backward_slots(): call(kernel, 'backward_slots', (images,), [image(rows, gate), image(rows,...  14.9 us
    pallas_call x1, Pallas kernels, backward_first(): call(kernel, 'backward_first', (images,), [image(rows, width), image(rows...  12.2 us
    convert_element_type x8, other arithmetic, send(): self.sent = self.add(slice(keep, 2 * keep)).astype(BF16)  11.9 us
  transfers between devices with their start and end apart: 39, of which 12 were waited for; matrix products, arithmetic and copies ran while one was open for 18% of the time, Pallas kernels for 23%

profile of v3, /device:TPU:0, one launch (start us, length us, event | category | flops | bytes accessed | tf_op | source)
XLA Modules:
  0.0 224.5 jit_solution(1166123752484985163)
XLA Ops:
  1.7 3.1 %collective-permute-start = (bf16[1,6,16,512]{3,2,1,0:T(8,128)(2,1)S(1)}, bf16[1,6,16,512]{3,2,1,0:T(8,128)(2,1)S(1)}, u32[]{:S(2)}, u32[]{:S(2)}) collective-permute-start(bf16[1,6,16,512]{3,2,1,0:T(8,128)(2,1)S(1)} %bitcast.58), channel_id=1, source_target_pairs={{0,8},{1,17},{2,10},{3,19},{4,12},{5,21},{6,14},{7,23},{8,0},{9,25... | collective-permute-start | bytes 294920 | tf_op jit(solution)/shard_map/ppermute | solution.py:689
  4.8 2.6 %collective-permute-start.1 = (bf16[1,6,16,512]{3,2,1,0:T(8,128)(2,1)S(1)}, bf16[1,6,16,512]{3,2,1,0:T(8,128)(2,1)S(1)}, u32[]{:S(2)}, u32[]{:S(2)}) collective-permute-start(bf16[1,6,16,512]{3,2,1,0:T(8,128)(2,1)S(1)} %bitcast.59), channel_id=1, source_target_pairs={{0,16},{1,9},{2,18},{3,11},{4,20},{5,13},{6,22},{7,15},{8,24},{9,1... | collective-permute-start | bytes 294920 | tf_op jit(solution)/shard_map/ppermute | solution.py:689
  7.4 1.4 fusion.54
  14.5 1.6 collective-permute-start.7
  16.4 1.7 collective-permute-start.3
  18.1 2.4 %collective-permute-start.4 = (bf16[1,12,16,512]{3,2,1,0:T(8,128)(2,1)S(1)}, bf16[1,12,16,512]{3,2,1,0:T(8,128)(2,1)S(1)}, u32[]{:S(2)}, u32[]{:S(2)}) collective-permute-start(bf16[1,12,16,512]{3,2,1,0:T(8,128)(2,1)S(1)} %pad_maximum_fusion.3), channel_id=1, source_target_pairs={{0,16},{1,9},{2,18},{3,11},{4,20},{5,13},{6,22},{7,15},{8,24},{9,1... | collective-permute-start | bytes 589832 | tf_op jit(solution)/shard_map/ppermute | solution.py:689
  21.1 1.6 collective-permute-start.8
  22.7 6.0 %collective-permute-done.3 = bf16[1,12,16,512]{3,2,1,0:T(8,128)(2,1)S(1)} collective-permute-done((bf16[1,12,16,512]{3,2,1,0:T(8,128)(2,1)S(1)}, bf16[1,12,16,512]{3,2,1,0:T(8,128)(2,1)S(1)}, u32[]{:S(2)}, u32[]{:S(2)}) %collective-permute-start.3) | collective-permute-done | bytes 196640 | tf_op jit(solution)/shard_map/ppermute | solution.py:689
  28.6 4.6 %collective-permute-done.4 = bf16[1,12,16,512]{3,2,1,0:T(8,128)(2,1)S(1)} collective-permute-done((bf16[1,12,16,512]{3,2,1,0:T(8,128)(2,1)S(1)}, bf16[1,12,16,512]{3,2,1,0:T(8,128)(2,1)S(1)}, u32[]{:S(2)}, u32[]{:S(2)}) %collective-permute-start.4) | collective-permute-done | bytes 196640 | tf_op jit(solution)/shard_map/ppermute | solution.py:689
  33.2 1.5 collective-permute-start.9
  39.1 2.1 collective-permute-done.9.refs_8_.refs_3_
  41.9 1.4 reshape.124
  43.3 1.1 pad.36.values_ref
  44.4 1.1 pad.37.cot_ref
  46.6 2.1 collective-permute-start.14
  49.3 10.3 %forward_save.2 = (bf16[5,208,1536]{2,1,0:T(8,128)(2,1)}, bf16[5,208,1536]{2,1,0:T(8,128)(2,1)}, bf16[5,208,1536]{2,1,0:T(8,128)(2,1)}, bf16[5,208,1536]{2,1,0:T...) custom-call(s32[32]{0:T(128)} %pad_add_fusion.owner_ref, ...), custom_call_target="tpu_custom_call" | custom-call | flops 4000000000 | bytes 20000000 | tf_op jit(solution)/shard_map/forward_save/pallas_call | solution.py:332
  60.9 12.9 %forward_save.3 = (bf16[5,208,1536]{2,1,0:T(8,128)(2,1)}, bf16[5,208,1536]{2,1,0:T(8,128)(2,1)}, bf16[5,208,1536]{2,1,0:T(8,128)(2,1)}, bf16[5,208,1536]{2,1,0:T...) custom-call(s32[32]{0:T(128)} %pad_add_fusion.owner_ref, ...), custom_call_target="tpu_custom_call", output_to_operand_aliasing={{0}: (18, {}), {1}: (19, {}), {2}: (20, {}), {3}: (21, {}),... | custom-call | flops 6000000000 | bytes 20000000 | tf_op jit(solution)/shard_map/forward_save/pallas_call | solution.py:332
  76.5 50.0 %forward_backward.1 = (bf16[5,208,512]{2,1,0:T(8,128)(2,1)}, f32[5,208,512]{2,1,0:T(8,128)}, bf16[5,208,1536]{2,1,0:T(8,128)(2,1)}, bf16[5,208,1536]{2,1,0:T(8,1...) custom-call(s32[32]{0:T(128)} %pad_add_fusion.owner_ref, ...), custom_call_target="tpu_custom_call" | custom-call | flops 40000000000 | bytes 20000000 | tf_op jit(solution)/shard_map/forward_backward/pallas_call | solution.py:458
  127.1 1.4 slice.196
  128.5 1.1 reshape.128
  129.6 1.8 collective-permute-done.20.refs_1_
  131.4 2.8 %add_convert_fusion = bf16[8,9,16,512]{3,2,1,0:T(8,128)(2,1)} fusion(bf16[16,9,16,512]{3,2,1,0:T(8,128)(2,1)} %collective-permute-done.20.refs_1_, bf16[16,9,16,512]{3,2,1,0:T(8,128)(2,1)S(1)} %copy-done), kind=kLoop, calls=%fused_computation | loop fusion | flops 2359296 | bytes 3538944 | tf_op jit(solution)/shard_map/convert_element_type | solution.py:768
  134.3 2.0 collective-permute-start.22
  136.3 14.9 %backward_slots.1 = (bf16[5,208,1536]{2,1,0:T(8,128)(2,1)}, bf16[16,3,16,512]{3,2,1,0:T(8,128)(2,1)}, bf16[16,3,16,512]{3,2,1,0:T(8,128)(2,1)}, bf16[48,1536]{1,0:T(8,128)(2,1)}, bf16[48,1536]{1,0:T(8,128)(2,1)}) custom-call(s32[32]{0:T(128)} %pad_add_fusion.owner_ref, bf16[5,208,1536]{2,1,0:T(8,128)(2,1)} %get-tuple-element.152.mixed_ref, ...), custom_call_target="tpu_custom_call" | custom-call | flops 8999999488 | bytes 20000000 | tf_op jit(solution)/shard_map/backward_slots/pallas_call | solution.py:540
  151.7 2.6 %add_convert_fusion.1 = bf16[8,6,16,512]{3,2,1,0:T(8,128)(2,1)} fusion(bf16[16,6,16,512]{3,2,1,0:T(8,128)(2,1)} %collective-permute-done.23.refs_7_, bf16[16,6,16,512]{3,2,1,0:T(8,128)(2,1)} %get-tuple-element.212.refs_6_), kind=kLoop, calls=%fused_computation.1 | loop fusion | flops 1572864 | bytes 2359296 | tf_op jit(solution)/shard_map/convert_element_type | solution.py:768
  154.4 1.5 collective-permute-start.27
  155.8 2.2 add_convert_fusion.2
  160.2 6.0 %collective-permute-start.25 = (bf16[48,1536]{1,0:T(8,128)(2,1)S(1)}, bf16[48,1536]{1,0:T(8,128)(2,1)}, u32[]{:S(2)}, u32[]{:S(2)}) collective-permute-start(bf16[48,1536]{1,0:T(8,128)(2,1)S(1)} %add_convert_fusion.12), channel_id=1, source_target_pairs={{0,16},{1,9},{2,18},{3,11},{4,20},{5,13},{6,22},{7,15},{8,24},{9,1... | collective-permute-start | bytes 442376 | tf_op jit(solution)/shard_map/ppermute | solution.py:689
  166.1 12.2 %backward_first.1 = (f32[980,512]{1,0:T(8,128)}, f32[8,1536]{1,0:T(8,128)}) custom-call(s32[32]{0:T(128)} %pad_add_fusion.owner_ref, bf16[5,208,512]{2,1,0:T(8,128)(2,1)} %pad.36.values_ref, bf16[5,208,1536]{2,1,0:T(8,128)(2,1)} %get-tuple-element.147.left_ref, bf16[5,208,1536]{2,1,0:T(8,128)(2,1)} %get-tuple-element.167.right_ref, ...), custom_call_target="tpu_custom_call" | custom-call | flops 6000000000 | bytes 20000000 | tf_op jit(solution)/shard_map/backward_first/pallas_call | solution.py:597
  179.3 3.6 %collective-permute-start.29 = (bf16[8,1536]{1,0:T(8,128)(2,1)S(1)}, bf16[8,1536]{1,0:T(8,128)(2,1)S(1)}, u32[]{:S(2)}, u32[]{:S(2)}) collective-permute-start(bf16[8,1536]{1,0:T(8,128)(2,1)S(1)} %convert_element_type.364), channel_id=1, source_target_pairs={{0,16},{1,9},{2,18},{3,11},{4,20},{5,13},{6,22},{7,15},{8,24},{9,1... | collective-permute-start | bytes 73736 | tf_op jit(solution)/shard_map/ppermute | solution.py:689
  182.8 1.4 add_convert_fusion.3
  184.3 1.1 add_convert_fusion.6
  185.5 1.5 collective-permute-start.32
  187.0 1.2 add_convert_fusion.5
  189.3 1.8 collective-permute-start.30
  191.1 4.3 %collective-permute-done.32.refs_9_ = bf16[4,9,16,512]{3,2,1,0:T(8,128)(2,1)S(1)} collective-permute-done((bf16[4,9,16,512]{3,2,1,0:T(8,128)(2,1)S(1)}, bf16[4,9,16,512]{3,2,1,0:T(8,128)(2,1)S(1)}, u32[]{:S(2)}, u32[]{:S(2)}) %collective-permute-start.32) | collective-permute-done | bytes 589856 | tf_op jit(solution)/shard_map/ppermute | solution.py:689
  195.4 1.4 convert_add_fusion
  198.0 1.6 collective-permute-done.31.refs_4_
  199.6 1.9 add_convert_fusion.10
  201.5 1.3 collective-permute-start.33
  202.8 5.1 %collective-permute-done.34.refs_10_ = bf16[2,9,16,512]{3,2,1,0:T(8,128)(2,1)S(1)} collective-permute-done((bf16[2,9,16,512]{3,2,1,0:T(8,128)(2,1)S(1)}, bf16[2,9,16,512]{3,2,1,0:T(8,128)(2,1)S(1)}, u32[]{:S(2)}, u32[]{:S(2)}) %collective-permute-start.34) | collective-permute-done | bytes 294944 | tf_op jit(solution)/shard_map/ppermute | solution.py:689
  207.9 1.1 convert_add_fusion.1
  210.9 2.0 collective-permute-start.38
  212.9 2.3 %collective-permute-done.35 = bf16[48,1536]{1,0:T(8,128)(2,1)S(1)} collective-permute-done((bf16[48,1536]{1,0:T(8,128)(2,1)S(1)}, bf16[48,1536]{1,0:T(8,128)(2,1)S(1)}, u32[]{:S(2)}, u32[]{:S(2)}) %collective-permute-start.35) | collective-permute-done | bytes 147488 | tf_op jit(solution)/shard_map/ppermute | solution.py:689
  215.4 1.8 collective-permute-done.37.refs_5_
  217.2 1.6 collective-permute-done.38.refs_11_
  219.4 2.5 %add_blocks.1 = (f32[2,16,3072]{2,1,0:T(8,128)}, f32[2,48,512]{2,1,0:T(8,128)}) custom-call(bf16[16,9,16,512]{3,2,1,0:T(8,128)(2,1)} %get-tuple-element.206.refs_0_, bf16[16,9,16,512]{3,2,1,0:T(8,128)(2,1)} %collective-permute-done.20.refs_1_, bf16[8,9,16,512]{3,2,1,0:T(8,128)(2,1)} %copy-done.1, bf16[4,9,16,512]{3,2,1,0:T(8,128)(2,1)} %collective-permute-done.26.refs_3_, ...), custom_call_target="tpu_custom_call" | custom-call | tf_op jit(solution)/shard_map/add_blocks/pallas_call | solution.py:669
  222.6 2.0 unpack_sums.1
  (180 shorter events, 27.9 us)
Async XLA Ops:
  1.7 7.7 %copy-start.24 = (f32[2,1536]{1,0:T(2,128)S(1)}, f32[2,1536]{1,0:T(2,128)}, u32[]{:S(2)}) copy-start(f32[2,1536]{1,0:T(2,128)} %param.24) | copy-start | bytes 36868
  1.7 9.2 %copy-start.23 = (f32[2,3072]{1,0:T(2,128)S(1)}, f32[2,3072]{1,0:T(2,128)}, u32[]{:S(2)}) copy-start(f32[2,3072]{1,0:T(2,128)} %param.22) | copy-start | bytes 73732
  1.7 12.3 %collective-permute-start = (bf16[1,6,16,512]{3,2,1,0:T(8,128)(2,1)S(1)}, bf16[1,6,16,512]{3,2,1,0:T(8,128)(2,1)S(1)}, u32[]{:S(2)}, u32[]{:S(2)}) collective-permute-start(bf16[1,6,16,512]{3,2,1,0:T(8,128)(2,1)S(1)} %bitcast.58), channel_id=1, source_target_pairs={{0,8},{1,17},{2,10},{3,19},{4,12},{5,21},{6,14},{7,23},{8,0},{9,25... | collective-permute-start | bytes 294920 | tf_op jit(solution)/shard_map/ppermute | solution.py:689
  4.8 9.6 %collective-permute-start.1 = (bf16[1,6,16,512]{3,2,1,0:T(8,128)(2,1)S(1)}, bf16[1,6,16,512]{3,2,1,0:T(8,128)(2,1)S(1)}, u32[]{:S(2)}, u32[]{:S(2)}) collective-permute-start(bf16[1,6,16,512]{3,2,1,0:T(8,128)(2,1)S(1)} %bitcast.59), channel_id=1, source_target_pairs={{0,16},{1,9},{2,18},{3,11},{4,20},{5,13},{6,22},{7,15},{8,24},{9,1... | collective-permute-start | bytes 294920 | tf_op jit(solution)/shard_map/ppermute | solution.py:689
  7.4 7.0 %collective-permute-start.2 = (bf16[1,6,16,512]{3,2,1,0:T(8,128)(2,1)S(1)}, bf16[1,6,16,512]{3,2,1,0:T(8,128)(2,1)S(1)}, u32[]{:S(2)}, u32[]{:S(2)}) collective-permute-start(bf16[1,6,16,512]{3,2,1,0:T(8,128)(2,1)S(1)} %bitcast.60), channel_id=1, source_target_pairs={{0,24},{1,25},{2,26},{3,27},{4,28},{5,29},{6,30},{7,31},{8,16},{9,... | collective-permute-start | bytes 294920 | tf_op jit(solution)/shard_map/ppermute | solution.py:689
  14.4 23.5 %copy-start.5 = (bf16[4,6,16,512]{3,2,1,0:T(8,128)(2,1)}, bf16[4,6,16,512]{3,2,1,0:T(8,128)(2,1)S(1)}, u32[]{:S(2)}) copy-start(bf16[4,6,16,512]{3,2,1,0:T(8,128)(2,1)S(1)} %pad_maximum_fusion.2.refs_5_.refs_0_) | copy-start | bytes 1179652
  14.5 18.7 %collective-permute-start.7 = (bf16[4,6,16,512]{3,2,1,0:T(8,128)(2,1)S(1)}, bf16[4,6,16,512]{3,2,1,0:T(8,128)(2,1)S(1)}, u32[]{:S(2)}, u32[]{:S(2)}) collective-permute-start(bf16[4,6,16,512]{3,2,1,0:T(8,128)(2,1)S(1)} %pad_maximum_fusion.2.refs_5_.refs_0_), channel_id=1, source_target_pairs={{0,2},{1,5},{2,0},{3,7},{4,6},{5,1},{6,4},{7,3},{8,10},{9,13},{10,... | collective-permute-start | bytes 1179656 | tf_op jit(solution)/shard_map/ppermute | solution.py:689
  16.4 12.2 %collective-permute-start.3 = (bf16[1,12,16,512]{3,2,1,0:T(8,128)(2,1)S(1)}, bf16[1,12,16,512]{3,2,1,0:T(8,128)(2,1)S(1)}, u32[]{:S(2)}, u32[]{:S(2)}) collective-permute-start(bf16[1,12,16,512]{3,2,1,0:T(8,128)(2,1)S(1)} %pad_maximum_fusion.3), channel_id=1, source_target_pairs={{0,8},{1,17},{2,10},{3,19},{4,12},{5,21},{6,14},{7,23},{8,0},{9,25... | collective-permute-start | bytes 589832 | tf_op jit(solution)/shard_map/ppermute | solution.py:689
  18.1 15.1 %collective-permute-start.4 = (bf16[1,12,16,512]{3,2,1,0:T(8,128)(2,1)S(1)}, bf16[1,12,16,512]{3,2,1,0:T(8,128)(2,1)S(1)}, u32[]{:S(2)}, u32[]{:S(2)}) collective-permute-start(bf16[1,12,16,512]{3,2,1,0:T(8,128)(2,1)S(1)} %pad_maximum_fusion.3), channel_id=1, source_target_pairs={{0,16},{1,9},{2,18},{3,11},{4,20},{5,13},{6,22},{7,15},{8,24},{9,1... | collective-permute-start | bytes 589832 | tf_op jit(solution)/shard_map/ppermute | solution.py:689
  20.5 12.7 %collective-permute-start.5 = (bf16[1,12,16,512]{3,2,1,0:T(8,128)(2,1)S(1)}, bf16[1,12,16,512]{3,2,1,0:T(8,128)(2,1)S(1)}, u32[]{:S(2)}, u32[]{:S(2)}) collective-permute-start(bf16[1,12,16,512]{3,2,1,0:T(8,128)(2,1)S(1)} %pad_maximum_fusion.3), channel_id=1, source_target_pairs={{0,24},{1,25},{2,26},{3,27},{4,28},{5,29},{6,30},{7,31},{8,16},{9,... | collective-permute-start | bytes 589832 | tf_op jit(solution)/shard_map/ppermute | solution.py:689
  21.1 17.6 %collective-permute-start.8 = (bf16[4,6,16,512]{3,2,1,0:T(8,128)(2,1)S(1)}, bf16[4,6,16,512]{3,2,1,0:T(8,128)(2,1)}, u32[]{:S(2)}, u32[]{:S(2)}) collective-permute-start(bf16[4,6,16,512]{3,2,1,0:T(8,128)(2,1)S(1)} %pad_maximum_fusion.2.refs_5_.refs_0_), channel_id=1, source_target_pairs={{0,4},{1,3},{2,6},{3,1},{4,0},{5,7},{6,2},{7,5},{8,12},{9,11},{10,... | collective-permute-start | bytes 1179656 | tf_op jit(solution)/shard_map/ppermute | solution.py:689
  33.2 7.9 %collective-permute-start.9 = (bf16[4,6,16,512]{3,2,1,0:T(8,128)(2,1)S(1)}, bf16[4,6,16,512]{3,2,1,0:T(8,128)(2,1)}, u32[]{:S(2)}, u32[]{:S(2)}) collective-permute-start(bf16[4,6,16,512]{3,2,1,0:T(8,128)(2,1)S(1)} %collective-permute-done.7.refs_6_.refs_1_), channel_id=1, source_target_pairs={{0,4},{1,3},{2,6},{3,1},{4,0},{5,7},{6,2},{7,5},{8,12},{9,11},{10,... | collective-permute-start | bytes 1179656 | tf_op jit(solution)/shard_map/ppermute | solution.py:689
  36.4 10.2 %collective-permute-start.10 = (bf16[4,6,16,512]{3,2,1,0:T(8,128)(2,1)S(1)}, bf16[4,6,16,512]{3,2,1,0:T(8,128)(2,1)}, u32[]{:S(2)}, u32[]{:S(2)}) collective-permute-start(bf16[4,6,16,512]{3,2,1,0:T(8,128)(2,1)S(1)} %pad_maximum_fusion.2.refs_5_.refs_0_), channel_id=1, source_target_pairs={{0,1},{1,0},{2,3},{3,2},{4,5},{5,4},{6,7},{7,6},{8,9},{9,8},{10,11... | collective-permute-start | bytes 1179656 | tf_op jit(solution)/shard_map/ppermute | solution.py:689
  38.0 21.6 %collective-permute-start.6 = (bf16[4,12,16,512]{3,2,1,0:T(8,128)(2,1)}, bf16[4,12,16,512]{3,2,1,0:T(8,128)(2,1)}, u32[]{:S(2)}, u32[]{:S(2)}) collective-permute-start(bf16[4,12,16,512]{3,2,1,0:T(8,128)(2,1)} %pad_maximum_fusion.refs_9_), channel_id=1, source_target_pairs={{0,2},{1,5},{2,0},{3,7},{4,6},{5,1},{6,4},{7,3},{8,10},{9,13},{10,... | collective-permute-start | bytes 2359304 | tf_op jit(solution)/shard_map/ppermute | solution.py:689
  38.5 10.7 %collective-permute-start.11 = (bf16[4,6,16,512]{3,2,1,0:T(8,128)(2,1)S(1)}, bf16[4,6,16,512]{3,2,1,0:T(8,128)(2,1)}, u32[]{:S(2)}, u32[]{:S(2)}) collective-permute-start(bf16[4,6,16,512]{3,2,1,0:T(8,128)(2,1)S(1)} %collective-permute-done.7.refs_6_.refs_1_), channel_id=1, source_target_pairs={{0,1},{1,0},{2,3},{3,2},{4,5},{5,4},{6,7},{7,6},{8,9},{9,8},{10,11... | collective-permute-start | bytes 1179656 | tf_op jit(solution)/shard_map/ppermute | solution.py:689
  38.7 10.5 %collective-permute-start.12 = (bf16[4,6,16,512]{3,2,1,0:T(8,128)(2,1)}, bf16[4,6,16,512]{3,2,1,0:T(8,128)(2,1)}, u32[]{:S(2)}, u32[]{:S(2)}) collective-permute-start(bf16[4,6,16,512]{3,2,1,0:T(8,128)(2,1)} %collective-permute-done.8.refs_7_.refs_2_), channel_id=1, source_target_pairs={{0,1},{1,0},{2,3},{3,2},{4,5},{5,4},{6,7},{7,6},{8,9},{9,8},{10,11... | collective-permute-start | bytes 1179656 | tf_op jit(solution)/shard_map/ppermute | solution.py:689
  41.1 8.1 %collective-permute-start.13 = (bf16[4,6,16,512]{3,2,1,0:T(8,128)(2,1)}, bf16[4,6,16,512]{3,2,1,0:T(8,128)(2,1)}, u32[]{:S(2)}, u32[]{:S(2)}) collective-permute-start(bf16[4,6,16,512]{3,2,1,0:T(8,128)(2,1)} %collective-permute-done.9.refs_8_.refs_3_), channel_id=1, source_target_pairs={{0,1},{1,0},{2,3},{3,2},{4,5},{5,4},{6,7},{7,6},{8,9},{9,8},{10,11... | collective-permute-start | bytes 1179656 | tf_op jit(solution)/shard_map/ppermute | solution.py:689
  46.6 14.2 %collective-permute-start.14 = (bf16[4,12,16,512]{3,2,1,0:T(8,128)(2,1)}, bf16[4,12,16,512]{3,2,1,0:T(8,128)(2,1)S(1)}, u32[]{:S(2)}, u32[]{:S(2)}) collective-permute-start(bf16[4,12,16,512]{3,2,1,0:T(8,128)(2,1)} %pad_maximum_fusion.refs_9_), channel_id=1, source_target_pairs={{0,4},{1,3},{2,6},{3,1},{4,0},{5,7},{6,2},{7,5},{8,12},{9,11},{10,... | collective-permute-start | bytes 2359304 | tf_op jit(solution)/shard_map/ppermute | solution.py:689
  59.6 14.2 %collective-permute-start.15 = (bf16[4,12,16,512]{3,2,1,0:T(8,128)(2,1)}, bf16[4,12,16,512]{3,2,1,0:T(8,128)(2,1)S(1)}, u32[]{:S(2)}, u32[]{:S(2)}) collective-permute-start(bf16[4,12,16,512]{3,2,1,0:T(8,128)(2,1)} %collective-permute-done.6.refs_10_), channel_id=1, source_target_pairs={{0,4},{1,3},{2,6},{3,1},{4,0},{5,7},{6,2},{7,5},{8,12},{9,11},{10,... | collective-permute-start | bytes 2359304 | tf_op jit(solution)/shard_map/ppermute | solution.py:689
  60.3 15.1 %collective-permute-start.16 = (bf16[4,12,16,512]{3,2,1,0:T(8,128)(2,1)}, bf16[4,12,16,512]{3,2,1,0:T(8,128)(2,1)S(1)}, u32[]{:S(2)}, u32[]{:S(2)}) collective-permute-start(bf16[4,12,16,512]{3,2,1,0:T(8,128)(2,1)} %pad_maximum_fusion.refs_9_), channel_id=1, source_target_pairs={{0,1},{1,0},{2,3},{3,2},{4,5},{5,4},{6,7},{7,6},{8,9},{9,8},{10,11... | collective-permute-start | bytes 2359304 | tf_op jit(solution)/shard_map/ppermute | solution.py:689
  60.3 15.1 %collective-permute-start.17 = (bf16[4,12,16,512]{3,2,1,0:T(8,128)(2,1)}, bf16[4,12,16,512]{3,2,1,0:T(8,128)(2,1)S(1)}, u32[]{:S(2)}, u32[]{:S(2)}) collective-permute-start(bf16[4,12,16,512]{3,2,1,0:T(8,128)(2,1)} %collective-permute-done.6.refs_10_), channel_id=1, source_target_pairs={{0,1},{1,0},{2,3},{3,2},{4,5},{5,4},{6,7},{7,6},{8,9},{9,8},{10,11... | collective-permute-start | bytes 2359304 | tf_op jit(solution)/shard_map/ppermute | solution.py:689
  60.8 13.0 %copy-start.32 = (bf16[4,12,16,512]{3,2,1,0:T(8,128)(2,1)}, bf16[4,12,16,512]{3,2,1,0:T(8,128)(2,1)S(1)}, u32[]{:S(2)}) copy-start(bf16[4,12,16,512]{3,2,1,0:T(8,128)(2,1)S(1)} %collective-permute-done.14.refs_11_) | copy-start | bytes 2359300
  60.8 14.6 %collective-permute-start.18 = (bf16[4,12,16,512]{3,2,1,0:T(8,128)(2,1)S(1)}, bf16[4,12,16,512]{3,2,1,0:T(8,128)(2,1)}, u32[]{:S(2)}, u32[]{:S(2)}) collective-permute-start(bf16[4,12,16,512]{3,2,1,0:T(8,128)(2,1)S(1)} %collective-permute-done.14.refs_11_), channel_id=1, source_target_pairs={{0,1},{1,0},{2,3},{3,2},{4,5},{5,4},{6,7},{7,6},{8,9},{9,8},{10,11... | collective-permute-start | bytes 2359304 | tf_op jit(solution)/shard_map/ppermute | solution.py:689
  60.9 13.4 %copy-start.18 = (f32[5,208,1]{1,0,2:T(8,128)S(1)}, f32[5,208,1]{1,0,2:T(8,128)}, u32[]{:S(2)}) copy-start(f32[5,208,1]{1,0,2:T(8,128)} %pad_bitcast_fusion) | copy-start | bytes 12484
  73.8 2.5 %collective-permute-start.19 = (bf16[4,12,16,512]{3,2,1,0:T(8,128)(2,1)S(1)}, bf16[4,12,16,512]{3,2,1,0:T(8,128)(2,1)}, u32[]{:S(2)}, u32[]{:S(2)}) collective-permute-start(bf16[4,12,16,512]{3,2,1,0:T(8,128)(2,1)S(1)} %collective-permute-done.15.refs_12_), channel_id=1, source_target_pairs={{0,1},{1,0},{2,3},{3,2},{4,5},{5,4},{6,7},{7,6},{8,9},{9,8},{10,11... | collective-permute-start | bytes 2359304 | tf_op jit(solution)/shard_map/ppermute | solution.py:689
  126.5 4.9 %collective-permute-start.20 = (bf16[16,9,16,512]{3,2,1,0:T(8,128)(2,1)}, bf16[16,9,16,512]{3,2,1,0:T(8,128)(2,1)}, u32[]{:S(2)}, u32[]{:S(2)}) collective-permute-start(bf16[16,9,16,512]{3,2,1,0:T(8,128)(2,1)} %get-tuple-element.144), channel_id=1, source_target_pairs={{0,1},{1,0},{2,3},{3,2},{4,5},{5,4},{6,7},{7,6},{8,9},{9,8},{10,11... | collective-permute-start | bytes 7077896 | tf_op jit(solution)/shard_map/ppermute | solution.py:689
  126.9 24.3 %collective-permute-start.23 = (bf16[16,6,16,512]{3,2,1,0:T(8,128)(2,1)}, bf16[16,6,16,512]{3,2,1,0:T(8,128)(2,1)}, u32[]{:S(2)}, u32[]{:S(2)}) collective-permute-start(bf16[16,6,16,512]{3,2,1,0:T(8,128)(2,1)} %get-tuple-element.145), channel_id=1, source_target_pairs={{0,1},{1,0},{2,3},{3,2},{4,5},{5,4},{6,7},{7,6},{8,9},{9,8},{10,11... | collective-permute-start | bytes 4718600 | tf_op jit(solution)/shard_map/ppermute | solution.py:689
  134.3 16.9 %collective-permute-start.22 = (bf16[8,9,16,512]{3,2,1,0:T(8,128)(2,1)}, bf16[8,9,16,512]{3,2,1,0:T(8,128)(2,1)S(1)}, u32[]{:S(2)}, u32[]{:S(2)}) collective-permute-start(bf16[8,9,16,512]{3,2,1,0:T(8,128)(2,1)} %add_convert_fusion), channel_id=1, source_target_pairs={{0,4},{1,3},{2,6},{3,1},{4,0},{5,7},{6,2},{7,5},{8,12},{9,11},{10,... | collective-permute-start | bytes 3538952 | tf_op jit(solution)/shard_map/ppermute | solution.py:689
  151.2 48.4 %copy-start.1 = (bf16[8,9,16,512]{3,2,1,0:T(8,128)(2,1)}, bf16[8,9,16,512]{3,2,1,0:T(8,128)(2,1)S(1)}, u32[]{:S(2)}) copy-start(bf16[8,9,16,512]{3,2,1,0:T(8,128)(2,1)S(1)} %collective-permute-done.22.refs_2_) | copy-start | bytes 3538948
  151.2 7.4 %collective-permute-start.24 = (bf16[16,3,16,512]{3,2,1,0:T(8,128)(2,1)}, bf16[16,3,16,512]{3,2,1,0:T(8,128)(2,1)S(1)}, u32[]{:S(2)}, u32[]{:S(2)}) collective-permute-start(bf16[16,3,16,512]{3,2,1,0:T(8,128)(2,1)} %get-tuple-element.174), channel_id=1, source_target_pairs={{0,1},{1,0},{2,3},{3,2},{4,5},{5,4},{6,7},{7,6},{8,9},{9,8},{10,11... | collective-permute-start | bytes 2359304 | tf_op jit(solution)/shard_map/ppermute | solution.py:689
  151.3 8.9 %collective-permute-start.21 = (bf16[48,1536]{1,0:T(8,128)(2,1)}, bf16[48,1536]{1,0:T(8,128)(2,1)S(1)}, u32[]{:S(2)}, u32[]{:S(2)}) collective-permute-start(bf16[48,1536]{1,0:T(8,128)(2,1)} %get-tuple-element.170), channel_id=1, source_target_pairs={{0,1},{1,0},{2,3},{3,2},{4,5},{5,4},{6,7},{7,6},{8,9},{9,8},{10,11... | collective-permute-start | bytes 442376 | tf_op jit(solution)/shard_map/ppermute | solution.py:689
  154.4 24.0 %collective-permute-start.27 = (bf16[8,6,16,512]{3,2,1,0:T(8,128)(2,1)}, bf16[8,6,16,512]{3,2,1,0:T(8,128)(2,1)}, u32[]{:S(2)}, u32[]{:S(2)}) collective-permute-start(bf16[8,6,16,512]{3,2,1,0:T(8,128)(2,1)} %add_convert_fusion.1), channel_id=1, source_target_pairs={{0,4},{1,3},{2,6},{3,1},{4,0},{5,7},{6,2},{7,5},{8,12},{9,11},{10,... | collective-permute-start | bytes 2359304 | tf_op jit(solution)/shard_map/ppermute | solution.py:689
  158.0 20.3 %collective-permute-start.26 = (bf16[4,9,16,512]{3,2,1,0:T(8,128)(2,1)}, bf16[4,9,16,512]{3,2,1,0:T(8,128)(2,1)}, u32[]{:S(2)}, u32[]{:S(2)}) collective-permute-start(bf16[4,9,16,512]{3,2,1,0:T(8,128)(2,1)} %add_convert_fusion.2), channel_id=1, source_target_pairs={{0,2},{1,5},{2,0},{3,7},{4,6},{5,1},{6,4},{7,3},{8,10},{9,13},{10,... | collective-permute-start | bytes 1769480 | tf_op jit(solution)/shard_map/ppermute | solution.py:689
  159.6 18.8 %collective-permute-start.28 = (bf16[8,3,16,512]{3,2,1,0:T(8,128)(2,1)}, bf16[8,3,16,512]{3,2,1,0:T(8,128)(2,1)S(1)}, u32[]{:S(2)}, u32[]{:S(2)}) collective-permute-start(bf16[8,3,16,512]{3,2,1,0:T(8,128)(2,1)} %add_convert_fusion.4), channel_id=1, source_target_pairs={{0,4},{1,3},{2,6},{3,1},{4,0},{5,7},{6,2},{7,5},{8,12},{9,11},{10,... | collective-permute-start | bytes 1179656 | tf_op jit(solution)/shard_map/ppermute | solution.py:689
  160.2 28.2 %collective-permute-start.25 = (bf16[48,1536]{1,0:T(8,128)(2,1)S(1)}, bf16[48,1536]{1,0:T(8,128)(2,1)}, u32[]{:S(2)}, u32[]{:S(2)}) collective-permute-start(bf16[48,1536]{1,0:T(8,128)(2,1)S(1)} %add_convert_fusion.12), channel_id=1, source_target_pairs={{0,16},{1,9},{2,18},{3,11},{4,20},{5,13},{6,22},{7,15},{8,24},{9,1... | collective-permute-start | bytes 442376 | tf_op jit(solution)/shard_map/ppermute | solution.py:689
  178.4 30.6 %copy-start.6 = (bf16[8,3,16,512]{3,2,1,0:T(8,128)(2,1)}, bf16[8,3,16,512]{3,2,1,0:T(8,128)(2,1)S(1)}, u32[]{:S(2)}) copy-start(bf16[8,3,16,512]{3,2,1,0:T(8,128)(2,1)S(1)} %collective-permute-done.28.refs_14_) | copy-start | bytes 1179652
  179.3 9.1 %collective-permute-start.29 = (bf16[8,1536]{1,0:T(8,128)(2,1)S(1)}, bf16[8,1536]{1,0:T(8,128)(2,1)S(1)}, u32[]{:S(2)}, u32[]{:S(2)}) collective-permute-start(bf16[8,1536]{1,0:T(8,128)(2,1)S(1)} %convert_element_type.364), channel_id=1, source_target_pairs={{0,16},{1,9},{2,18},{3,11},{4,20},{5,13},{6,22},{7,15},{8,24},{9,1... | collective-permute-start | bytes 73736 | tf_op jit(solution)/shard_map/ppermute | solution.py:689
  185.5 9.9 %collective-permute-start.32 = (bf16[4,9,16,512]{3,2,1,0:T(8,128)(2,1)S(1)}, bf16[4,9,16,512]{3,2,1,0:T(8,128)(2,1)S(1)}, u32[]{:S(2)}, u32[]{:S(2)}) collective-permute-start(bf16[4,9,16,512]{3,2,1,0:T(8,128)(2,1)S(1)} %pad_maximum_fusion.1), channel_id=1, source_target_pairs={{0,2},{1,5},{2,0},{3,7},{4,6},{5,1},{6,4},{7,3},{8,10},{9,13},{10,... | collective-permute-start | bytes 1769480 | tf_op jit(solution)/shard_map/ppermute | solution.py:689
  188.3 11.3 %collective-permute-start.31 = (bf16[2,9,16,512]{3,2,1,0:T(8,128)(2,1)S(1)}, bf16[2,9,16,512]{3,2,1,0:T(8,128)(2,1)S(1)}, u32[]{:S(2)}, u32[]{:S(2)}) collective-permute-start(bf16[2,9,16,512]{3,2,1,0:T(8,128)(2,1)S(1)} %add_convert_fusion.5), channel_id=1, source_target_pairs={{0,16},{1,9},{2,18},{3,11},{4,20},{5,13},{6,22},{7,15},{8,24},{9,1... | collective-permute-start | bytes 884744 | tf_op jit(solution)/shard_map/ppermute | solution.py:689
  189.3 12.1 %collective-permute-start.30 = (bf16[48,1536]{1,0:T(8,128)(2,1)S(1)}, bf16[48,1536]{1,0:T(8,128)(2,1)S(1)}, u32[]{:S(2)}, u32[]{:S(2)}) collective-permute-start(bf16[48,1536]{1,0:T(8,128)(2,1)S(1)} %add_convert_fusion.11), channel_id=1, source_target_pairs={{0,8},{1,17},{2,10},{3,19},{4,12},{5,21},{6,14},{7,23},{8,0},{9,25... | collective-permute-start | bytes 442376 | tf_op jit(solution)/shard_map/ppermute | solution.py:689
  195.4 14.4 %copy-start.4 = (bf16[4,9,16,512]{3,2,1,0:T(8,128)(2,1)}, bf16[4,9,16,512]{3,2,1,0:T(8,128)(2,1)S(1)}, u32[]{:S(2)}) copy-start(bf16[4,9,16,512]{3,2,1,0:T(8,128)(2,1)S(1)} %collective-permute-done.32.refs_9_) | copy-start | bytes 1769476
  197.9 10.0 %collective-permute-start.34 = (bf16[2,9,16,512]{3,2,1,0:T(8,128)(2,1)S(1)}, bf16[2,9,16,512]{3,2,1,0:T(8,128)(2,1)S(1)}, u32[]{:S(2)}, u32[]{:S(2)}) collective-permute-start(bf16[2,9,16,512]{3,2,1,0:T(8,128)(2,1)S(1)} %fusion.12), channel_id=1, source_target_pairs={{0,16},{1,9},{2,18},{3,11},{4,20},{5,13},{6,22},{7,15},{8,24},{9,1... | collective-permute-start | bytes 884744 | tf_op jit(solution)/shard_map/ppermute | solution.py:689
  199.6 10.4 %copy-start.8 = (bf16[2,9,16,512]{3,2,1,0:T(8,128)(2,1)}, bf16[2,9,16,512]{3,2,1,0:T(8,128)(2,1)S(1)}, u32[]{:S(2)}) copy-start(bf16[2,9,16,512]{3,2,1,0:T(8,128)(2,1)S(1)} %collective-permute-done.31.refs_4_) | copy-start | bytes 884740
  201.5 8.5 %collective-permute-start.33 = (bf16[48,1536]{1,0:T(8,128)(2,1)S(1)}, bf16[48,1536]{1,0:T(8,128)(2,1)S(1)}, u32[]{:S(2)}, u32[]{:S(2)}) collective-permute-start(bf16[48,1536]{1,0:T(8,128)(2,1)S(1)} %add_convert_fusion.9), channel_id=1, source_target_pairs={{0,2},{1,5},{2,0},{3,7},{4,6},{5,1},{6,4},{7,3},{8,10},{9,13},{10,... | collective-permute-start | bytes 442376 | tf_op jit(solution)/shard_map/ppermute | solution.py:689
  210.0 5.2 %collective-permute-start.35 = (bf16[48,1536]{1,0:T(8,128)(2,1)S(1)}, bf16[48,1536]{1,0:T(8,128)(2,1)S(1)}, u32[]{:S(2)}, u32[]{:S(2)}) collective-permute-start(bf16[48,1536]{1,0:T(8,128)(2,1)S(1)} %add_convert_fusion.8), channel_id=1, source_target_pairs={{0,4},{1,3},{2,6},{3,1},{4,0},{5,7},{6,2},{7,5},{8,12},{9,11},{10,... | collective-permute-start | bytes 442376 | tf_op jit(solution)/shard_map/ppermute | solution.py:689
  210.9 6.3 %collective-permute-start.37 = (bf16[1,9,16,512]{3,2,1,0:T(8,128)(2,1)}, bf16[1,9,16,512]{3,2,1,0:T(8,128)(2,1)S(1)}, u32[]{:S(2)}, u32[]{:S(2)}) collective-permute-start(bf16[1,9,16,512]{3,2,1,0:T(8,128)(2,1)} %add_convert_fusion.10), channel_id=1, source_target_pairs={{0,8},{1,17},{2,10},{3,19},{4,12},{5,21},{6,14},{7,23},{8,0},{9,25... | collective-permute-start | bytes 442376 | tf_op jit(solution)/shard_map/ppermute | solution.py:689
  210.9 7.9 %collective-permute-start.38 = (bf16[1,9,16,512]{3,2,1,0:T(8,128)(2,1)S(1)}, bf16[1,9,16,512]{3,2,1,0:T(8,128)(2,1)S(1)}, u32[]{:S(2)}, u32[]{:S(2)}) collective-permute-start(bf16[1,9,16,512]{3,2,1,0:T(8,128)(2,1)S(1)} %fusion.30), channel_id=1, source_target_pairs={{0,8},{1,17},{2,10},{3,19},{4,12},{5,21},{6,14},{7,23},{8,0},{9,25... | collective-permute-start | bytes 442376 | tf_op jit(solution)/shard_map/ppermute | solution.py:689
  215.3 6.7 %collective-permute-start.36 = (bf16[48,1536]{1,0:T(8,128)(2,1)S(1)}, bf16[48,1536]{1,0:T(8,128)(2,1)S(1)}, u32[]{:S(2)}, u32[]{:S(2)}) collective-permute-start(bf16[48,1536]{1,0:T(8,128)(2,1)S(1)} %add_convert_fusion.7.mine_ref), channel_id=1, source_target_pairs={{0,1},{1,0},{2,3},{3,2},{4,5},{5,4},{6,7},{7,6},{8,9},{9,8},{10,11... | collective-permute-start | bytes 442376 | tf_op jit(solution)/shard_map/ppermute | solution.py:689
  (27 other events, 99.5 us)

commit v4 on v3

--- a/solution.py
+++ b/solution.py
@@ -187,15 +187,17 @@
     for unused, ref in places:
         pltpu.make_async_copy(ref, ref, sem).wait()
 
-
 def put_weight_grads(owner, jobs, result, stage, outs, sem):
     half = stage.shape[1]
+    spots = [(0, 0, outs[0])] + [(1, at * outs[1].shape[0], out) for at, out in enumerate(outs[1:])]
 
     def send(group, rows):
         for side in range(2):
             for at in range(half):
                 stage[side, at, group] = result[rows(owner[side * half + at])]
-            pltpu.make_async_copy(stage.at[side, :, group], outs[side].at[:, group], sem).start()
+        for side, first, out in spots:
+            part = stage.at[side, first : first + out.shape[0], group]
+            pltpu.make_async_copy(part, out.at[:, group], sem).start()
 
     for left, right, place in jobs:
         if left.shape[1] > right.shape[1]:
@@ -211,8 +213,8 @@
                 columns = slice(group * GROUP, (group + 1) * GROUP)
                 result[: left.shape[1]] = dot_first(left[...], right[:, columns]).astype(BF16)
                 send(place + group, lambda block: pl.ds(pl.multiple_of(block * BLOCK, BLOCK), BLOCK))
-    for side in range(2):
-        pltpu.make_async_copy(stage.at[side], outs[side], sem).wait()
+    for side, first, out in spots:
+        pltpu.make_async_copy(stage.at[side, first : first + out.shape[0]], out, sem).wait()
 
 
 def put_sums(both, slots, outs, odd):
@@ -393,8 +395,8 @@
         rest = refs[n_w + n_p :]
         out = {name: ref.at[0] for name, ref in zip(outs, rest)}
         sums = dict(zip(shapes, rest[n_o:]))
-        last_outs, before_outs = rest[n_o + n_s :][:2], rest[n_o + n_s + 2 :][:2]
-        rest = rest[n_o + n_s + 4 :]
+        last_outs, before_outs = rest[n_o + n_s :][:3], rest[n_o + n_s + 3 :][:2]
+        rest = rest[n_o + n_s + 5 :]
         kept = dict(zip(image_scratch, rest))
         rest = rest[len(image_scratch) :]
         every = dict(zip(all_scratch, rest))
@@ -466,11 +468,12 @@
         + anywhere(n_p),
         [((images, rows, columns), dtype) for columns, dtype in outs.values()]
         + [(shape, F32) for shape in shapes.values()]
-        + [(last_shape, BF16)] * 2
+        + [(last_shape, BF16)]
+        + [((half // 2, *last_shape[1:]), BF16)] * 2
         + [(before_shape, BF16)] * 2,
         [image(rows, columns) for columns, unused in outs.values()]
         + [whole(shape) for shape in shapes.values()]
-        + anywhere(4),
+        + anywhere(5),
         [pltpu.VMEM((rows, gate), dtype) for dtype in image_scratch.values()]
         + [pltpu.VMEM((images * rows, columns), BF16) for columns in all_scratch.values()]
         + [out_scratch(width, hidden), in_scratch(width, hidden), out_scratch(width, hidden)]
@@ -494,7 +497,7 @@
         *pieces,
     )
     blocks = results[n_o + n_s :]
-    return dict(zip(outs, results)), dict(zip(shapes, results[n_o:])), blocks[:2], blocks[2:]
+    return dict(zip(outs, results)), dict(zip(shapes, results[n_o:])), blocks[:3], blocks[3:]
 
 
 def backward_slots(kept, mixed_grad, valid, mixer_back, w, owner, both, slots):
@@ -716,8 +719,8 @@
         last = after(last, wait)
         yield [*pieces, last, *others, self.swap(last)]
 
-    def sum(self, mine, theirs):
-        return TreeSum(self, mine, theirs)
+    def sum(self, mine, *theirs):
+        return TreeSum(self, mine, *theirs)
 
     def finish(self, terms, groups, per):
         return add_blocks(terms, groups, per)
@@ -745,10 +748,12 @@
 
 
 class TreeSum:
-    def __init__(self, links, mine, theirs):
+    def __init__(self, links, mine, *theirs):
         self.links, self.step = links, links.steps
-        self.sent, self.got = theirs, links.swap(theirs)
-        self.columns, self.shared = [[mine, self.got]], []
+        gots = [links.swap(part) for part in theirs[::-1]]
+        self.sent, self.got = theirs[-1], gots[0]
+        self.columns, self.shared = [[mine, gots[-1]]], []
+        self.upper = gots[0] if len(gots) > 1 else None
 
     def add(self, at):
         total = []
@@ -762,10 +767,15 @@
         return total
 
     def send(self, wait):
-        self.columns, self.shared = after((self.columns, self.shared), wait)
         self.step -= 1
         keep = 1 << self.step
-        self.sent = self.add(slice(keep, 2 * keep)).astype(BF16)
+        if self.upper is not None:
+            mine, upper = after((self.columns[0][0], self.upper), wait)
+            self.sent = (mine[keep:].astype(F32) + upper.astype(F32)).astype(BF16)
+            self.upper = None
+        else:
+            self.columns, self.shared = after((self.columns, self.shared), wait)
+            self.sent = self.add(slice(keep, 2 * keep)).astype(BF16)
         self.got = self.links.swap(self.sent, self.step)
         (self.columns[0] if len(self.columns) == 1 else self.shared).append(self.got)
         return self.sent
@@ -783,9 +793,9 @@
 
 
 class PlainSum:
-    def __init__(self, mine, theirs):
-        self.blocks = jnp.concatenate([mine, theirs]).astype(F32)
-        self.sent = self.got = theirs
+    def __init__(self, mine, *theirs):
+        self.blocks = jnp.concatenate([mine, *theirs]).astype(F32)
+        self.sent = self.got = theirs[0]
 
     def send(self, wait):
         return self.sent
@@ -813,8 +823,8 @@
             yield gathered, gathered
         yield [pack_blocks(gathered, self.blocks)]
 
-    def sum(self, mine, theirs):
-        return PlainSum(mine, theirs)
+    def sum(self, mine, *theirs):
+        return PlainSum(mine, *theirs)
 
     def finish(self, terms, groups, per):
         in_grad, out_grad = [], []

time: 226 us -> 225 us (level)
    convert_element_type x8 -> x7, other arithmetic: 11.9 us -> 9.03 us  [send(): self.sent = self.add(slice(keep, 2 * keep)).astype(BF16)]
    convert_element_type x0 -> x1, other arithmetic: none -> 2.77 us  [send(): self.sent = (mine[keep:].astype(F32) + upper.astype(F32)).astype(BF16)]
    ppermute x39 -> x40, waiting for transfers between devices: 32.6 us -> 31.4 us  [swap(): lax.ppermute(values, AXES, [(i, i ^ bits[i % 2]) for i in range(self.devi...]
    ppermute x39 -> x40, starting transfers between devices: 42.3 us -> 42.5 us  [swap(): lax.ppermute(values, AXES, [(i, i ^ bits[i % 2]) for i in range(self.devi...]
  transfers between devices with their start and end apart: 39 -> 40, of which waited for: 12 -> 12; matrix products, arithmetic and copies ran while one was open for 18% -> 18% of each run, Pallas kernels for 23% -> 24%
where the time goes in v4:
time: 225 us; the launch traced here: 224 us
  Pallas kernels  105 us (47%)
  starting transfers between devices  42.5 us (19%)
  waiting for transfers between devices  31.4 us (14%)
  other arithmetic  30.5 us (14%)
  local copies, waits for them, and re-layouts  12.8 us (6%)
    pallas_call x1, Pallas kernels, forward_backward(): call(kernel, 'forward_backward', (images,), [image(rows, width), whole(b_...  49.9 us
    ppermute x40, starting transfers between devices, swap(): lax.ppermute(values, AXES, [(i, i ^ bits[i % 2]) for i in range(self.devi...  42.5 us
    ppermute x40, waiting for transfers between devices, swap(): lax.ppermute(values, AXES, [(i, i ^ bits[i % 2]) for i in range(self.devi...  31.4 us
    pallas_call x2, Pallas kernels, forward_save(): call(kernel, 'forward_save', (count,), [some(width), whole((rows, 1)), so...  23.3 us
    pallas_call x1, Pallas kernels, backward_slots(): call(kernel, 'backward_slots', (images,), [image(rows, gate), image(rows,...  14.9 us
    pallas_call x1, Pallas kernels, backward_first(): call(kernel, 'backward_first', (images,), [image(rows, width), image(rows...  12.2 us
    convert_element_type x7, other arithmetic, send(): self.sent = self.add(slice(keep, 2 * keep)).astype(BF16)  9.03 us
  transfers between devices with their start and end apart: 40, of which 12 were waited for; matrix products, arithmetic and copies ran while one was open for 18% of the time, Pallas kernels for 24%

profile of v4, /device:TPU:0, one launch (start us, length us, event | category | flops | bytes accessed | tf_op | source)
XLA Modules:
  0.0 223.6 jit_solution(17131359188826968076)
XLA Ops:
  1.7 3.1 %collective-permute-start = (bf16[1,6,16,512]{3,2,1,0:T(8,128)(2,1)S(1)}, bf16[1,6,16,512]{3,2,1,0:T(8,128)(2,1)S(1)}, u32[]{:S(2)}, u32[]{:S(2)}) collective-permute-start(bf16[1,6,16,512]{3,2,1,0:T(8,128)(2,1)S(1)} %bitcast.58), channel_id=1, source_target_pairs={{0,8},{1,17},{2,10},{3,19},{4,12},{5,21},{6,14},{7,23},{8,0},{9,25... | collective-permute-start | bytes 294920 | tf_op jit(solution)/shard_map/ppermute | solution.py:692
  4.8 2.6 %collective-permute-start.1 = (bf16[1,6,16,512]{3,2,1,0:T(8,128)(2,1)S(1)}, bf16[1,6,16,512]{3,2,1,0:T(8,128)(2,1)S(1)}, u32[]{:S(2)}, u32[]{:S(2)}) collective-permute-start(bf16[1,6,16,512]{3,2,1,0:T(8,128)(2,1)S(1)} %bitcast.59), channel_id=1, source_target_pairs={{0,16},{1,9},{2,18},{3,11},{4,20},{5,13},{6,22},{7,15},{8,24},{9,1... | collective-permute-start | bytes 294920 | tf_op jit(solution)/shard_map/ppermute | solution.py:692
  7.4 1.4 fusion.54
  14.5 1.6 collective-permute-start.7
  16.4 1.7 collective-permute-start.3
  18.1 2.4 %collective-permute-start.4 = (bf16[1,12,16,512]{3,2,1,0:T(8,128)(2,1)S(1)}, bf16[1,12,16,512]{3,2,1,0:T(8,128)(2,1)S(1)}, u32[]{:S(2)}, u32[]{:S(2)}) collective-permute-start(bf16[1,12,16,512]{3,2,1,0:T(8,128)(2,1)S(1)} %pad_maximum_fusion.3), channel_id=1, source_target_pairs={{0,16},{1,9},{2,18},{3,11},{4,20},{5,13},{6,22},{7,15},{8,24},{9,1... | collective-permute-start | bytes 589832 | tf_op jit(solution)/shard_map/ppermute | solution.py:692
  21.1 1.6 collective-permute-start.8
  22.7 6.0 %collective-permute-done.3 = bf16[1,12,16,512]{3,2,1,0:T(8,128)(2,1)S(1)} collective-permute-done((bf16[1,12,16,512]{3,2,1,0:T(8,128)(2,1)S(1)}, bf16[1,12,16,512]{3,2,1,0:T(8,128)(2,1)S(1)}, u32[]{:S(2)}, u32[]{:S(2)}) %collective-permute-start.3) | collective-permute-done | bytes 196640 | tf_op jit(solution)/shard_map/ppermute | solution.py:692
  28.6 4.6 %collective-permute-done.4 = bf16[1,12,16,512]{3,2,1,0:T(8,128)(2,1)S(1)} collective-permute-done((bf16[1,12,16,512]{3,2,1,0:T(8,128)(2,1)S(1)}, bf16[1,12,16,512]{3,2,1,0:T(8,128)(2,1)S(1)}, u32[]{:S(2)}, u32[]{:S(2)}) %collective-permute-start.4) | collective-permute-done | bytes 196640 | tf_op jit(solution)/shard_map/ppermute | solution.py:692
  33.2 1.5 collective-permute-start.9
  39.1 2.1 collective-permute-done.9.refs_8_.refs_3_
  42.0 1.4 reshape.124
  43.3 1.1 pad.36.values_ref
  44.4 1.1 pad.37.cot_ref
  46.6 2.1 collective-permute-start.14
  49.3 10.3 %forward_save.2 = (bf16[5,208,1536]{2,1,0:T(8,128)(2,1)}, bf16[5,208,1536]{2,1,0:T(8,128)(2,1)}, bf16[5,208,1536]{2,1,0:T(8,128)(2,1)}, bf16[5,208,1536]{2,1,0:T...) custom-call(s32[32]{0:T(128)} %pad_add_fusion.owner_ref, ...), custom_call_target="tpu_custom_call" | custom-call | flops 4000000000 | bytes 20000000 | tf_op jit(solution)/shard_map/forward_save/pallas_call | solution.py:334
  61.0 12.9 %forward_save.3 = (bf16[5,208,1536]{2,1,0:T(8,128)(2,1)}, bf16[5,208,1536]{2,1,0:T(8,128)(2,1)}, bf16[5,208,1536]{2,1,0:T(8,128)(2,1)}, bf16[5,208,1536]{2,1,0:T...) custom-call(s32[32]{0:T(128)} %pad_add_fusion.owner_ref, ...), custom_call_target="tpu_custom_call", output_to_operand_aliasing={{0}: (18, {}), {1}: (19, {}), {2}: (20, {}), {3}: (21, {}),... | custom-call | flops 6000000000 | bytes 20000000 | tf_op jit(solution)/shard_map/forward_save/pallas_call | solution.py:334
  74.5 1.0 copy.65.valid_ref
  76.6 49.9 %forward_backward.1 = (bf16[5,208,512]{2,1,0:T(8,128)(2,1)}, f32[5,208,512]{2,1,0:T(8,128)}, bf16[5,208,1536]{2,1,0:T(8,128)(2,1)}, bf16[5,208,1536]{2,1,0:T(8,1...) custom-call(s32[32]{0:T(128)} %pad_add_fusion.owner_ref, ...), custom_call_target="tpu_custom_call" | custom-call | flops 40000000000 | bytes 20000000 | tf_op jit(solution)/shard_map/forward_backward/pallas_call | solution.py:460
  127.2 1.4 slice.193
  128.6 1.1 reshape.128
  129.8 2.8 %add_convert_fusion = bf16[8,9,16,512]{3,2,1,0:T(8,128)(2,1)} fusion(bf16[8,9,16,512]{3,2,1,0:T(8,128)(2,1)} %collective-permute-done.20, bf16[16,9,16,512]{3,2,1,0:T(8,128)(2,1)S(1)} %copy-done), kind=kLoop, calls=%fused_computation | loop fusion | flops 2359296 | bytes 3538944 | tf_op jit(solution)/shard_map/convert_element_type | solution.py:774
  132.6 2.0 collective-permute-start.22
  134.6 14.9 %backward_slots.1 = (bf16[5,208,1536]{2,1,0:T(8,128)(2,1)}, bf16[16,3,16,512]{3,2,1,0:T(8,128)(2,1)}, bf16[16,3,16,512]{3,2,1,0:T(8,128)(2,1)}, bf16[48,1536]{1,0:T(8,128)(2,1)}, bf16[48,1536]{1,0:T(8,128)(2,1)}) custom-call(s32[32]{0:T(128)} %pad_add_fusion.owner_ref, bf16[5,208,1536]{2,1,0:T(8,128)(2,1)} %get-tuple-element.153.mixed_ref, ...), custom_call_target="tpu_custom_call" | custom-call | flops 8999999488 | bytes 20000000 | tf_op jit(solution)/shard_map/backward_slots/pallas_call | solution.py:543
  150.3 2.6 %add_convert_fusion.1 = bf16[8,6,16,512]{3,2,1,0:T(8,128)(2,1)} fusion(bf16[16,6,16,512]{3,2,1,0:T(8,128)(2,1)} %collective-permute-done.23.refs_7_, bf16[16,6,16,512]{3,2,1,0:T(8,128)(2,1)} %get-tuple-element.214.refs_6_), kind=kLoop, calls=%fused_computation.1 | loop fusion | flops 1572864 | bytes 2359296 | tf_op jit(solution)/shard_map/convert_element_type | solution.py:778
  152.8 1.3 collective-permute-start.28
  154.1 2.2 add_convert_fusion.2
  158.7 5.8 %collective-permute-start.26 = (bf16[48,1536]{1,0:T(8,128)(2,1)S(1)}, bf16[48,1536]{1,0:T(8,128)(2,1)}, u32[]{:S(2)}, u32[]{:S(2)}) collective-permute-start(bf16[48,1536]{1,0:T(8,128)(2,1)S(1)} %add_convert_fusion.12), channel_id=1, source_target_pairs={{0,16},{1,9},{2,18},{3,11},{4,20},{5,13},{6,22},{7,15},{8,24},{9,1... | collective-permute-start | bytes 442376 | tf_op jit(solution)/shard_map/ppermute | solution.py:692
  164.4 12.2 %backward_first.1 = (f32[980,512]{1,0:T(8,128)}, f32[8,1536]{1,0:T(8,128)}) custom-call(s32[32]{0:T(128)} %pad_add_fusion.owner_ref, bf16[5,208,512]{2,1,0:T(8,128)(2,1)} %pad.36.values_ref, bf16[5,208,1536]{2,1,0:T(8,128)(2,1)} %get-tuple-element.148.left_ref, bf16[5,208,1536]{2,1,0:T(8,128)(2,1)} %get-tuple-element.168.right_ref, ...), custom_call_target="tpu_custom_call" | custom-call | flops 6000000000 | bytes 20000000 | tf_op jit(solution)/shard_map/backward_first/pallas_call | solution.py:600
  177.5 3.8 %collective-permute-start.30 = (bf16[8,1536]{1,0:T(8,128)(2,1)S(1)}, bf16[8,1536]{1,0:T(8,128)(2,1)S(1)}, u32[]{:S(2)}, u32[]{:S(2)}) collective-permute-start(bf16[8,1536]{1,0:T(8,128)(2,1)S(1)} %convert_element_type.364), channel_id=1, source_target_pairs={{0,16},{1,9},{2,18},{3,11},{4,20},{5,13},{6,22},{7,15},{8,24},{9,1... | collective-permute-start | bytes 73736 | tf_op jit(solution)/shard_map/ppermute | solution.py:692
  181.3 1.4 add_convert_fusion.3
  182.8 1.1 add_convert_fusion.6
  183.9 1.4 collective-permute-start.33
  185.3 1.2 add_convert_fusion.5
  187.6 1.8 collective-permute-start.31
  189.4 4.5 %collective-permute-done.33.refs_9_ = bf16[4,9,16,512]{3,2,1,0:T(8,128)(2,1)S(1)} collective-permute-done((bf16[4,9,16,512]{3,2,1,0:T(8,128)(2,1)S(1)}, bf16[4,9,16,512]{3,2,1,0:T(8,128)(2,1)S(1)}, u32[]{:S(2)}, u32[]{:S(2)}) %collective-permute-start.33) | collective-permute-done | bytes 589856 | tf_op jit(solution)/shard_map/ppermute | solution.py:692
  193.9 1.4 convert_add_fusion
  196.5 1.8 collective-permute-done.32.refs_4_
  198.3 1.9 add_convert_fusion.10
  200.2 1.4 collective-permute-start.34
  201.6 4.7 %collective-permute-done.35.refs_10_ = bf16[2,9,16,512]{3,2,1,0:T(8,128)(2,1)S(1)} collective-permute-done((bf16[2,9,16,512]{3,2,1,0:T(8,128)(2,1)S(1)}, bf16[2,9,16,512]{3,2,1,0:T(8,128)(2,1)S(1)}, u32[]{:S(2)}, u32[]{:S(2)}) %collective-permute-start.35) | collective-permute-done | bytes 294944 | tf_op jit(solution)/shard_map/ppermute | solution.py:692
  206.3 1.1 convert_add_fusion.1
  209.4 2.0 collective-permute-start.39
  211.4 2.3 %collective-permute-done.36 = bf16[48,1536]{1,0:T(8,128)(2,1)S(1)} collective-permute-done((bf16[48,1536]{1,0:T(8,128)(2,1)S(1)}, bf16[48,1536]{1,0:T(8,128)(2,1)S(1)}, u32[]{:S(2)}, u32[]{:S(2)}) %collective-permute-start.36) | collective-permute-done | bytes 147488 | tf_op jit(solution)/shard_map/ppermute | solution.py:692
  213.8 2.4 %collective-permute-done.38.refs_5_ = bf16[1,9,16,512]{3,2,1,0:T(8,128)(2,1)S(1)} collective-permute-done((bf16[1,9,16,512]{3,2,1,0:T(8,128)(2,1)}, bf16[1,9,16,512]{3,2,1,0:T(8,128)(2,1)S(1)}, u32[]{:S(2)}, u32[]{:S(2)}) %collective-permute-start.38) | collective-permute-done | bytes 147488 | tf_op jit(solution)/shard_map/ppermute | solution.py:692
  216.2 1.6 collective-permute-done.39.refs_11_
  218.4 2.5 %add_blocks.1 = (f32[2,16,3072]{2,1,0:T(8,128)}, f32[2,48,512]{2,1,0:T(8,128)}) custom-call(bf16[16,9,16,512]{3,2,1,0:T(8,128)(2,1)} %get-tuple-element.208.refs_0_, bf16[8,9,16,512]{3,2,1,0:T(8,128)(2,1)} %collective-permute-done.25.refs_1_, bf16[8,9,16,512]{3,2,1,0:T(8,128)(2,1)} %copy-done.1, bf16[4,9,16,512]{3,2,1,0:T(8,128)(2,1)} %collective-permute-done.27.refs_3_, ...), custom_call_target="tpu_custom_call" | custom-call | tf_op jit(solution)/shard_map/add_blocks/pallas_call | solution.py:672
  221.6 2.0 unpack_sums.1
  (182 shorter events, 27.4 us)
Async XLA Ops:
  1.7 9.2 %copy-start.23 = (f32[2,3072]{1,0:T(2,128)S(1)}, f32[2,3072]{1,0:T(2,128)}, u32[]{:S(2)}) copy-start(f32[2,3072]{1,0:T(2,128)} %param.22) | copy-start | bytes 73732
  1.7 12.3 %collective-permute-start = (bf16[1,6,16,512]{3,2,1,0:T(8,128)(2,1)S(1)}, bf16[1,6,16,512]{3,2,1,0:T(8,128)(2,1)S(1)}, u32[]{:S(2)}, u32[]{:S(2)}) collective-permute-start(bf16[1,6,16,512]{3,2,1,0:T(8,128)(2,1)S(1)} %bitcast.58), channel_id=1, source_target_pairs={{0,8},{1,17},{2,10},{3,19},{4,12},{5,21},{6,14},{7,23},{8,0},{9,25... | collective-permute-start | bytes 294920 | tf_op jit(solution)/shard_map/ppermute | solution.py:692
  4.8 9.6 %collective-permute-start.1 = (bf16[1,6,16,512]{3,2,1,0:T(8,128)(2,1)S(1)}, bf16[1,6,16,512]{3,2,1,0:T(8,128)(2,1)S(1)}, u32[]{:S(2)}, u32[]{:S(2)}) collective-permute-start(bf16[1,6,16,512]{3,2,1,0:T(8,128)(2,1)S(1)} %bitcast.59), channel_id=1, source_target_pairs={{0,16},{1,9},{2,18},{3,11},{4,20},{5,13},{6,22},{7,15},{8,24},{9,1... | collective-permute-start | bytes 294920 | tf_op jit(solution)/shard_map/ppermute | solution.py:692
  7.4 7.0 %collective-permute-start.2 = (bf16[1,6,16,512]{3,2,1,0:T(8,128)(2,1)S(1)}, bf16[1,6,16,512]{3,2,1,0:T(8,128)(2,1)S(1)}, u32[]{:S(2)}, u32[]{:S(2)}) collective-permute-start(bf16[1,6,16,512]{3,2,1,0:T(8,128)(2,1)S(1)} %bitcast.60), channel_id=1, source_target_pairs={{0,24},{1,25},{2,26},{3,27},{4,28},{5,29},{6,30},{7,31},{8,16},{9,... | collective-permute-start | bytes 294920 | tf_op jit(solution)/shard_map/ppermute | solution.py:692
  14.4 23.5 %copy-start.5 = (bf16[4,6,16,512]{3,2,1,0:T(8,128)(2,1)}, bf16[4,6,16,512]{3,2,1,0:T(8,128)(2,1)S(1)}, u32[]{:S(2)}) copy-start(bf16[4,6,16,512]{3,2,1,0:T(8,128)(2,1)S(1)} %pad_maximum_fusion.2.refs_5_.refs_0_) | copy-start | bytes 1179652
  14.5 18.7 %collective-permute-start.7 = (bf16[4,6,16,512]{3,2,1,0:T(8,128)(2,1)S(1)}, bf16[4,6,16,512]{3,2,1,0:T(8,128)(2,1)S(1)}, u32[]{:S(2)}, u32[]{:S(2)}) collective-permute-start(bf16[4,6,16,512]{3,2,1,0:T(8,128)(2,1)S(1)} %pad_maximum_fusion.2.refs_5_.refs_0_), channel_id=1, source_target_pairs={{0,2},{1,5},{2,0},{3,7},{4,6},{5,1},{6,4},{7,3},{8,10},{9,13},{10,... | collective-permute-start | bytes 1179656 | tf_op jit(solution)/shard_map/ppermute | solution.py:692
  16.4 12.2 %collective-permute-start.3 = (bf16[1,12,16,512]{3,2,1,0:T(8,128)(2,1)S(1)}, bf16[1,12,16,512]{3,2,1,0:T(8,128)(2,1)S(1)}, u32[]{:S(2)}, u32[]{:S(2)}) collective-permute-start(bf16[1,12,16,512]{3,2,1,0:T(8,128)(2,1)S(1)} %pad_maximum_fusion.3), channel_id=1, source_target_pairs={{0,8},{1,17},{2,10},{3,19},{4,12},{5,21},{6,14},{7,23},{8,0},{9,25... | collective-permute-start | bytes 589832 | tf_op jit(solution)/shard_map/ppermute | solution.py:692
  18.1 15.1 %collective-permute-start.4 = (bf16[1,12,16,512]{3,2,1,0:T(8,128)(2,1)S(1)}, bf16[1,12,16,512]{3,2,1,0:T(8,128)(2,1)S(1)}, u32[]{:S(2)}, u32[]{:S(2)}) collective-permute-start(bf16[1,12,16,512]{3,2,1,0:T(8,128)(2,1)S(1)} %pad_maximum_fusion.3), channel_id=1, source_target_pairs={{0,16},{1,9},{2,18},{3,11},{4,20},{5,13},{6,22},{7,15},{8,24},{9,1... | collective-permute-start | bytes 589832 | tf_op jit(solution)/shard_map/ppermute | solution.py:692
  20.5 12.7 %collective-permute-start.5 = (bf16[1,12,16,512]{3,2,1,0:T(8,128)(2,1)S(1)}, bf16[1,12,16,512]{3,2,1,0:T(8,128)(2,1)S(1)}, u32[]{:S(2)}, u32[]{:S(2)}) collective-permute-start(bf16[1,12,16,512]{3,2,1,0:T(8,128)(2,1)S(1)} %pad_maximum_fusion.3), channel_id=1, source_target_pairs={{0,24},{1,25},{2,26},{3,27},{4,28},{5,29},{6,30},{7,31},{8,16},{9,... | collective-permute-start | bytes 589832 | tf_op jit(solution)/shard_map/ppermute | solution.py:692
  21.1 17.6 %collective-permute-start.8 = (bf16[4,6,16,512]{3,2,1,0:T(8,128)(2,1)S(1)}, bf16[4,6,16,512]{3,2,1,0:T(8,128)(2,1)}, u32[]{:S(2)}, u32[]{:S(2)}) collective-permute-start(bf16[4,6,16,512]{3,2,1,0:T(8,128)(2,1)S(1)} %pad_maximum_fusion.2.refs_5_.refs_0_), channel_id=1, source_target_pairs={{0,4},{1,3},{2,6},{3,1},{4,0},{5,7},{6,2},{7,5},{8,12},{9,11},{10,... | collective-permute-start | bytes 1179656 | tf_op jit(solution)/shard_map/ppermute | solution.py:692
  33.2 7.9 %collective-permute-start.9 = (bf16[4,6,16,512]{3,2,1,0:T(8,128)(2,1)S(1)}, bf16[4,6,16,512]{3,2,1,0:T(8,128)(2,1)}, u32[]{:S(2)}, u32[]{:S(2)}) collective-permute-start(bf16[4,6,16,512]{3,2,1,0:T(8,128)(2,1)S(1)} %collective-permute-done.7.refs_6_.refs_1_), channel_id=1, source_target_pairs={{0,4},{1,3},{2,6},{3,1},{4,0},{5,7},{6,2},{7,5},{8,12},{9,11},{10,... | collective-permute-start | bytes 1179656 | tf_op jit(solution)/shard_map/ppermute | solution.py:692
  36.4 10.3 %collective-permute-start.10 = (bf16[4,6,16,512]{3,2,1,0:T(8,128)(2,1)S(1)}, bf16[4,6,16,512]{3,2,1,0:T(8,128)(2,1)}, u32[]{:S(2)}, u32[]{:S(2)}) collective-permute-start(bf16[4,6,16,512]{3,2,1,0:T(8,128)(2,1)S(1)} %pad_maximum_fusion.2.refs_5_.refs_0_), channel_id=1, source_target_pairs={{0,1},{1,0},{2,3},{3,2},{4,5},{5,4},{6,7},{7,6},{8,9},{9,8},{10,11... | collective-permute-start | bytes 1179656 | tf_op jit(solution)/shard_map/ppermute | solution.py:692
  38.0 21.7 %collective-permute-start.6 = (bf16[4,12,16,512]{3,2,1,0:T(8,128)(2,1)}, bf16[4,12,16,512]{3,2,1,0:T(8,128)(2,1)}, u32[]{:S(2)}, u32[]{:S(2)}) collective-permute-start(bf16[4,12,16,512]{3,2,1,0:T(8,128)(2,1)} %pad_maximum_fusion.refs_9_), channel_id=1, source_target_pairs={{0,2},{1,5},{2,0},{3,7},{4,6},{5,1},{6,4},{7,3},{8,10},{9,13},{10,... | collective-permute-start | bytes 2359304 | tf_op jit(solution)/shard_map/ppermute | solution.py:692
  38.5 10.8 %collective-permute-start.11 = (bf16[4,6,16,512]{3,2,1,0:T(8,128)(2,1)S(1)}, bf16[4,6,16,512]{3,2,1,0:T(8,128)(2,1)}, u32[]{:S(2)}, u32[]{:S(2)}) collective-permute-start(bf16[4,6,16,512]{3,2,1,0:T(8,128)(2,1)S(1)} %collective-permute-done.7.refs_6_.refs_1_), channel_id=1, source_target_pairs={{0,1},{1,0},{2,3},{3,2},{4,5},{5,4},{6,7},{7,6},{8,9},{9,8},{10,11... | collective-permute-start | bytes 1179656 | tf_op jit(solution)/shard_map/ppermute | solution.py:692
  38.7 10.6 %collective-permute-start.12 = (bf16[4,6,16,512]{3,2,1,0:T(8,128)(2,1)}, bf16[4,6,16,512]{3,2,1,0:T(8,128)(2,1)}, u32[]{:S(2)}, u32[]{:S(2)}) collective-permute-start(bf16[4,6,16,512]{3,2,1,0:T(8,128)(2,1)} %collective-permute-done.8.refs_7_.refs_2_), channel_id=1, source_target_pairs={{0,1},{1,0},{2,3},{3,2},{4,5},{5,4},{6,7},{7,6},{8,9},{9,8},{10,11... | collective-permute-start | bytes 1179656 | tf_op jit(solution)/shard_map/ppermute | solution.py:692
  41.1 8.2 %collective-permute-start.13 = (bf16[4,6,16,512]{3,2,1,0:T(8,128)(2,1)}, bf16[4,6,16,512]{3,2,1,0:T(8,128)(2,1)}, u32[]{:S(2)}, u32[]{:S(2)}) collective-permute-start(bf16[4,6,16,512]{3,2,1,0:T(8,128)(2,1)} %collective-permute-done.9.refs_8_.refs_3_), channel_id=1, source_target_pairs={{0,1},{1,0},{2,3},{3,2},{4,5},{5,4},{6,7},{7,6},{8,9},{9,8},{10,11... | collective-permute-start | bytes 1179656 | tf_op jit(solution)/shard_map/ppermute | solution.py:692
  46.6 14.3 %collective-permute-start.14 = (bf16[4,12,16,512]{3,2,1,0:T(8,128)(2,1)}, bf16[4,12,16,512]{3,2,1,0:T(8,128)(2,1)S(1)}, u32[]{:S(2)}, u32[]{:S(2)}) collective-permute-start(bf16[4,12,16,512]{3,2,1,0:T(8,128)(2,1)} %pad_maximum_fusion.refs_9_), channel_id=1, source_target_pairs={{0,4},{1,3},{2,6},{3,1},{4,0},{5,7},{6,2},{7,5},{8,12},{9,11},{10,... | collective-permute-start | bytes 2359304 | tf_op jit(solution)/shard_map/ppermute | solution.py:692
  59.7 14.3 %collective-permute-start.15 = (bf16[4,12,16,512]{3,2,1,0:T(8,128)(2,1)}, bf16[4,12,16,512]{3,2,1,0:T(8,128)(2,1)S(1)}, u32[]{:S(2)}, u32[]{:S(2)}) collective-permute-start(bf16[4,12,16,512]{3,2,1,0:T(8,128)(2,1)} %collective-permute-done.6.refs_10_), channel_id=1, source_target_pairs={{0,4},{1,3},{2,6},{3,1},{4,0},{5,7},{6,2},{7,5},{8,12},{9,11},{10,... | collective-permute-start | bytes 2359304 | tf_op jit(solution)/shard_map/ppermute | solution.py:692
  60.4 15.1 %collective-permute-start.16 = (bf16[4,12,16,512]{3,2,1,0:T(8,128)(2,1)}, bf16[4,12,16,512]{3,2,1,0:T(8,128)(2,1)S(1)}, u32[]{:S(2)}, u32[]{:S(2)}) collective-permute-start(bf16[4,12,16,512]{3,2,1,0:T(8,128)(2,1)} %pad_maximum_fusion.refs_9_), channel_id=1, source_target_pairs={{0,1},{1,0},{2,3},{3,2},{4,5},{5,4},{6,7},{7,6},{8,9},{9,8},{10,11... | collective-permute-start | bytes 2359304 | tf_op jit(solution)/shard_map/ppermute | solution.py:692
  60.4 15.1 %collective-permute-start.17 = (bf16[4,12,16,512]{3,2,1,0:T(8,128)(2,1)}, bf16[4,12,16,512]{3,2,1,0:T(8,128)(2,1)S(1)}, u32[]{:S(2)}, u32[]{:S(2)}) collective-permute-start(bf16[4,12,16,512]{3,2,1,0:T(8,128)(2,1)} %collective-permute-done.6.refs_10_), channel_id=1, source_target_pairs={{0,1},{1,0},{2,3},{3,2},{4,5},{5,4},{6,7},{7,6},{8,9},{9,8},{10,11... | collective-permute-start | bytes 2359304 | tf_op jit(solution)/shard_map/ppermute | solution.py:692
  60.9 13.0 %copy-start.32 = (bf16[4,12,16,512]{3,2,1,0:T(8,128)(2,1)}, bf16[4,12,16,512]{3,2,1,0:T(8,128)(2,1)S(1)}, u32[]{:S(2)}) copy-start(bf16[4,12,16,512]{3,2,1,0:T(8,128)(2,1)S(1)} %collective-permute-done.14.refs_11_) | copy-start | bytes 2359300
  60.9 14.6 %collective-permute-start.18 = (bf16[4,12,16,512]{3,2,1,0:T(8,128)(2,1)S(1)}, bf16[4,12,16,512]{3,2,1,0:T(8,128)(2,1)}, u32[]{:S(2)}, u32[]{:S(2)}) collective-permute-start(bf16[4,12,16,512]{3,2,1,0:T(8,128)(2,1)S(1)} %collective-permute-done.14.refs_11_), channel_id=1, source_target_pairs={{0,1},{1,0},{2,3},{3,2},{4,5},{5,4},{6,7},{7,6},{8,9},{9,8},{10,11... | collective-permute-start | bytes 2359304 | tf_op jit(solution)/shard_map/ppermute | solution.py:692
  61.0 13.5 %copy-start.18 = (f32[5,208,1]{1,0,2:T(8,128)S(1)}, f32[5,208,1]{1,0,2:T(8,128)}, u32[]{:S(2)}) copy-start(f32[5,208,1]{1,0,2:T(8,128)} %pad_bitcast_fusion) | copy-start | bytes 12484
  74.0 2.6 %collective-permute-start.19 = (bf16[4,12,16,512]{3,2,1,0:T(8,128)(2,1)S(1)}, bf16[4,12,16,512]{3,2,1,0:T(8,128)(2,1)}, u32[]{:S(2)}, u32[]{:S(2)}) collective-permute-start(bf16[4,12,16,512]{3,2,1,0:T(8,128)(2,1)S(1)} %collective-permute-done.15.refs_12_), channel_id=1, source_target_pairs={{0,1},{1,0},{2,3},{3,2},{4,5},{5,4},{6,7},{7,6},{8,9},{9,8},{10,11... | collective-permute-start | bytes 2359304 | tf_op jit(solution)/shard_map/ppermute | solution.py:692
  126.6 3.3 %collective-permute-start.20 = (bf16[8,9,16,512]{3,2,1,0:T(8,128)(2,1)}, bf16[8,9,16,512]{3,2,1,0:T(8,128)(2,1)}, u32[]{:S(2)}, u32[]{:S(2)}) collective-permute-start(bf16[8,9,16,512]{3,2,1,0:T(8,128)(2,1)} %get-tuple-element.145), channel_id=1, source_target_pairs={{0,1},{1,0},{2,3},{3,2},{4,5},{5,4},{6,7},{7,6},{8,9},{9,8},{10,11... | collective-permute-start | bytes 3538952 | tf_op jit(solution)/shard_map/ppermute | solution.py:692
  127.0 22.6 %collective-permute-start.23 = (bf16[16,6,16,512]{3,2,1,0:T(8,128)(2,1)}, bf16[16,6,16,512]{3,2,1,0:T(8,128)(2,1)}, u32[]{:S(2)}, u32[]{:S(2)}) collective-permute-start(bf16[16,6,16,512]{3,2,1,0:T(8,128)(2,1)} %get-tuple-element.146), channel_id=1, source_target_pairs={{0,1},{1,0},{2,3},{3,2},{4,5},{5,4},{6,7},{7,6},{8,9},{9,8},{10,11... | collective-permute-start | bytes 4718600 | tf_op jit(solution)/shard_map/ppermute | solution.py:692
  132.6 17.0 %collective-permute-start.22 = (bf16[8,9,16,512]{3,2,1,0:T(8,128)(2,1)}, bf16[8,9,16,512]{3,2,1,0:T(8,128)(2,1)S(1)}, u32[]{:S(2)}, u32[]{:S(2)}) collective-permute-start(bf16[8,9,16,512]{3,2,1,0:T(8,128)(2,1)} %add_convert_fusion), channel_id=1, source_target_pairs={{0,4},{1,3},{2,6},{3,1},{4,0},{5,7},{6,2},{7,5},{8,12},{9,11},{10,... | collective-permute-start | bytes 3538952 | tf_op jit(solution)/shard_map/ppermute | solution.py:692
  134.6 19.5 %collective-permute-start.25 = (bf16[8,9,16,512]{3,2,1,0:T(8,128)(2,1)}, bf16[8,9,16,512]{3,2,1,0:T(8,128)(2,1)}, u32[]{:S(2)}, u32[]{:S(2)}) collective-permute-start(bf16[8,9,16,512]{3,2,1,0:T(8,128)(2,1)} %get-tuple-element.176), channel_id=1, source_target_pairs={{0,1},{1,0},{2,3},{3,2},{4,5},{5,4},{6,7},{7,6},{8,9},{9,8},{10,11... | collective-permute-start | bytes 3538952 | tf_op jit(solution)/shard_map/ppermute | solution.py:692
  149.6 48.7 %copy-start.1 = (bf16[8,9,16,512]{3,2,1,0:T(8,128)(2,1)}, bf16[8,9,16,512]{3,2,1,0:T(8,128)(2,1)S(1)}, u32[]{:S(2)}) copy-start(bf16[8,9,16,512]{3,2,1,0:T(8,128)(2,1)S(1)} %collective-permute-done.22.refs_2_) | copy-start | bytes 3538948
  149.6 7.4 %collective-permute-start.24 = (bf16[16,3,16,512]{3,2,1,0:T(8,128)(2,1)}, bf16[16,3,16,512]{3,2,1,0:T(8,128)(2,1)S(1)}, u32[]{:S(2)}, u32[]{:S(2)}) collective-permute-start(bf16[16,3,16,512]{3,2,1,0:T(8,128)(2,1)} %get-tuple-element.175), channel_id=1, source_target_pairs={{0,1},{1,0},{2,3},{3,2},{4,5},{5,4},{6,7},{7,6},{8,9},{9,8},{10,11... | collective-permute-start | bytes 2359304 | tf_op jit(solution)/shard_map/ppermute | solution.py:692
  150.2 8.4 %collective-permute-start.21 = (bf16[48,1536]{1,0:T(8,128)(2,1)}, bf16[48,1536]{1,0:T(8,128)(2,1)S(1)}, u32[]{:S(2)}, u32[]{:S(2)}) collective-permute-start(bf16[48,1536]{1,0:T(8,128)(2,1)} %get-tuple-element.171), channel_id=1, source_target_pairs={{0,1},{1,0},{2,3},{3,2},{4,5},{5,4},{6,7},{7,6},{8,9},{9,8},{10,11... | collective-permute-start | bytes 442376 | tf_op jit(solution)/shard_map/ppermute | solution.py:692
  152.8 23.8 %collective-permute-start.28 = (bf16[8,6,16,512]{3,2,1,0:T(8,128)(2,1)}, bf16[8,6,16,512]{3,2,1,0:T(8,128)(2,1)}, u32[]{:S(2)}, u32[]{:S(2)}) collective-permute-start(bf16[8,6,16,512]{3,2,1,0:T(8,128)(2,1)} %add_convert_fusion.1), channel_id=1, source_target_pairs={{0,4},{1,3},{2,6},{3,1},{4,0},{5,7},{6,2},{7,5},{8,12},{9,11},{10,... | collective-permute-start | bytes 2359304 | tf_op jit(solution)/shard_map/ppermute | solution.py:692
  156.3 20.3 %collective-permute-start.27 = (bf16[4,9,16,512]{3,2,1,0:T(8,128)(2,1)}, bf16[4,9,16,512]{3,2,1,0:T(8,128)(2,1)}, u32[]{:S(2)}, u32[]{:S(2)}) collective-permute-start(bf16[4,9,16,512]{3,2,1,0:T(8,128)(2,1)} %add_convert_fusion.2), channel_id=1, source_target_pairs={{0,2},{1,5},{2,0},{3,7},{4,6},{5,1},{6,4},{7,3},{8,10},{9,13},{10,... | collective-permute-start | bytes 1769480 | tf_op jit(solution)/shard_map/ppermute | solution.py:692
  158.1 18.5 %collective-permute-start.29 = (bf16[8,3,16,512]{3,2,1,0:T(8,128)(2,1)}, bf16[8,3,16,512]{3,2,1,0:T(8,128)(2,1)S(1)}, u32[]{:S(2)}, u32[]{:S(2)}) collective-permute-start(bf16[8,3,16,512]{3,2,1,0:T(8,128)(2,1)} %add_convert_fusion.4), channel_id=1, source_target_pairs={{0,4},{1,3},{2,6},{3,1},{4,0},{5,7},{6,2},{7,5},{8,12},{9,11},{10,... | collective-permute-start | bytes 1179656 | tf_op jit(solution)/shard_map/ppermute | solution.py:692
  158.7 28.0 %collective-permute-start.26 = (bf16[48,1536]{1,0:T(8,128)(2,1)S(1)}, bf16[48,1536]{1,0:T(8,128)(2,1)}, u32[]{:S(2)}, u32[]{:S(2)}) collective-permute-start(bf16[48,1536]{1,0:T(8,128)(2,1)S(1)} %add_convert_fusion.12), channel_id=1, source_target_pairs={{0,16},{1,9},{2,18},{3,11},{4,20},{5,13},{6,22},{7,15},{8,24},{9,1... | collective-permute-start | bytes 442376 | tf_op jit(solution)/shard_map/ppermute | solution.py:692
  176.6 30.8 %copy-start.6 = (bf16[8,3,16,512]{3,2,1,0:T(8,128)(2,1)}, bf16[8,3,16,512]{3,2,1,0:T(8,128)(2,1)S(1)}, u32[]{:S(2)}) copy-start(bf16[8,3,16,512]{3,2,1,0:T(8,128)(2,1)S(1)} %collective-permute-done.29.refs_14_) | copy-start | bytes 1179652
  177.5 9.2 %collective-permute-start.30 = (bf16[8,1536]{1,0:T(8,128)(2,1)S(1)}, bf16[8,1536]{1,0:T(8,128)(2,1)S(1)}, u32[]{:S(2)}, u32[]{:S(2)}) collective-permute-start(bf16[8,1536]{1,0:T(8,128)(2,1)S(1)} %convert_element_type.364), channel_id=1, source_target_pairs={{0,16},{1,9},{2,18},{3,11},{4,20},{5,13},{6,22},{7,15},{8,24},{9,1... | collective-permute-start | bytes 73736 | tf_op jit(solution)/shard_map/ppermute | solution.py:692
  183.9 9.9 %collective-permute-start.33 = (bf16[4,9,16,512]{3,2,1,0:T(8,128)(2,1)S(1)}, bf16[4,9,16,512]{3,2,1,0:T(8,128)(2,1)S(1)}, u32[]{:S(2)}, u32[]{:S(2)}) collective-permute-start(bf16[4,9,16,512]{3,2,1,0:T(8,128)(2,1)S(1)} %pad_maximum_fusion.1), channel_id=1, source_target_pairs={{0,2},{1,5},{2,0},{3,7},{4,6},{5,1},{6,4},{7,3},{8,10},{9,13},{10,... | collective-permute-start | bytes 1769480 | tf_op jit(solution)/shard_map/ppermute | solution.py:692
  186.6 11.7 %collective-permute-start.32 = (bf16[2,9,16,512]{3,2,1,0:T(8,128)(2,1)S(1)}, bf16[2,9,16,512]{3,2,1,0:T(8,128)(2,1)S(1)}, u32[]{:S(2)}, u32[]{:S(2)}) collective-permute-start(bf16[2,9,16,512]{3,2,1,0:T(8,128)(2,1)S(1)} %add_convert_fusion.5), channel_id=1, source_target_pairs={{0,16},{1,9},{2,18},{3,11},{4,20},{5,13},{6,22},{7,15},{8,24},{9,1... | collective-permute-start | bytes 884744 | tf_op jit(solution)/shard_map/ppermute | solution.py:692
  187.6 12.5 %collective-permute-start.31 = (bf16[48,1536]{1,0:T(8,128)(2,1)S(1)}, bf16[48,1536]{1,0:T(8,128)(2,1)S(1)}, u32[]{:S(2)}, u32[]{:S(2)}) collective-permute-start(bf16[48,1536]{1,0:T(8,128)(2,1)S(1)} %add_convert_fusion.11), channel_id=1, source_target_pairs={{0,8},{1,17},{2,10},{3,19},{4,12},{5,21},{6,14},{7,23},{8,0},{9,25... | collective-permute-start | bytes 442376 | tf_op jit(solution)/shard_map/ppermute | solution.py:692
  193.9 14.4 %copy-start.4 = (bf16[4,9,16,512]{3,2,1,0:T(8,128)(2,1)}, bf16[4,9,16,512]{3,2,1,0:T(8,128)(2,1)S(1)}, u32[]{:S(2)}) copy-start(bf16[4,9,16,512]{3,2,1,0:T(8,128)(2,1)S(1)} %collective-permute-done.33.refs_9_) | copy-start | bytes 1769476
  196.4 9.9 %collective-permute-start.35 = (bf16[2,9,16,512]{3,2,1,0:T(8,128)(2,1)S(1)}, bf16[2,9,16,512]{3,2,1,0:T(8,128)(2,1)S(1)}, u32[]{:S(2)}, u32[]{:S(2)}) collective-permute-start(bf16[2,9,16,512]{3,2,1,0:T(8,128)(2,1)S(1)} %fusion.12), channel_id=1, source_target_pairs={{0,16},{1,9},{2,18},{3,11},{4,20},{5,13},{6,22},{7,15},{8,24},{9,1... | collective-permute-start | bytes 884744 | tf_op jit(solution)/shard_map/ppermute | solution.py:692
  198.3 10.1 %copy-start.8 = (bf16[2,9,16,512]{3,2,1,0:T(8,128)(2,1)}, bf16[2,9,16,512]{3,2,1,0:T(8,128)(2,1)S(1)}, u32[]{:S(2)}) copy-start(bf16[2,9,16,512]{3,2,1,0:T(8,128)(2,1)S(1)} %collective-permute-done.32.refs_4_) | copy-start | bytes 884740
  200.2 8.2 %collective-permute-start.34 = (bf16[48,1536]{1,0:T(8,128)(2,1)S(1)}, bf16[48,1536]{1,0:T(8,128)(2,1)S(1)}, u32[]{:S(2)}, u32[]{:S(2)}) collective-permute-start(bf16[48,1536]{1,0:T(8,128)(2,1)S(1)} %add_convert_fusion.9), channel_id=1, source_target_pairs={{0,2},{1,5},{2,0},{3,7},{4,6},{5,1},{6,4},{7,3},{8,10},{9,13},{10,... | collective-permute-start | bytes 442376 | tf_op jit(solution)/shard_map/ppermute | solution.py:692
  208.5 5.2 %collective-permute-start.36 = (bf16[48,1536]{1,0:T(8,128)(2,1)S(1)}, bf16[48,1536]{1,0:T(8,128)(2,1)S(1)}, u32[]{:S(2)}, u32[]{:S(2)}) collective-permute-start(bf16[48,1536]{1,0:T(8,128)(2,1)S(1)} %add_convert_fusion.8), channel_id=1, source_target_pairs={{0,4},{1,3},{2,6},{3,1},{4,0},{5,7},{6,2},{7,5},{8,12},{9,11},{10,... | collective-permute-start | bytes 442376 | tf_op jit(solution)/shard_map/ppermute | solution.py:692
  209.4 6.8 %collective-permute-start.38 = (bf16[1,9,16,512]{3,2,1,0:T(8,128)(2,1)}, bf16[1,9,16,512]{3,2,1,0:T(8,128)(2,1)S(1)}, u32[]{:S(2)}, u32[]{:S(2)}) collective-permute-start(bf16[1,9,16,512]{3,2,1,0:T(8,128)(2,1)} %add_convert_fusion.10), channel_id=1, source_target_pairs={{0,8},{1,17},{2,10},{3,19},{4,12},{5,21},{6,14},{7,23},{8,0},{9,25... | collective-permute-start | bytes 442376 | tf_op jit(solution)/shard_map/ppermute | solution.py:692
  209.4 8.4 %collective-permute-start.39 = (bf16[1,9,16,512]{3,2,1,0:T(8,128)(2,1)S(1)}, bf16[1,9,16,512]{3,2,1,0:T(8,128)(2,1)S(1)}, u32[]{:S(2)}, u32[]{:S(2)}) collective-permute-start(bf16[1,9,16,512]{3,2,1,0:T(8,128)(2,1)S(1)} %fusion.30), channel_id=1, source_target_pairs={{0,8},{1,17},{2,10},{3,19},{4,12},{5,21},{6,14},{7,23},{8,0},{9,25... | collective-permute-start | bytes 442376 | tf_op jit(solution)/shard_map/ppermute | solution.py:692
  213.7 7.2 %collective-permute-start.37 = (bf16[48,1536]{1,0:T(8,128)(2,1)S(1)}, bf16[48,1536]{1,0:T(8,128)(2,1)S(1)}, u32[]{:S(2)}, u32[]{:S(2)}) collective-permute-start(bf16[48,1536]{1,0:T(8,128)(2,1)S(1)} %add_convert_fusion.7.mine_ref), channel_id=1, source_target_pairs={{0,1},{1,0},{2,3},{3,2},{4,5},{5,4},{6,7},{7,6},{8,9},{9,8},{10,11... | collective-permute-start | bytes 442376 | tf_op jit(solution)/shard_map/ppermute | solution.py:692
  (28 other events, 106.2 us)

commit v5 on v4

--- a/solution.py
+++ b/solution.py
@@ -612,51 +612,59 @@
     )(owner, values, left_grad, right_grad, upstream, w["gain_one"], *pieces)
 
 
-def unpack_sums(odd, mine, theirs, slots, width):
+def put_outputs(is_odd, mine, theirs, outs, slots, width):
+    gain_one, bias_one, b_in, gain_two, bias_two, spatial, b_sp, b_out = outs
     gate = mine.shape[1]
     high = mine.shape[0] - 8
     strips = gate // STRIP
-
-    def kernel(odd_ref, mine_ref, theirs_ref, gain_one, bias_one, b_in, gain_two, bias_two, spatial, b_sp, b_out):
-        is_odd = odd_ref[0] == 1
-        held = mine_ref[...].astype(F32), theirs_ref[...].astype(F32)
-        for block in range(2):
-            value = jnp.where(is_odd, held[1 - block], held[block])
-            square = [value[:high, strip * STRIP : (strip + 1) * STRIP] for strip in range(strips)]
-            square = jnp.concatenate(square + [jnp.zeros((STRIP, STRIP), F32)], 0)[:STRIP]
-            b_sp[block : block + 1] = square[slots : slots + 1, :slots]
-            spatial[:, block, :] = square.T[:slots, :slots]
-            line = lambda place: value[high + place : high + place + 1]
-            b_in[block : block + 1, :gate] = line(0)
-            b_in[block : block + 1, gate:] = line(1)
-            gain_two[block : block + 1] = line(2)
-            bias_two[block : block + 1] = line(3)
-            narrow = line(4)
-            if block == 0:
-                narrow = narrow + (held[0][high + 5 : high + 6] + held[1][high + 5 : high + 6])
-            for place, out in enumerate((b_out, gain_one, bias_one)):
-                out[block : block + 1] = narrow[:, place * width : (place + 1) * width]
-
-    shapes = [(2, width), (2, width), (2, 2 * gate), (2, gate), (2, gate), (slots, 2, slots), (2, slots), (2, width)]
-    results = pl.pallas_call(
+    held = mine[...].astype(F32), theirs[...].astype(F32)
+    for block in range(2):
+        value = jnp.where(is_odd, held[1 - block], held[block])
+        square = [value[:high, strip * STRIP : (strip + 1) * STRIP] for strip in range(strips)]
+        square = jnp.concatenate(square + [jnp.zeros((STRIP, STRIP), F32)], 0)[:STRIP]
+        b_sp[block : block + 1] = square[slots : slots + 1, :slots]
+        spatial[:, block, :] = square.T[:slots, :slots]
+        line = lambda place: value[high + place : high + place + 1]
+        b_in[block : block + 1, :gate] = line(0)
+        b_in[block : block + 1, gate:] = line(1)
+        gain_two[block : block + 1] = line(2)
+        bias_two[block : block + 1] = line(3)
+        narrow = line(4)
+        if block == 0:
+            narrow = narrow + (held[0][high + 5 : high + 6] + held[1][high + 5 : high + 6])
+        for place, out in enumerate((b_out, gain_one, bias_one)):
+            out[block : block + 1] = narrow[:, place * width : (place + 1) * width]
+
+
+def small_shapes(slots, gate, width):
+    return [(2, width), (2, width), (2, 2 * gate), (2, gate), (2, gate), (slots, 2, slots), (2, slots), (2, width)]
+
+
+def unpack_sums(odd, mine, theirs, slots, width):
+    def kernel(odd_ref, mine_ref, theirs_ref, *outs):
+        put_outputs(odd_ref[0] == 1, mine_ref, theirs_ref, outs, slots, width)
+
+    return pl.pallas_call(
         kernel,
         in_specs=[pl.BlockSpec(memory_space=pltpu.SMEM)] + [pl.BlockSpec(memory_space=pltpu.VMEM)] * 2,
-        out_shape=[jax.ShapeDtypeStruct(shape, F32) for shape in shapes],
+        out_shape=[jax.ShapeDtypeStruct(shape, F32) for shape in small_shapes(slots, mine.shape[1], width)],
         compiler_params=pltpu.CompilerParams(vmem_limit_bytes=60 << 20),
         name="unpack_sums",
     )(odd, mine, theirs)
-    return [*results[:5], results[5].transpose(1, 0, 2), *results[6:]]
-
-
-def add_blocks(terms, groups, per):
+
+
+def add_blocks(terms, groups, per, odd, mine, theirs, slots):
     arrays = []
     for pairs in terms.values():
         arrays += [array for array, unused in pairs if not any(array is other for other in arrays)]
     index = {id(array): at for at, array in enumerate(arrays)}
     width = arrays[0].shape[-1]
 
-    def kernel(*refs):
-        in_out, out_out = refs[-2:]
+    n_a = len(arrays)
+
+    def kernel(odd_ref, *refs):
+        mine_ref, theirs_ref, in_out, out_out, *outs = refs[n_a:]
+        put_outputs(odd_ref[0] == 1, mine_ref, theirs_ref, outs, slots, width)
         for (block, group), pairs in terms.items():
             total = None
             for array, at in pairs:
@@ -668,16 +676,19 @@
                 first = (group - groups) * BLOCK
                 out_out[block, first : first + BLOCK] = total
 
-    shapes = [(2, BLOCK, groups * GROUP), (2, per * BLOCK, width)]
-    return pl.pallas_call(
+    shapes = [(2, BLOCK, groups * GROUP), (2, per * BLOCK, width)] + small_shapes(slots, mine.shape[1], width)
+    results = pl.pallas_call(
         kernel,
         grid=(1,),
-        in_specs=[pl.BlockSpec((1,) + array.shape[1:], lambda i: (0, 0, 0, 0)) for array in arrays],
+        in_specs=[pl.BlockSpec(memory_space=pltpu.SMEM)]
+        + [pl.BlockSpec((1,) + array.shape[1:], lambda i: (0, 0, 0, 0)) for array in arrays]
+        + [whole(mine.shape)] * 2,
         out_specs=[whole(shape) for shape in shapes],
         out_shape=[jax.ShapeDtypeStruct(shape, F32) for shape in shapes],
         compiler_params=pltpu.CompilerParams(vmem_limit_bytes=60 << 20),
         name="add_blocks",
-    )(*arrays)
+    )(odd, *arrays, mine, theirs)
+    return results[:2], results[2:]
 
 
 class Tree:
@@ -722,8 +733,8 @@
     def sum(self, mine, *theirs):
         return TreeSum(self, mine, *theirs)
 
-    def finish(self, terms, groups, per):
-        return add_blocks(terms, groups, per)
+    def finish(self, terms, groups, per, ends, slots):
+        return add_blocks(terms, groups, per, *ends, slots)
 
     def total(self, mine, theirs):
         far = self.steps - 2
@@ -826,16 +837,17 @@
     def sum(self, mine, *theirs):
         return PlainSum(mine, *theirs)
 
-    def finish(self, terms, groups, per):
+    def finish(self, terms, groups, per, ends, slots):
         in_grad, out_grad = [], []
         for block in range(2):
             inner = jnp.concatenate([terms[block, group] for group in range(groups)], 2)
             outer = jnp.concatenate([terms[block, groups + part] for part in range(per)], 1)
             in_grad.append(inner.reshape(self.width, -1))
             out_grad.append(outer.reshape(self.gate, -1))
-        return [
+        large = [
             lax.psum_scatter(jnp.stack(grad), AXES, scatter_dimension=1, tiled=True) for grad in (in_grad, out_grad)
         ]
+        return large, unpack_sums(*ends, slots, self.width)
 
     def total(self, mine, theirs):
         yield mine
@@ -1016,10 +1028,10 @@
     spots = [(0, group) for group in range(steps)] + [(0, groups + part) for part in range(per)]
     spots += [(0, steps + group) for group in range(steps)]
     terms |= zip(spots, both.terms())
-    in_grad, out_grad = links.finish(terms, groups, per)
-    gain_one, bias_one, b_in, gain_two, bias_two, spatial_grad, b_sp, b_out = unpack_sums(
-        odd.reshape(1), *summed, slots, width
-    )
+    large, small = links.finish(terms, groups, per, (odd.reshape(1), *summed), slots)
+    in_grad, out_grad = large
+    gain_one, bias_one, b_in, gain_two, bias_two, spatial_grad, b_sp, b_out = small
+    spatial_grad = spatial_grad.transpose(1, 0, 2)
 
     return (
         layer_out,

time: 225 us -> 222 us (0.987)
  transfers between devices with their start and end apart: 40 -> 40, of which waited for: 12 -> 12; matrix products, arithmetic and copies ran while one was open for 18% -> 18% of each run, Pallas kernels for 24% -> 23%
where the time goes in v5:
time: 222 us; the launch traced here: 221 us
  Pallas kernels  103 us (46%)
  starting transfers between devices  42.4 us (19%)
  waiting for transfers between devices  31.4 us (14%)
  other arithmetic  30.4 us (14%)
  local copies, waits for them, and re-layouts  12.2 us (5%)
    pallas_call x1, Pallas kernels, forward_backward(): call(kernel, 'forward_backward', (images,), [image(rows, width), whole(b_...  49.9 us
    ppermute x40, starting transfers between devices, swap(): lax.ppermute(values, AXES, [(i, i ^ bits[i % 2]) for i in range(self.devi...  42.4 us
    ppermute x40, waiting for transfers between devices, swap(): lax.ppermute(values, AXES, [(i, i ^ bits[i % 2]) for i in range(self.devi...  31.4 us
    pallas_call x2, Pallas kernels, forward_save(): call(kernel, 'forward_save', (count,), [some(width), whole((rows, 1)), so...  23.2 us
    pallas_call x1, Pallas kernels, backward_slots(): call(kernel, 'backward_slots', (images,), [image(rows, gate), image(rows,...  14.9 us
    pallas_call x1, Pallas kernels, backward_first(): call(kernel, 'backward_first', (images,), [image(rows, width), image(rows...  12.2 us
    convert_element_type x7, other arithmetic, send(): self.sent = self.add(slice(keep, 2 * keep)).astype(BF16)  9.05 us
  transfers between devices with their start and end apart: 40, of which 12 were waited for; matrix products, arithmetic and copies ran while one was open for 18% of the time, Pallas kernels for 23%

profile of v5, /device:TPU:0, one launch (start us, length us, event | category | flops | bytes accessed | tf_op | source)
XLA Modules:
  0.0 221.3 jit_solution(903202038545593595)
XLA Ops:
  1.7 3.1 %collective-permute-start = (bf16[1,6,16,512]{3,2,1,0:T(8,128)(2,1)S(1)}, bf16[1,6,16,512]{3,2,1,0:T(8,128)(2,1)S(1)}, u32[]{:S(2)}, u32[]{:S(2)}) collective-permute-start(bf16[1,6,16,512]{3,2,1,0:T(8,128)(2,1)S(1)} %bitcast.58), channel_id=1, source_target_pairs={{0,8},{1,17},{2,10},{3,19},{4,12},{5,21},{6,14},{7,23},{8,0},{9,25... | collective-permute-start | bytes 294920 | tf_op jit(solution)/shard_map/ppermute | solution.py:703
  4.8 2.6 %collective-permute-start.1 = (bf16[1,6,16,512]{3,2,1,0:T(8,128)(2,1)S(1)}, bf16[1,6,16,512]{3,2,1,0:T(8,128)(2,1)S(1)}, u32[]{:S(2)}, u32[]{:S(2)}) collective-permute-start(bf16[1,6,16,512]{3,2,1,0:T(8,128)(2,1)S(1)} %bitcast.59), channel_id=1, source_target_pairs={{0,16},{1,9},{2,18},{3,11},{4,20},{5,13},{6,22},{7,15},{8,24},{9,1... | collective-permute-start | bytes 294920 | tf_op jit(solution)/shard_map/ppermute | solution.py:703
  7.4 1.4 fusion.54
  14.5 1.6 collective-permute-start.7
  16.4 1.7 collective-permute-start.3
  18.1 2.4 %collective-permute-start.4 = (bf16[1,12,16,512]{3,2,1,0:T(8,128)(2,1)S(1)}, bf16[1,12,16,512]{3,2,1,0:T(8,128)(2,1)S(1)}, u32[]{:S(2)}, u32[]{:S(2)}) collective-permute-start(bf16[1,12,16,512]{3,2,1,0:T(8,128)(2,1)S(1)} %pad_maximum_fusion.3), channel_id=1, source_target_pairs={{0,16},{1,9},{2,18},{3,11},{4,20},{5,13},{6,22},{7,15},{8,24},{9,1... | collective-permute-start | bytes 589832 | tf_op jit(solution)/shard_map/ppermute | solution.py:703
  21.1 1.6 collective-permute-start.8
  22.7 6.0 %collective-permute-done.3 = bf16[1,12,16,512]{3,2,1,0:T(8,128)(2,1)S(1)} collective-permute-done((bf16[1,12,16,512]{3,2,1,0:T(8,128)(2,1)S(1)}, bf16[1,12,16,512]{3,2,1,0:T(8,128)(2,1)S(1)}, u32[]{:S(2)}, u32[]{:S(2)}) %collective-permute-start.3) | collective-permute-done | bytes 196640 | tf_op jit(solution)/shard_map/ppermute | solution.py:703
  28.6 4.6 %collective-permute-done.4 = bf16[1,12,16,512]{3,2,1,0:T(8,128)(2,1)S(1)} collective-permute-done((bf16[1,12,16,512]{3,2,1,0:T(8,128)(2,1)S(1)}, bf16[1,12,16,512]{3,2,1,0:T(8,128)(2,1)S(1)}, u32[]{:S(2)}, u32[]{:S(2)}) %collective-permute-start.4) | collective-permute-done | bytes 196640 | tf_op jit(solution)/shard_map/ppermute | solution.py:703
  33.2 1.5 collective-permute-start.9
  39.1 2.1 collective-permute-done.9.refs_8_.refs_3_
  41.9 1.4 reshape.124
  43.3 1.1 pad.36.values_ref
  44.4 1.1 pad.37.cot_ref
  46.6 2.1 collective-permute-start.14
  49.3 10.3 %forward_save.2 = (bf16[5,208,1536]{2,1,0:T(8,128)(2,1)}, bf16[5,208,1536]{2,1,0:T(8,128)(2,1)}, bf16[5,208,1536]{2,1,0:T(8,128)(2,1)}, bf16[5,208,1536]{2,1,0:T...) custom-call(s32[32]{0:T(128)} %pad_add_fusion.owner_ref, ...), custom_call_target="tpu_custom_call" | custom-call | flops 4000000000 | bytes 20000000 | tf_op jit(solution)/shard_map/forward_save/pallas_call | solution.py:334
  60.9 12.9 %forward_save.3 = (bf16[5,208,1536]{2,1,0:T(8,128)(2,1)}, bf16[5,208,1536]{2,1,0:T(8,128)(2,1)}, bf16[5,208,1536]{2,1,0:T(8,128)(2,1)}, bf16[5,208,1536]{2,1,0:T...) custom-call(s32[32]{0:T(128)} %pad_add_fusion.owner_ref, ...), custom_call_target="tpu_custom_call", output_to_operand_aliasing={{0}: (18, {}), {1}: (19, {}), {2}: (20, {}), {3}: (21, {}),... | custom-call | flops 6000000000 | bytes 20000000 | tf_op jit(solution)/shard_map/forward_save/pallas_call | solution.py:334
  74.4 1.0 copy.65.valid_ref
  76.5 49.9 %forward_backward.1 = (bf16[5,208,512]{2,1,0:T(8,128)(2,1)}, f32[5,208,512]{2,1,0:T(8,128)}, bf16[5,208,1536]{2,1,0:T(8,128)(2,1)}, bf16[5,208,1536]{2,1,0:T(8,1...) custom-call(s32[32]{0:T(128)} %pad_add_fusion.owner_ref, ...), custom_call_target="tpu_custom_call" | custom-call | flops 40000000000 | bytes 20000000 | tf_op jit(solution)/shard_map/forward_backward/pallas_call | solution.py:460
  127.0 1.4 slice.193
  128.5 1.1 reshape.128
  129.7 2.8 %add_convert_fusion = bf16[8,9,16,512]{3,2,1,0:T(8,128)(2,1)} fusion(bf16[8,9,16,512]{3,2,1,0:T(8,128)(2,1)} %collective-permute-done.20, bf16[16,9,16,512]{3,2,1,0:T(8,128)(2,1)S(1)} %copy-done), kind=kLoop, calls=%fused_computation | loop fusion | flops 2359296 | bytes 3538944 | tf_op jit(solution)/shard_map/convert_element_type | solution.py:785
  132.5 2.0 collective-permute-start.22
  134.5 14.9 %backward_slots.1 = (bf16[5,208,1536]{2,1,0:T(8,128)(2,1)}, bf16[16,3,16,512]{3,2,1,0:T(8,128)(2,1)}, bf16[16,3,16,512]{3,2,1,0:T(8,128)(2,1)}, bf16[48,1536]{1,0:T(8,128)(2,1)}, bf16[48,1536]{1,0:T(8,128)(2,1)}) custom-call(s32[32]{0:T(128)} %pad_add_fusion.owner_ref, bf16[5,208,1536]{2,1,0:T(8,128)(2,1)} %get-tuple-element.153.mixed_ref, ...), custom_call_target="tpu_custom_call" | custom-call | flops 8999999488 | bytes 20000000 | tf_op jit(solution)/shard_map/backward_slots/pallas_call | solution.py:543
  150.1 2.6 %add_convert_fusion.1 = bf16[8,6,16,512]{3,2,1,0:T(8,128)(2,1)} fusion(bf16[16,6,16,512]{3,2,1,0:T(8,128)(2,1)} %collective-permute-done.23.refs_7_, bf16[16,6,16,512]{3,2,1,0:T(8,128)(2,1)} %get-tuple-element.214.refs_6_), kind=kLoop, calls=%fused_computation.1 | loop fusion | flops 1572864 | bytes 2359296 | tf_op jit(solution)/shard_map/convert_element_type | solution.py:789
  152.7 1.3 collective-permute-start.27
  154.0 2.2 add_convert_fusion.2
  156.9 1.0 add_convert_fusion.4
  158.5 5.8 %collective-permute-start.31 = (bf16[48,1536]{1,0:T(8,128)(2,1)S(1)}, bf16[48,1536]{1,0:T(8,128)(2,1)}, u32[]{:S(2)}, u32[]{:S(2)}) collective-permute-start(bf16[48,1536]{1,0:T(8,128)(2,1)S(1)} %add_convert_fusion.12), channel_id=1, source_target_pairs={{0,16},{1,9},{2,18},{3,11},{4,20},{5,13},{6,22},{7,15},{8,24},{9,1... | collective-permute-start | bytes 442376 | tf_op jit(solution)/shard_map/ppermute | solution.py:703
  164.3 12.2 %backward_first.1 = (f32[980,512]{1,0:T(8,128)}, f32[8,1536]{1,0:T(8,128)}) custom-call(s32[32]{0:T(128)} %pad_add_fusion.owner_ref, bf16[5,208,512]{2,1,0:T(8,128)(2,1)} %pad.36.values_ref, bf16[5,208,1536]{2,1,0:T(8,128)(2,1)} %get-tuple-element.148.left_ref, bf16[5,208,1536]{2,1,0:T(8,128)(2,1)} %get-tuple-element.168.right_ref, ...), custom_call_target="tpu_custom_call" | custom-call | flops 6000000000 | bytes 20000000 | tf_op jit(solution)/shard_map/backward_first/pallas_call | solution.py:600
  177.4 3.7 %collective-permute-start.32 = (bf16[8,1536]{1,0:T(8,128)(2,1)S(1)}, bf16[8,1536]{1,0:T(8,128)(2,1)S(1)}, u32[]{:S(2)}, u32[]{:S(2)}) collective-permute-start(bf16[8,1536]{1,0:T(8,128)(2,1)S(1)} %convert_element_type.363), channel_id=1, source_target_pairs={{0,16},{1,9},{2,18},{3,11},{4,20},{5,13},{6,22},{7,15},{8,24},{9,1... | collective-permute-start | bytes 73736 | tf_op jit(solution)/shard_map/ppermute | solution.py:703
  181.2 1.4 add_convert_fusion.3
  182.6 1.1 add_convert_fusion.6
  183.8 1.4 collective-permute-start.30
  185.2 1.2 add_convert_fusion.5
  187.5 1.8 collective-permute-start.35
  189.3 4.4 %collective-permute-done.30.refs_9_ = bf16[4,9,16,512]{3,2,1,0:T(8,128)(2,1)S(1)} collective-permute-done((bf16[4,9,16,512]{3,2,1,0:T(8,128)(2,1)S(1)}, bf16[4,9,16,512]{3,2,1,0:T(8,128)(2,1)S(1)}, u32[]{:S(2)}, u32[]{:S(2)}) %collective-permute-start.30) | collective-permute-done | bytes 589856 | tf_op jit(solution)/shard_map/ppermute | solution.py:703
  193.7 1.4 convert_add_fusion
  196.3 1.8 collective-permute-done.29.refs_4_
  198.2 1.9 add_convert_fusion.10
  200.1 1.4 collective-permute-start.37
  201.4 4.7 %collective-permute-done.34.refs_10_ = bf16[2,9,16,512]{3,2,1,0:T(8,128)(2,1)S(1)} collective-permute-done((bf16[2,9,16,512]{3,2,1,0:T(8,128)(2,1)S(1)}, bf16[2,9,16,512]{3,2,1,0:T(8,128)(2,1)S(1)}, u32[]{:S(2)}, u32[]{:S(2)}) %collective-permute-start.34) | collective-permute-done | bytes 294944 | tf_op jit(solution)/shard_map/ppermute | solution.py:703
  206.2 1.1 convert_add_fusion.1
  209.2 2.0 collective-permute-start.36
  211.2 2.3 %collective-permute-done.38 = bf16[48,1536]{1,0:T(8,128)(2,1)S(1)} collective-permute-done((bf16[48,1536]{1,0:T(8,128)(2,1)S(1)}, bf16[48,1536]{1,0:T(8,128)(2,1)S(1)}, u32[]{:S(2)}, u32[]{:S(2)}) %collective-permute-start.38) | collective-permute-done | bytes 147488 | tf_op jit(solution)/shard_map/ppermute | solution.py:703
  213.7 2.4 %collective-permute-done.33.refs_5_ = bf16[1,9,16,512]{3,2,1,0:T(8,128)(2,1)S(1)} collective-permute-done((bf16[1,9,16,512]{3,2,1,0:T(8,128)(2,1)}, bf16[1,9,16,512]{3,2,1,0:T(8,128)(2,1)S(1)}, u32[]{:S(2)}, u32[]{:S(2)}) %collective-permute-start.33) | collective-permute-done | bytes 147488 | tf_op jit(solution)/shard_map/ppermute | solution.py:703
  216.0 1.6 collective-permute-done.36.refs_11_
  218.3 2.8 %add_blocks.1 = (f32[2,16,3072]{2,1,0:T(8,128)}, f32[2,48,512]{2,1,0:T(8,128)}, f32[2,512]{1,0:T(2,128)}, f32[2,512]{1,0:T(2,128)}, f32[2,3072]{1,0:T(2,128)}, /...) custom-call(s32[1]{0:T(128)} %bitcast.18.odd_ref, ...), custom_call_target="tpu_custom_call" | custom-call | tf_op jit(solution)/shard_map/add_blocks/pallas_call | solution.py:680
  (181 shorter events, 25.6 us)
Async XLA Ops:
  1.7 9.2 %copy-start.23 = (f32[2,3072]{1,0:T(2,128)S(1)}, f32[2,3072]{1,0:T(2,128)}, u32[]{:S(2)}) copy-start(f32[2,3072]{1,0:T(2,128)} %param.22) | copy-start | bytes 73732
  1.7 12.3 %collective-permute-start = (bf16[1,6,16,512]{3,2,1,0:T(8,128)(2,1)S(1)}, bf16[1,6,16,512]{3,2,1,0:T(8,128)(2,1)S(1)}, u32[]{:S(2)}, u32[]{:S(2)}) collective-permute-start(bf16[1,6,16,512]{3,2,1,0:T(8,128)(2,1)S(1)} %bitcast.58), channel_id=1, source_target_pairs={{0,8},{1,17},{2,10},{3,19},{4,12},{5,21},{6,14},{7,23},{8,0},{9,25... | collective-permute-start | bytes 294920 | tf_op jit(solution)/shard_map/ppermute | solution.py:703
  4.8 9.6 %collective-permute-start.1 = (bf16[1,6,16,512]{3,2,1,0:T(8,128)(2,1)S(1)}, bf16[1,6,16,512]{3,2,1,0:T(8,128)(2,1)S(1)}, u32[]{:S(2)}, u32[]{:S(2)}) collective-permute-start(bf16[1,6,16,512]{3,2,1,0:T(8,128)(2,1)S(1)} %bitcast.59), channel_id=1, source_target_pairs={{0,16},{1,9},{2,18},{3,11},{4,20},{5,13},{6,22},{7,15},{8,24},{9,1... | collective-permute-start | bytes 294920 | tf_op jit(solution)/shard_map/ppermute | solution.py:703
  7.4 7.0 %collective-permute-start.2 = (bf16[1,6,16,512]{3,2,1,0:T(8,128)(2,1)S(1)}, bf16[1,6,16,512]{3,2,1,0:T(8,128)(2,1)S(1)}, u32[]{:S(2)}, u32[]{:S(2)}) collective-permute-start(bf16[1,6,16,512]{3,2,1,0:T(8,128)(2,1)S(1)} %bitcast.60), channel_id=1, source_target_pairs={{0,24},{1,25},{2,26},{3,27},{4,28},{5,29},{6,30},{7,31},{8,16},{9,... | collective-permute-start | bytes 294920 | tf_op jit(solution)/shard_map/ppermute | solution.py:703
  14.4 23.5 %copy-start.5 = (bf16[4,6,16,512]{3,2,1,0:T(8,128)(2,1)}, bf16[4,6,16,512]{3,2,1,0:T(8,128)(2,1)S(1)}, u32[]{:S(2)}) copy-start(bf16[4,6,16,512]{3,2,1,0:T(8,128)(2,1)S(1)} %pad_maximum_fusion.2.refs_5_.refs_0_) | copy-start | bytes 1179652
  14.5 18.7 %collective-permute-start.7 = (bf16[4,6,16,512]{3,2,1,0:T(8,128)(2,1)S(1)}, bf16[4,6,16,512]{3,2,1,0:T(8,128)(2,1)S(1)}, u32[]{:S(2)}, u32[]{:S(2)}) collective-permute-start(bf16[4,6,16,512]{3,2,1,0:T(8,128)(2,1)S(1)} %pad_maximum_fusion.2.refs_5_.refs_0_), channel_id=1, source_target_pairs={{0,2},{1,5},{2,0},{3,7},{4,6},{5,1},{6,4},{7,3},{8,10},{9,13},{10,... | collective-permute-start | bytes 1179656 | tf_op jit(solution)/shard_map/ppermute | solution.py:703
  16.4 12.2 %collective-permute-start.3 = (bf16[1,12,16,512]{3,2,1,0:T(8,128)(2,1)S(1)}, bf16[1,12,16,512]{3,2,1,0:T(8,128)(2,1)S(1)}, u32[]{:S(2)}, u32[]{:S(2)}) collective-permute-start(bf16[1,12,16,512]{3,2,1,0:T(8,128)(2,1)S(1)} %pad_maximum_fusion.3), channel_id=1, source_target_pairs={{0,8},{1,17},{2,10},{3,19},{4,12},{5,21},{6,14},{7,23},{8,0},{9,25... | collective-permute-start | bytes 589832 | tf_op jit(solution)/shard_map/ppermute | solution.py:703
  18.1 15.1 %collective-permute-start.4 = (bf16[1,12,16,512]{3,2,1,0:T(8,128)(2,1)S(1)}, bf16[1,12,16,512]{3,2,1,0:T(8,128)(2,1)S(1)}, u32[]{:S(2)}, u32[]{:S(2)}) collective-permute-start(bf16[1,12,16,512]{3,2,1,0:T(8,128)(2,1)S(1)} %pad_maximum_fusion.3), channel_id=1, source_target_pairs={{0,16},{1,9},{2,18},{3,11},{4,20},{5,13},{6,22},{7,15},{8,24},{9,1... | collective-permute-start | bytes 589832 | tf_op jit(solution)/shard_map/ppermute | solution.py:703
  20.5 12.7 %collective-permute-start.5 = (bf16[1,12,16,512]{3,2,1,0:T(8,128)(2,1)S(1)}, bf16[1,12,16,512]{3,2,1,0:T(8,128)(2,1)S(1)}, u32[]{:S(2)}, u32[]{:S(2)}) collective-permute-start(bf16[1,12,16,512]{3,2,1,0:T(8,128)(2,1)S(1)} %pad_maximum_fusion.3), channel_id=1, source_target_pairs={{0,24},{1,25},{2,26},{3,27},{4,28},{5,29},{6,30},{7,31},{8,16},{9,... | collective-permute-start | bytes 589832 | tf_op jit(solution)/shard_map/ppermute | solution.py:703
  21.1 17.6 %collective-permute-start.8 = (bf16[4,6,16,512]{3,2,1,0:T(8,128)(2,1)S(1)}, bf16[4,6,16,512]{3,2,1,0:T(8,128)(2,1)}, u32[]{:S(2)}, u32[]{:S(2)}) collective-permute-start(bf16[4,6,16,512]{3,2,1,0:T(8,128)(2,1)S(1)} %pad_maximum_fusion.2.refs_5_.refs_0_), channel_id=1, source_target_pairs={{0,4},{1,3},{2,6},{3,1},{4,0},{5,7},{6,2},{7,5},{8,12},{9,11},{10,... | collective-permute-start | bytes 1179656 | tf_op jit(solution)/shard_map/ppermute | solution.py:703
  33.2 7.9 %collective-permute-start.9 = (bf16[4,6,16,512]{3,2,1,0:T(8,128)(2,1)S(1)}, bf16[4,6,16,512]{3,2,1,0:T(8,128)(2,1)}, u32[]{:S(2)}, u32[]{:S(2)}) collective-permute-start(bf16[4,6,16,512]{3,2,1,0:T(8,128)(2,1)S(1)} %collective-permute-done.7.refs_6_.refs_1_), channel_id=1, source_target_pairs={{0,4},{1,3},{2,6},{3,1},{4,0},{5,7},{6,2},{7,5},{8,12},{9,11},{10,... | collective-permute-start | bytes 1179656 | tf_op jit(solution)/shard_map/ppermute | solution.py:703
  36.4 10.2 %collective-permute-start.10 = (bf16[4,6,16,512]{3,2,1,0:T(8,128)(2,1)S(1)}, bf16[4,6,16,512]{3,2,1,0:T(8,128)(2,1)}, u32[]{:S(2)}, u32[]{:S(2)}) collective-permute-start(bf16[4,6,16,512]{3,2,1,0:T(8,128)(2,1)S(1)} %pad_maximum_fusion.2.refs_5_.refs_0_), channel_id=1, source_target_pairs={{0,1},{1,0},{2,3},{3,2},{4,5},{5,4},{6,7},{7,6},{8,9},{9,8},{10,11... | collective-permute-start | bytes 1179656 | tf_op jit(solution)/shard_map/ppermute | solution.py:703
  38.0 21.6 %collective-permute-start.6 = (bf16[4,12,16,512]{3,2,1,0:T(8,128)(2,1)}, bf16[4,12,16,512]{3,2,1,0:T(8,128)(2,1)}, u32[]{:S(2)}, u32[]{:S(2)}) collective-permute-start(bf16[4,12,16,512]{3,2,1,0:T(8,128)(2,1)} %pad_maximum_fusion.refs_9_), channel_id=1, source_target_pairs={{0,2},{1,5},{2,0},{3,7},{4,6},{5,1},{6,4},{7,3},{8,10},{9,13},{10,... | collective-permute-start | bytes 2359304 | tf_op jit(solution)/shard_map/ppermute | solution.py:703
  38.5 10.7 %collective-permute-start.11 = (bf16[4,6,16,512]{3,2,1,0:T(8,128)(2,1)S(1)}, bf16[4,6,16,512]{3,2,1,0:T(8,128)(2,1)}, u32[]{:S(2)}, u32[]{:S(2)}) collective-permute-start(bf16[4,6,16,512]{3,2,1,0:T(8,128)(2,1)S(1)} %collective-permute-done.7.refs_6_.refs_1_), channel_id=1, source_target_pairs={{0,1},{1,0},{2,3},{3,2},{4,5},{5,4},{6,7},{7,6},{8,9},{9,8},{10,11... | collective-permute-start | bytes 1179656 | tf_op jit(solution)/shard_map/ppermute | solution.py:703
  38.7 10.5 %collective-permute-start.12 = (bf16[4,6,16,512]{3,2,1,0:T(8,128)(2,1)}, bf16[4,6,16,512]{3,2,1,0:T(8,128)(2,1)}, u32[]{:S(2)}, u32[]{:S(2)}) collective-permute-start(bf16[4,6,16,512]{3,2,1,0:T(8,128)(2,1)} %collective-permute-done.8.refs_7_.refs_2_), channel_id=1, source_target_pairs={{0,1},{1,0},{2,3},{3,2},{4,5},{5,4},{6,7},{7,6},{8,9},{9,8},{10,11... | collective-permute-start | bytes 1179656 | tf_op jit(solution)/shard_map/ppermute | solution.py:703
  41.1 8.1 %collective-permute-start.13 = (bf16[4,6,16,512]{3,2,1,0:T(8,128)(2,1)}, bf16[4,6,16,512]{3,2,1,0:T(8,128)(2,1)}, u32[]{:S(2)}, u32[]{:S(2)}) collective-permute-start(bf16[4,6,16,512]{3,2,1,0:T(8,128)(2,1)} %collective-permute-done.9.refs_8_.refs_3_), channel_id=1, source_target_pairs={{0,1},{1,0},{2,3},{3,2},{4,5},{5,4},{6,7},{7,6},{8,9},{9,8},{10,11... | collective-permute-start | bytes 1179656 | tf_op jit(solution)/shard_map/ppermute | solution.py:703
  46.6 14.3 %collective-permute-start.14 = (bf16[4,12,16,512]{3,2,1,0:T(8,128)(2,1)}, bf16[4,12,16,512]{3,2,1,0:T(8,128)(2,1)S(1)}, u32[]{:S(2)}, u32[]{:S(2)}) collective-permute-start(bf16[4,12,16,512]{3,2,1,0:T(8,128)(2,1)} %pad_maximum_fusion.refs_9_), channel_id=1, source_target_pairs={{0,4},{1,3},{2,6},{3,1},{4,0},{5,7},{6,2},{7,5},{8,12},{9,11},{10,... | collective-permute-start | bytes 2359304 | tf_op jit(solution)/shard_map/ppermute | solution.py:703
  59.6 14.2 %collective-permute-start.15 = (bf16[4,12,16,512]{3,2,1,0:T(8,128)(2,1)}, bf16[4,12,16,512]{3,2,1,0:T(8,128)(2,1)S(1)}, u32[]{:S(2)}, u32[]{:S(2)}) collective-permute-start(bf16[4,12,16,512]{3,2,1,0:T(8,128)(2,1)} %collective-permute-done.6.refs_10_), channel_id=1, source_target_pairs={{0,4},{1,3},{2,6},{3,1},{4,0},{5,7},{6,2},{7,5},{8,12},{9,11},{10,... | collective-permute-start | bytes 2359304 | tf_op jit(solution)/shard_map/ppermute | solution.py:703
  60.3 15.1 %collective-permute-start.16 = (bf16[4,12,16,512]{3,2,1,0:T(8,128)(2,1)}, bf16[4,12,16,512]{3,2,1,0:T(8,128)(2,1)S(1)}, u32[]{:S(2)}, u32[]{:S(2)}) collective-permute-start(bf16[4,12,16,512]{3,2,1,0:T(8,128)(2,1)} %pad_maximum_fusion.refs_9_), channel_id=1, source_target_pairs={{0,1},{1,0},{2,3},{3,2},{4,5},{5,4},{6,7},{7,6},{8,9},{9,8},{10,11... | collective-permute-start | bytes 2359304 | tf_op jit(solution)/shard_map/ppermute | solution.py:703
  60.3 15.1 %collective-permute-start.17 = (bf16[4,12,16,512]{3,2,1,0:T(8,128)(2,1)}, bf16[4,12,16,512]{3,2,1,0:T(8,128)(2,1)S(1)}, u32[]{:S(2)}, u32[]{:S(2)}) collective-permute-start(bf16[4,12,16,512]{3,2,1,0:T(8,128)(2,1)} %collective-permute-done.6.refs_10_), channel_id=1, source_target_pairs={{0,1},{1,0},{2,3},{3,2},{4,5},{5,4},{6,7},{7,6},{8,9},{9,8},{10,11... | collective-permute-start | bytes 2359304 | tf_op jit(solution)/shard_map/ppermute | solution.py:703
  60.8 13.0 %copy-start.32 = (bf16[4,12,16,512]{3,2,1,0:T(8,128)(2,1)}, bf16[4,12,16,512]{3,2,1,0:T(8,128)(2,1)S(1)}, u32[]{:S(2)}) copy-start(bf16[4,12,16,512]{3,2,1,0:T(8,128)(2,1)S(1)} %collective-permute-done.14.refs_11_) | copy-start | bytes 2359300
  60.8 14.6 %collective-permute-start.18 = (bf16[4,12,16,512]{3,2,1,0:T(8,128)(2,1)S(1)}, bf16[4,12,16,512]{3,2,1,0:T(8,128)(2,1)}, u32[]{:S(2)}, u32[]{:S(2)}) collective-permute-start(bf16[4,12,16,512]{3,2,1,0:T(8,128)(2,1)S(1)} %collective-permute-done.14.refs_11_), channel_id=1, source_target_pairs={{0,1},{1,0},{2,3},{3,2},{4,5},{5,4},{6,7},{7,6},{8,9},{9,8},{10,11... | collective-permute-start | bytes 2359304 | tf_op jit(solution)/shard_map/ppermute | solution.py:703
  60.9 13.4 %copy-start.18 = (f32[5,208,1]{1,0,2:T(8,128)S(1)}, f32[5,208,1]{1,0,2:T(8,128)}, u32[]{:S(2)}) copy-start(f32[5,208,1]{1,0,2:T(8,128)} %pad_bitcast_fusion) | copy-start | bytes 12484
  73.8 2.6 %collective-permute-start.19 = (bf16[4,12,16,512]{3,2,1,0:T(8,128)(2,1)S(1)}, bf16[4,12,16,512]{3,2,1,0:T(8,128)(2,1)}, u32[]{:S(2)}, u32[]{:S(2)}) collective-permute-start(bf16[4,12,16,512]{3,2,1,0:T(8,128)(2,1)S(1)} %collective-permute-done.15.refs_12_), channel_id=1, source_target_pairs={{0,1},{1,0},{2,3},{3,2},{4,5},{5,4},{6,7},{7,6},{8,9},{9,8},{10,11... | collective-permute-start | bytes 2359304 | tf_op jit(solution)/shard_map/ppermute | solution.py:703
  126.4 3.3 %collective-permute-start.20 = (bf16[8,9,16,512]{3,2,1,0:T(8,128)(2,1)}, bf16[8,9,16,512]{3,2,1,0:T(8,128)(2,1)}, u32[]{:S(2)}, u32[]{:S(2)}) collective-permute-start(bf16[8,9,16,512]{3,2,1,0:T(8,128)(2,1)} %get-tuple-element.145), channel_id=1, source_target_pairs={{0,1},{1,0},{2,3},{3,2},{4,5},{5,4},{6,7},{7,6},{8,9},{9,8},{10,11... | collective-permute-start | bytes 3538952 | tf_op jit(solution)/shard_map/ppermute | solution.py:703
  126.8 22.6 %collective-permute-start.23 = (bf16[16,6,16,512]{3,2,1,0:T(8,128)(2,1)}, bf16[16,6,16,512]{3,2,1,0:T(8,128)(2,1)}, u32[]{:S(2)}, u32[]{:S(2)}) collective-permute-start(bf16[16,6,16,512]{3,2,1,0:T(8,128)(2,1)} %get-tuple-element.146), channel_id=1, source_target_pairs={{0,1},{1,0},{2,3},{3,2},{4,5},{5,4},{6,7},{7,6},{8,9},{9,8},{10,11... | collective-permute-start | bytes 4718600 | tf_op jit(solution)/shard_map/ppermute | solution.py:703
  132.5 16.9 %collective-permute-start.22 = (bf16[8,9,16,512]{3,2,1,0:T(8,128)(2,1)}, bf16[8,9,16,512]{3,2,1,0:T(8,128)(2,1)S(1)}, u32[]{:S(2)}, u32[]{:S(2)}) collective-permute-start(bf16[8,9,16,512]{3,2,1,0:T(8,128)(2,1)} %add_convert_fusion), channel_id=1, source_target_pairs={{0,4},{1,3},{2,6},{3,1},{4,0},{5,7},{6,2},{7,5},{8,12},{9,11},{10,... | collective-permute-start | bytes 3538952 | tf_op jit(solution)/shard_map/ppermute | solution.py:703
  134.5 19.5 %collective-permute-start.25 = (bf16[8,9,16,512]{3,2,1,0:T(8,128)(2,1)}, bf16[8,9,16,512]{3,2,1,0:T(8,128)(2,1)}, u32[]{:S(2)}, u32[]{:S(2)}) collective-permute-start(bf16[8,9,16,512]{3,2,1,0:T(8,128)(2,1)} %get-tuple-element.176), channel_id=1, source_target_pairs={{0,1},{1,0},{2,3},{3,2},{4,5},{5,4},{6,7},{7,6},{8,9},{9,8},{10,11... | collective-permute-start | bytes 3538952 | tf_op jit(solution)/shard_map/ppermute | solution.py:703
  149.4 48.7 %copy-start.1 = (bf16[8,9,16,512]{3,2,1,0:T(8,128)(2,1)}, bf16[8,9,16,512]{3,2,1,0:T(8,128)(2,1)S(1)}, u32[]{:S(2)}) copy-start(bf16[8,9,16,512]{3,2,1,0:T(8,128)(2,1)S(1)} %collective-permute-done.22.refs_2_) | copy-start | bytes 3538948
  149.4 7.4 %collective-permute-start.24 = (bf16[16,3,16,512]{3,2,1,0:T(8,128)(2,1)}, bf16[16,3,16,512]{3,2,1,0:T(8,128)(2,1)S(1)}, u32[]{:S(2)}, u32[]{:S(2)}) collective-permute-start(bf16[16,3,16,512]{3,2,1,0:T(8,128)(2,1)} %get-tuple-element.175), channel_id=1, source_target_pairs={{0,1},{1,0},{2,3},{3,2},{4,5},{5,4},{6,7},{7,6},{8,9},{9,8},{10,11... | collective-permute-start | bytes 2359304 | tf_op jit(solution)/shard_map/ppermute | solution.py:703
  150.0 8.5 %collective-permute-start.21 = (bf16[48,1536]{1,0:T(8,128)(2,1)}, bf16[48,1536]{1,0:T(8,128)(2,1)S(1)}, u32[]{:S(2)}, u32[]{:S(2)}) collective-permute-start(bf16[48,1536]{1,0:T(8,128)(2,1)} %get-tuple-element.171), channel_id=1, source_target_pairs={{0,1},{1,0},{2,3},{3,2},{4,5},{5,4},{6,7},{7,6},{8,9},{9,8},{10,11... | collective-permute-start | bytes 442376 | tf_op jit(solution)/shard_map/ppermute | solution.py:703
  152.7 23.9 %collective-permute-start.27 = (bf16[8,6,16,512]{3,2,1,0:T(8,128)(2,1)}, bf16[8,6,16,512]{3,2,1,0:T(8,128)(2,1)}, u32[]{:S(2)}, u32[]{:S(2)}) collective-permute-start(bf16[8,6,16,512]{3,2,1,0:T(8,128)(2,1)} %add_convert_fusion.1), channel_id=1, source_target_pairs={{0,4},{1,3},{2,6},{3,1},{4,0},{5,7},{6,2},{7,5},{8,12},{9,11},{10,... | collective-permute-start | bytes 2359304 | tf_op jit(solution)/shard_map/ppermute | solution.py:703
  156.2 20.3 %collective-permute-start.26 = (bf16[4,9,16,512]{3,2,1,0:T(8,128)(2,1)}, bf16[4,9,16,512]{3,2,1,0:T(8,128)(2,1)}, u32[]{:S(2)}, u32[]{:S(2)}) collective-permute-start(bf16[4,9,16,512]{3,2,1,0:T(8,128)(2,1)} %add_convert_fusion.2), channel_id=1, source_target_pairs={{0,2},{1,5},{2,0},{3,7},{4,6},{5,1},{6,4},{7,3},{8,10},{9,13},{10,... | collective-permute-start | bytes 1769480 | tf_op jit(solution)/shard_map/ppermute | solution.py:703
  157.9 18.6 %collective-permute-start.28 = (bf16[8,3,16,512]{3,2,1,0:T(8,128)(2,1)}, bf16[8,3,16,512]{3,2,1,0:T(8,128)(2,1)S(1)}, u32[]{:S(2)}, u32[]{:S(2)}) collective-permute-start(bf16[8,3,16,512]{3,2,1,0:T(8,128)(2,1)} %add_convert_fusion.4), channel_id=1, source_target_pairs={{0,4},{1,3},{2,6},{3,1},{4,0},{5,7},{6,2},{7,5},{8,12},{9,11},{10,... | collective-permute-start | bytes 1179656 | tf_op jit(solution)/shard_map/ppermute | solution.py:703
  158.5 28.0 %collective-permute-start.31 = (bf16[48,1536]{1,0:T(8,128)(2,1)S(1)}, bf16[48,1536]{1,0:T(8,128)(2,1)}, u32[]{:S(2)}, u32[]{:S(2)}) collective-permute-start(bf16[48,1536]{1,0:T(8,128)(2,1)S(1)} %add_convert_fusion.12), channel_id=1, source_target_pairs={{0,16},{1,9},{2,18},{3,11},{4,20},{5,13},{6,22},{7,15},{8,24},{9,1... | collective-permute-start | bytes 442376 | tf_op jit(solution)/shard_map/ppermute | solution.py:703
  176.5 30.8 %copy-start.6 = (bf16[8,3,16,512]{3,2,1,0:T(8,128)(2,1)}, bf16[8,3,16,512]{3,2,1,0:T(8,128)(2,1)S(1)}, u32[]{:S(2)}) copy-start(bf16[8,3,16,512]{3,2,1,0:T(8,128)(2,1)S(1)} %collective-permute-done.28.refs_14_) | copy-start | bytes 1179652
  177.4 9.1 %collective-permute-start.32 = (bf16[8,1536]{1,0:T(8,128)(2,1)S(1)}, bf16[8,1536]{1,0:T(8,128)(2,1)S(1)}, u32[]{:S(2)}, u32[]{:S(2)}) collective-permute-start(bf16[8,1536]{1,0:T(8,128)(2,1)S(1)} %convert_element_type.363), channel_id=1, source_target_pairs={{0,16},{1,9},{2,18},{3,11},{4,20},{5,13},{6,22},{7,15},{8,24},{9,1... | collective-permute-start | bytes 73736 | tf_op jit(solution)/shard_map/ppermute | solution.py:703
  183.8 9.9 %collective-permute-start.30 = (bf16[4,9,16,512]{3,2,1,0:T(8,128)(2,1)S(1)}, bf16[4,9,16,512]{3,2,1,0:T(8,128)(2,1)S(1)}, u32[]{:S(2)}, u32[]{:S(2)}) collective-permute-start(bf16[4,9,16,512]{3,2,1,0:T(8,128)(2,1)S(1)} %pad_maximum_fusion.1), channel_id=1, source_target_pairs={{0,2},{1,5},{2,0},{3,7},{4,6},{5,1},{6,4},{7,3},{8,10},{9,13},{10,... | collective-permute-start | bytes 1769480 | tf_op jit(solution)/shard_map/ppermute | solution.py:703
  186.5 11.7 %collective-permute-start.29 = (bf16[2,9,16,512]{3,2,1,0:T(8,128)(2,1)S(1)}, bf16[2,9,16,512]{3,2,1,0:T(8,128)(2,1)S(1)}, u32[]{:S(2)}, u32[]{:S(2)}) collective-permute-start(bf16[2,9,16,512]{3,2,1,0:T(8,128)(2,1)S(1)} %add_convert_fusion.5), channel_id=1, source_target_pairs={{0,16},{1,9},{2,18},{3,11},{4,20},{5,13},{6,22},{7,15},{8,24},{9,1... | collective-permute-start | bytes 884744 | tf_op jit(solution)/shard_map/ppermute | solution.py:703
  187.5 12.5 %collective-permute-start.35 = (bf16[48,1536]{1,0:T(8,128)(2,1)S(1)}, bf16[48,1536]{1,0:T(8,128)(2,1)S(1)}, u32[]{:S(2)}, u32[]{:S(2)}) collective-permute-start(bf16[48,1536]{1,0:T(8,128)(2,1)S(1)} %add_convert_fusion.11), channel_id=1, source_target_pairs={{0,8},{1,17},{2,10},{3,19},{4,12},{5,21},{6,14},{7,23},{8,0},{9,25... | collective-permute-start | bytes 442376 | tf_op jit(solution)/shard_map/ppermute | solution.py:703
  193.7 14.4 %copy-start.4 = (bf16[4,9,16,512]{3,2,1,0:T(8,128)(2,1)}, bf16[4,9,16,512]{3,2,1,0:T(8,128)(2,1)S(1)}, u32[]{:S(2)}) copy-start(bf16[4,9,16,512]{3,2,1,0:T(8,128)(2,1)S(1)} %collective-permute-done.30.refs_9_) | copy-start | bytes 1769476
  196.2 9.9 %collective-permute-start.34 = (bf16[2,9,16,512]{3,2,1,0:T(8,128)(2,1)S(1)}, bf16[2,9,16,512]{3,2,1,0:T(8,128)(2,1)S(1)}, u32[]{:S(2)}, u32[]{:S(2)}) collective-permute-start(bf16[2,9,16,512]{3,2,1,0:T(8,128)(2,1)S(1)} %fusion.12), channel_id=1, source_target_pairs={{0,16},{1,9},{2,18},{3,11},{4,20},{5,13},{6,22},{7,15},{8,24},{9,1... | collective-permute-start | bytes 884744 | tf_op jit(solution)/shard_map/ppermute | solution.py:703
  198.2 10.1 %copy-start.8 = (bf16[2,9,16,512]{3,2,1,0:T(8,128)(2,1)}, bf16[2,9,16,512]{3,2,1,0:T(8,128)(2,1)S(1)}, u32[]{:S(2)}) copy-start(bf16[2,9,16,512]{3,2,1,0:T(8,128)(2,1)S(1)} %collective-permute-done.29.refs_4_) | copy-start | bytes 884740
  200.1 8.2 %collective-permute-start.37 = (bf16[48,1536]{1,0:T(8,128)(2,1)S(1)}, bf16[48,1536]{1,0:T(8,128)(2,1)S(1)}, u32[]{:S(2)}, u32[]{:S(2)}) collective-permute-start(bf16[48,1536]{1,0:T(8,128)(2,1)S(1)} %add_convert_fusion.9), channel_id=1, source_target_pairs={{0,2},{1,5},{2,0},{3,7},{4,6},{5,1},{6,4},{7,3},{8,10},{9,13},{10,... | collective-permute-start | bytes 442376 | tf_op jit(solution)/shard_map/ppermute | solution.py:703
  208.3 5.2 %collective-permute-start.38 = (bf16[48,1536]{1,0:T(8,128)(2,1)S(1)}, bf16[48,1536]{1,0:T(8,128)(2,1)S(1)}, u32[]{:S(2)}, u32[]{:S(2)}) collective-permute-start(bf16[48,1536]{1,0:T(8,128)(2,1)S(1)} %add_convert_fusion.8), channel_id=1, source_target_pairs={{0,4},{1,3},{2,6},{3,1},{4,0},{5,7},{6,2},{7,5},{8,12},{9,11},{10,... | collective-permute-start | bytes 442376 | tf_op jit(solution)/shard_map/ppermute | solution.py:703
  209.2 6.8 %collective-permute-start.33 = (bf16[1,9,16,512]{3,2,1,0:T(8,128)(2,1)}, bf16[1,9,16,512]{3,2,1,0:T(8,128)(2,1)S(1)}, u32[]{:S(2)}, u32[]{:S(2)}) collective-permute-start(bf16[1,9,16,512]{3,2,1,0:T(8,128)(2,1)} %add_convert_fusion.10), channel_id=1, source_target_pairs={{0,8},{1,17},{2,10},{3,19},{4,12},{5,21},{6,14},{7,23},{8,0},{9,25... | collective-permute-start | bytes 442376 | tf_op jit(solution)/shard_map/ppermute | solution.py:703
  209.2 8.4 %collective-permute-start.36 = (bf16[1,9,16,512]{3,2,1,0:T(8,128)(2,1)S(1)}, bf16[1,9,16,512]{3,2,1,0:T(8,128)(2,1)S(1)}, u32[]{:S(2)}, u32[]{:S(2)}) collective-permute-start(bf16[1,9,16,512]{3,2,1,0:T(8,128)(2,1)S(1)} %fusion.30), channel_id=1, source_target_pairs={{0,8},{1,17},{2,10},{3,19},{4,12},{5,21},{6,14},{7,23},{8,0},{9,25... | collective-permute-start | bytes 442376 | tf_op jit(solution)/shard_map/ppermute | solution.py:703
  213.6 4.0 %collective-permute-start.39 = (bf16[48,1536]{1,0:T(8,128)(2,1)S(1)}, bf16[48,1536]{1,0:T(8,128)(2,1)S(1)}, u32[]{:S(2)}, u32[]{:S(2)}) collective-permute-start(bf16[48,1536]{1,0:T(8,128)(2,1)S(1)} %add_convert_fusion.7.refs_15_), channel_id=1, source_target_pairs={{0,1},{1,0},{2,3},{3,2},{4,5},{5,4},{6,7},{7,6},{8,9},{9,8},{10,11... | collective-permute-start | bytes 442376 | tf_op jit(solution)/shard_map/ppermute | solution.py:703
  (28 other events, 103.1 us)
